TPU v7x, 128 devices: a whole 4x4x4 slice. The times are simulated.
128 devices in a mesh: pipe: 2 (over y_hi), vocab: 8 (over x, core), dp: 8 (over z, y_lo).
Axes of the slice: x: 4, y: 4 (y_hi: 2, y_lo: 2; y = y_hi * 2 + y_lo), z: 4, core: 2. Of those that a mesh axis runs over, the one named last changes fastest.
Arguments:
- hidden: bfloat16 [2048, 7168], P(('pipe', 'dp')), may hold values from -750 to 750
- gain: bfloat16 [7168], replicated, may hold values from 0.5 to 1.5
- targets: int32 [2048], P(('pipe', 'dp')), may hold values from 0 to 32767
- table: bfloat16 [32768, 7168], P(('vocab', 'dp')), may hold values from -8 to 8
Outputs:
- hidden_grad: bfloat16 [2048, 7168], P(('pipe', 'dp'))
- table_grad: bfloat16 [32768, 7168], P(('vocab', 'dp'), 'pipe')
- token_loss: float32 [2048], P(('pipe', 'dp'))
All inputs are finite; a program needn't handle non-finite values.
Results may differ from a plain program's by a relative error of at most 0.022.
Values may be sent and summed in bfloat16 or wider, within the bound.
No kernel may reach another device: no remote copies, remote signals or barrier semaphores. Data moves between devices by JAX's collectives and lax.ppermute only.
A program may use at most 128 MiB of HBM per device.

v0:
```python
import jax
import jax.numpy as jnp
from jax import lax
from jax.sharding import PartitionSpec as P

NORM_EPS = 1e-06


def norm_backward(normed_grad, hidden_wide, inverse, gain_wide):
    upward = normed_grad * gain_wide
    inner_sum = jnp.sum(upward * hidden_wide, axis=1, keepdims=True)
    result = (
        inverse * upward
        - hidden_wide * (inverse * inverse * inverse) * inner_sum / hidden_wide.shape[1]
    )
    return result.astype(jnp.bfloat16)


def on_device(hidden, gain, targets, table):
    tok_rows = hidden.shape[0]
    vocab_rows = table.shape[0]
    hidden_wide = hidden.astype(jnp.float32)
    inverse = lax.rsqrt(jnp.mean(hidden_wide * hidden_wide, axis=1, keepdims=True) + NORM_EPS)
    gain_wide = gain.astype(jnp.float32)
    normed = (hidden_wide * inverse * gain_wide).astype(jnp.bfloat16)
    gathered, wanted = (
        lax.all_gather(normed, "dp", axis=0, tiled=True),
        lax.all_gather(targets, "dp", axis=0, tiled=True),
    )
    logits = lax.dot_general(
        gathered, table, (((1,), (1,)), ((), ())), preferred_element_type=jnp.float32
    )
    first_row = (lax.axis_index("vocab") * lax.axis_size("dp") + lax.axis_index("dp")) * vocab_rows
    columns = lax.broadcasted_iota(jnp.int32, (1, vocab_rows), 1) + first_row
    is_target = columns == wanted[:, None]
    picked = jnp.sum(jnp.where(is_target, logits, jnp.zeros_like(logits)), axis=1)
    local_top = jnp.max(logits, axis=1)
    row_top = lax.pmax(local_top, ("vocab", "dp"))
    row_total, target_logit = lax.psum(
        (jnp.sum(jnp.exp(logits - row_top[:, None]), axis=1), picked), ("vocab", "dp")
    )
    log_norm = row_top + jnp.log(row_total)
    group_loss = log_norm - target_logit
    token_loss = lax.dynamic_slice_in_dim(group_loss, lax.axis_index("dp") * tok_rows, tok_rows)
    dlogits = (jnp.exp(logits - log_norm[:, None]) - is_target.astype(jnp.float32)).astype(
        jnp.bfloat16
    )
    grad_rows = lax.dot_general(
        dlogits, gathered, (((0,), (0,)), ((), ())), preferred_element_type=jnp.float32
    )
    table_grad = lax.psum_scatter(
        grad_rows.astype(jnp.bfloat16), "pipe", scatter_dimension=1, tiled=True
    )
    replica_sum = lax.psum_scatter(
        jnp.dot(dlogits, table, preferred_element_type=jnp.float32).astype(jnp.bfloat16),
        "dp",
        scatter_dimension=0,
        tiled=True,
    )
    normed_grad = lax.psum(replica_sum, "vocab").astype(jnp.float32)
    hidden_grad = norm_backward(normed_grad, hidden_wide, inverse, gain_wide)
    return (hidden_grad, table_grad, token_loss)


def solution(mesh):
    placed = (P(("pipe", "dp"), None), P(), P(("pipe", "dp")), P(("vocab", "dp"), None))
    return jax.shard_map(
        on_device,
        mesh=mesh,
        in_specs=placed,
        out_specs=(P(("pipe", "dp"), None), P(("vocab", "dp"), "pipe"), P(("pipe", "dp"))),
        check_vma=False,
    )
```

profile of v0, /device:TPU:0, one launch (start us, length us, event | category | flops | bytes accessed | tf_op | source)
XLA Modules:
  0.0 1068.2 jit_solution(18331892698368341102)
XLA Ops:
  7.2 0.0 copy-start.2
  7.2 0.0 all-gather.3.cloned.1.call-start
  7.2 1.9 fusion
  9.2 0.7 convert_element_type.28
  9.9 3.2 fusion.2
  13.1 0.0 all-gather.3.cloned.1.call-update
  13.2 0.0 reduce-scatter.3.cloned.1.call-start
  13.2 0.0 copy-done.2
  13.2 20.1 %all-gather = s32[8,1,128]{2,1,0:T(1,128)S(1)} all-gather(s32[1,1,128]{2,1,0:T(1,128)S(1)} %bitcast.9), channel_id=1, replica_groups=mesh['pipe'=2,'vocab'=8,'dp'=8] {'dp'}, dimensions={0}, use_global_device_ids=true | all-gather | bytes 4608 | tf_op jit(solution)/shard_map/all_gather | solution.py:28
  33.4 268.7 %all-gather.3.cloned.1.call-done = bf16[1024,7168]{1,0:T(8,128)(2,1)} async-done(((bf16[128,7168]{1,0:T(8,128)(2,1)}), bf16[1024,7168]{1,0:T(8,128)(2,1)}) %all-gather.3.cloned.1.call-update) | async-done | bytes 14680080 | tf_op jit(solution)/shard_map/all_gather | solution.py:27
  302.1 13.2 %fusion.14 = (f32[1024]{0:T(1024)S(1)}, f32[1024,512]{0,1:T(8,128)S(1)}) fusion(bf16[1024,7168]{1,0:T(8,128)(2,1)} %all-gather.3.cloned.1.call-done, bf16[512,7168]{1,0:T(8,128)(2,1)} %param.7), kind=kOutput, calls=%fused_computation.26 | convolution fusion | flops 7516716032 | bytes 24121344 | tf_op jit(solution)/shard_map/dot_general | solution.py:30
  315.3 142.8 %pmax.7 = f32[1024]{0:T(1024)S(1)} all-reduce(f32[1024]{0:T(1024)S(1)} %get-tuple-element.11), channel_id=1, replica_groups=mesh['pipe'=2,'vocab'=8,'dp'=8] {'vocab','dp'}, use_global_device_ids=true, to_apply=%region_2.3 | all-reduce | flops 1024 | bytes 8192 | tf_op jit(solution)/shard_map/pmax | solution.py:38
  458.1 0.5 fusion.10
  458.6 140.6 %all-reduce = (f32[1024]{0:T(1024)S(1)}, f32[1024]{0:T(1024)S(1)}) all-reduce(f32[1024]{0:T(1024)S(1)} %get-tuple-element.4, f32[1024]{0:T(1024)S(1)} %get-tuple-element.3), channel_id=1, replica_groups=mesh['pipe'=2,'vocab'=8,'dp'=8] {'vocab','dp'}, use_global_device_ids=true, to_apply=%region_4.5 | all-reduce | flops 2048 | bytes 16384 | tf_op jit(solution)/shard_map/psum | solution.py:39
  599.3 14.3 %convolution_convert_fusion = bf16[1024,7168]{1,0:T(8,128)(2,1)} fusion(bf16[512,7168]{1,0:T(8,128)(2,1)} %param.7, f32[1024,512]{0,1:T(8,128)S(1)} %get-tuple-element.12, s32[1024]{0:T(1024)S(1)} %bitcast.7, f32[1024]{0:T(1024)S(1)} %get-tuple-element.8, s32[512]{0:T(512)S(1)} %iota_add_fusion), kind=kOutput, calls=%fused_computation | convolution fusion | flops 7526154240 | bytes 24127488 | tf_op jit(solution)/shard_map/dot_general | solution.py:55
  613.6 0.0 reduce-scatter.3.cloned.1.call-update
  613.6 0.0 all-reduce.3.cloned.1.call-start
  613.7 284.9 %reduce-scatter.3.cloned.1.call-done = bf16[128,7168]{1,0:T(8,128)(2,1)} async-done(((bf16[1024,7168]{1,0:T(8,128)(2,1)}), bf16[128,7168]{1,0:T(8,128)(2,1)}) %reduce-scatter.3.cloned.1.call-update) | async-done | bytes 1835024 | tf_op jit(solution)/shard_map/reduce_scatter | solution.py:54
  898.5 0.0 all-reduce.3.cloned.1.call-update
  898.5 0.2 reduce-scatter.5.cloned.1.call-start
  898.8 15.3 %convolution_convert_fusion.1 = bf16[512,7168]{1,0:T(8,128)(2,1)} fusion(bf16[1024,7168]{1,0:T(8,128)(2,1)} %all-gather.3.cloned.1.call-done, f32[1024,512]{0,1:T(8,128)S(1)} %get-tuple-element.12, s32[1024]{0:T(1024)S(1)} %bitcast.8, f32[1024]{0:T(1024)S(1)} %get-tuple-element.8, s32[512]{0:T(512)S(1)} %iota_add_fusion), kind=kOutput, calls=%fused_computation.1 | convolution fusion | flops 7522484224 | bytes 24127488 | tf_op jit(solution)/shard_map/dot_general | solution.py:48
  914.1 0.0 copy-start
  914.1 0.0 reduce-scatter.5.cloned.1.call-update
  914.1 0.6 dynamic_slice.3
  914.7 52.0 %all-reduce.3.cloned.1.call-done = bf16[128,7168]{1,0:T(8,128)(2,1)} async-done(((bf16[128,7168]{1,0:T(8,128)(2,1)}), bf16[128,7168]{1,0:T(8,128)(2,1)}) %all-reduce.3.cloned.1.call-update) | async-done | bytes 1835024 | tf_op jit(solution)/shard_map/psum | solution.py:60
  966.7 0.0 copy-done
  966.7 0.0 copy-start.1
  966.7 2.4 fusion.7
  969.2 0.0 copy-done.1
  969.2 2.4 fusion.6
  971.6 90.0 %reduce-scatter.5.cloned.1.call-done = bf16[512,3584]{1,0:T(8,128)(2,1)} async-done(((bf16[512,7168]{1,0:T(8,128)(2,1)}), bf16[512,3584]{1,0:T(8,128)(2,1)}) %reduce-scatter.5.cloned.1.call-update) | async-done | bytes 3670032 | tf_op jit(solution)/shard_map/reduce_scatter | solution.py:51
  (3 shorter events, 0.0 us)
Async XLA Ops:
  7.2 6.1 copy-start.2
  7.2 294.9 %all-gather.3.cloned.1.call-start = ((), (), s32[]{:S(2)}) async-start(), calls=%async_computation.2 | async-start | bytes 16515072 | tf_op jit(solution)/shard_map/all_gather | solution.py:27
  13.2 885.4 %reduce-scatter.3.cloned.1.call-start = ((), (), s32[]{:S(2)}) async-start(), calls=%async_computation.3 | async-start | bytes 16515072 | tf_op jit(solution)/shard_map/reduce_scatter | solution.py:54
  613.6 353.1 %all-reduce.3.cloned.1.call-start = ((), (), s32[]{:S(2)}) async-start(), calls=%async_computation.4 | async-start | bytes 3670016 | tf_op jit(solution)/shard_map/psum | solution.py:60
  898.5 163.1 %reduce-scatter.5.cloned.1.call-start = ((), (), s32[]{:S(2)}) async-start(), calls=%async_computation.5 | async-start | bytes 11010048 | tf_op jit(solution)/shard_map/reduce_scatter | solution.py:51
  914.1 52.6 %copy-start = (bf16[128,7168]{1,0:T(8,128)(2,1)S(1)}, bf16[128,7168]{1,0:T(8,128)(2,1)}, u32[]{:S(2)}) copy-start(bf16[128,7168]{1,0:T(8,128)(2,1)} %param.4) | copy-start | bytes 5505028
  966.7 2.4 copy-start.1
Sparse Core Ops, SparseCore 0:
  13.3 288.7 all-gather.2
  613.7 284.7 reduce-scatter.2
  900.9 65.7 all-reduce.2
  969.6 92.0 reduce-scatter.4
where the time goes:
time: 1070 us
  waiting for transfers between devices  696 us (65%)
  blocking collectives  304 us (28%)
  matrix products  42.8 us (4%)
  between operations  13.8 us (1%)
  other arithmetic  11.3 us (1%)
    reduce_scatter x1, waiting for transfers between devices, on_device(): lax.psum_scatter(jnp.dot(dlogits, table, preferred_element_type=jnp.float...  285 us
    all_gather x1, waiting for transfers between devices, on_device(): lax.all_gather(normed, 'dp', axis=0, tiled=True)  269 us
    pmax x1, blocking collectives, on_device(): row_top = lax.pmax(local_top, ('vocab', 'dp'))  143 us
    psum x1, blocking collectives, on_device(): lax.psum((jnp.sum(jnp.exp(logits - row_top[:, None]), axis=1), picked), (...  141 us
    reduce_scatter x1, waiting for transfers between devices, on_device(): lax.psum_scatter(grad_rows.astype(jnp.bfloat16), 'pipe', scatter_dimensio...  90 us
    psum x1, waiting for transfers between devices, on_device(): normed_grad = lax.psum(replica_sum, 'vocab').astype(jnp.float32)  52 us
  transfers between devices with their start and end apart: 4, of which 4 were waited for; matrix products, arithmetic and copies ran while one was open for 2% of the time, Pallas kernels for 0%

commit v1 on v0

v1 whole, which is shorter than its diff:
```python
import jax
import jax.numpy as jnp
from jax import lax
from jax.sharding import PartitionSpec as P

NORM_EPS = 1e-06


def norm_backward(normed_grad, hidden_wide, inverse, gain_wide):
    upward = normed_grad * gain_wide
    inner_sum = jnp.sum(upward * hidden_wide, axis=1, keepdims=True)
    result = (
        inverse * upward
        - hidden_wide * (inverse * inverse * inverse) * inner_sum / hidden_wide.shape[1]
    )
    return result.astype(jnp.bfloat16)


def on_device(hidden, gain, targets, table):
    tok_rows, width = hidden.shape
    vocab_rows = table.shape[0]
    n_vocab, n_dp, n_pipe = lax.axis_size("vocab"), lax.axis_size("dp"), lax.axis_size("pipe")
    my_vocab, my_dp, my_pipe = lax.axis_index("vocab"), lax.axis_index("dp"), lax.axis_index("pipe")
    part = tok_rows // n_vocab

    hidden_wide = hidden.astype(jnp.float32)
    inverse = lax.rsqrt(jnp.mean(hidden_wide * hidden_wide, axis=1, keepdims=True) + NORM_EPS)
    gain_wide = gain.astype(jnp.float32)
    normed = (hidden_wide * inverse * gain_wide).astype(jnp.bfloat16)

    mine = lax.dynamic_slice_in_dim(normed, my_vocab * part, part)
    over_dp = lax.all_gather(mine, "dp", axis=0, tiled=True)
    gathered = lax.all_gather(over_dp, "vocab", axis=0, tiled=True)
    spread = jnp.broadcast_to(targets.reshape(1, 1, tok_rows), (n_dp, 1, tok_rows))
    wanted = lax.all_to_all(spread, "dp", 0, 0)
    wanted = wanted.reshape(n_dp, n_vocab, part).transpose(1, 0, 2).reshape(-1)

    logits = lax.dot_general(
        gathered, table, (((1,), (1,)), ((), ())), preferred_element_type=jnp.float32
    )
    first_row = (my_vocab * n_dp + my_dp) * vocab_rows
    columns = lax.broadcasted_iota(jnp.int32, (1, vocab_rows), 1) + first_row
    is_target = columns == wanted[:, None]
    picked = jnp.sum(jnp.where(is_target, logits, jnp.zeros_like(logits)), axis=1)
    local_top = jnp.max(logits, axis=1)
    local_total = jnp.sum(jnp.exp(logits - local_top[:, None]), axis=1)

    group = ("vocab", "dp")
    n_group = n_vocab * n_dp
    stats = jnp.stack(
        [s.reshape(n_group, part) for s in (local_top, local_total, picked)], axis=1
    )
    stats = lax.all_to_all(stats, group, 0, 0, tiled=True)
    tops, totals, picks = stats[:, 0], stats[:, 1], stats[:, 2]
    row_top = jnp.max(tops, axis=0)
    row_total = jnp.sum(totals * jnp.exp(tops - row_top), axis=0)
    own_norm = row_top + jnp.log(row_total)
    own_loss = own_norm - jnp.sum(picks, axis=0)
    both = jnp.stack([own_norm, own_loss])
    both = lax.all_to_all(
        jnp.broadcast_to(both[None], (n_group, 2, part)), group, 0, 0, tiled=True
    )
    log_norm = both[:, 0].reshape(-1)
    loss = both[:, 1].reshape(n_vocab, n_dp, part)
    token_loss = lax.dynamic_slice_in_dim(loss, my_dp, 1, axis=1).reshape(-1)

    dlogits = (jnp.exp(logits - log_norm[:, None]) - is_target.astype(jnp.float32)).astype(
        jnp.bfloat16
    )
    half = width // n_pipe

    def table_half(end):
        cols = lax.dynamic_slice_in_dim(gathered, end * half, half, axis=1)
        return lax.dot_general(
            dlogits, cols, (((0,), (0,)), ((), ())), preferred_element_type=jnp.float32
        )

    sent = table_half((my_pipe + 1) % n_pipe).astype(jnp.bfloat16)
    received = lax.ppermute(sent, "pipe", [(i, (i + 1) % n_pipe) for i in range(n_pipe)])

    replica_sum = jnp.dot(dlogits, table, preferred_element_type=jnp.float32).astype(jnp.bfloat16)
    over_vocab = lax.psum_scatter(replica_sum, "vocab", scatter_dimension=0, tiled=True)
    summed = lax.psum_scatter(over_vocab, "dp", scatter_dimension=0, tiled=True)
    table_grad = (table_half(my_pipe) + received.astype(jnp.float32)).astype(jnp.bfloat16)
    normed_grad = lax.all_gather(summed, "vocab", axis=0, tiled=True).astype(jnp.float32)
    hidden_grad = norm_backward(normed_grad, hidden_wide, inverse, gain_wide)
    return (hidden_grad, table_grad, token_loss)


def solution(mesh):
    placed = (P(("pipe", "dp"), None), P(), P(("pipe", "dp")), P(("vocab", "dp"), None))
    return jax.shard_map(
        on_device,
        mesh=mesh,
        in_specs=placed,
        out_specs=(P(("pipe", "dp"), None), P(("vocab", "dp"), "pipe"), P(("pipe", "dp"))),
        check_vma=False,
    )
```

time: 1070 us -> 425 us (0.40)
  waiting for transfers between devices: 696 us -> 314 us
  blocking collectives: 304 us -> 28.4 us
    reduce_scatter x2, waiting for transfers between devices: 375 us -> 151 us  [the longest x1 79.6 us: on_device(): lax.psum_scatter(replica_sum, 'vocab', scatter_dimension=0, tiled=True)]
    all_gather x1 -> x3, waiting for transfers between devices: 269 us -> 116 us  [the longest x1 65.5 us: on_device(): gathered = lax.all_gather(over_dp, 'vocab', axis=0, tiled=True)]
    pmax x1 -> x0, blocking collectives: 143 us -> none  [on_device(): row_top = lax.pmax(local_top, ('vocab', 'dp'))]
    psum x1 -> x0, blocking collectives: 141 us -> none  [on_device(): lax.psum((jnp.sum(jnp.exp(logits - row_top[:, None]), axis=1), picked), (...]
    psum x1 -> x0, waiting for transfers between devices: 52 us -> none  [on_device(): normed_grad = lax.psum(replica_sum, 'vocab').astype(jnp.float32)]
    ppermute x0 -> x1, waiting for transfers between devices: none -> 41.8 us  [on_device(): lax.ppermute(sent, 'pipe', [(i, (i + 1) % n_pipe) for i in range(n_pipe)])]
    all_to_all x0 -> x2, blocking collectives: none -> 28.4 us  [the longest x1 16.3 us: on_device(): stats = lax.all_to_all(stats, group, 0, 0, tiled=True)]
    all_gather x1 -> x0, blocking collectives: 20.1 us -> none  [on_device(): lax.all_gather(targets, 'dp', axis=0, tiled=True)]
  transfers between devices with their start and end apart: 4 -> 7, of which waited for: 4 -> 6; matrix products, arithmetic and copies ran while one was open for 2% -> 5% of each run, Pallas kernels for 0% -> 0%
where the time goes in v1:
time: 425 us
  waiting for transfers between devices  314 us (74%)
  matrix products  44.9 us (11%)
  blocking collectives  28.4 us (7%)
  other arithmetic  14.1 us (3%)
  between operations  13.9 us (3%)
  starting transfers between devices  6.51 us (2%)
    reduce_scatter x1, waiting for transfers between devices, on_device(): lax.psum_scatter(replica_sum, 'vocab', scatter_dimension=0, tiled=True)  79.6 us
    reduce_scatter x1, waiting for transfers between devices, on_device(): summed = lax.psum_scatter(over_vocab, 'dp', scatter_dimension=0, tiled=True)  71.4 us
    all_gather x1, waiting for transfers between devices, on_device(): gathered = lax.all_gather(over_dp, 'vocab', axis=0, tiled=True)  65.5 us
    all_gather x1, waiting for transfers between devices, on_device(): over_dp = lax.all_gather(mine, 'dp', axis=0, tiled=True)  50.1 us
    ppermute x1, waiting for transfers between devices, on_device(): lax.ppermute(sent, 'pipe', [(i, (i + 1) % n_pipe) for i in range(n_pipe)])  41.8 us
    dot_general x2, matrix products, table_half(): lax.dot_general(dlogits, cols, (((0,), (0,)), ((), ())), preferred_elemen...  17.6 us
    all_to_all x1, blocking collectives, on_device(): stats = lax.all_to_all(stats, group, 0, 0, tiled=True)  16.3 us
    dot_general x1, matrix products, on_device(): jnp.dot(dlogits, table, preferred_element_type=jnp.float32)  14.1 us
  transfers between devices with their start and end apart: 7, of which 6 were waited for; matrix products, arithmetic and copies ran while one was open for 5% of the time, Pallas kernels for 0%

profile of v1, /device:TPU:0, one launch (start us, length us, event | category | flops | bytes accessed | tf_op | source)
XLA Modules:
  0.0 424.7 jit_solution(14484463105721137161)
XLA Ops:
  7.2 0.0 all-gather.4.cloned.1.call-start
  7.2 0.0 copy-start.2
  7.2 1.9 multiply_reduce_fusion.1
  9.2 0.0 copy-start.3
  9.2 3.7 convert_element_type.33
  12.9 0.1 dynamic-slice
  13.0 1.8 fusion.13
  14.8 0.0 all-gather.4.cloned.1.call-update
  14.8 0.0 all-gather.6.cloned.1.call-start
  14.9 50.1 %all-gather.4.cloned.1.call-done = bf16[128,7168]{1,0:T(8,128)(2,1)} async-done(((bf16[16,7168]{1,0:T(8,128)(2,1)}), bf16[128,7168]{1,0:T(8,128)(2,1)}) %all-gather.4.cloned.1.call-update) | async-done | bytes 1835024 | tf_op jit(solution)/shard_map/all_gather | solution.py:32
  65.0 0.0 all-gather.6.cloned.1.call-update
  65.0 0.6 broadcast_in_dim.6
  65.6 3.3 all-to-all-start
  68.9 0.0 reduce-scatter.3.cloned.1.call-start
  69.0 5.9 %all-to-all-done = s32[8,1,128]{2,1,0:T(1,128)S(1)} async-done(((s32[8,1,128]{2,1,0:T(1,128)}), s32[8,1,128]{2,1,0:T(1,128)S(1)}, u32[]{:S(2)}, u32[]{:S(2)}) %all-to-all-start) | async-done | bytes 4128 | tf_op jit(solution)/shard_map/all_to_all | solution.py:35
  74.9 0.5 broadcast.40
  75.4 0.7 reduce.13
  76.1 0.1 reshape.73
  76.2 0.1 eq.18
  76.3 65.5 %all-gather.6.cloned.1.call-done = bf16[1024,7168]{1,0:T(8,128)(2,1)} async-done(((bf16[128,7168]{1,0:T(8,128)(2,1)}), bf16[1024,7168]{1,0:T(8,128)(2,1)}) %all-gather.6.cloned.1.call-update) | async-done | bytes 14680080 | tf_op jit(solution)/shard_map/all_gather | solution.py:33
  141.8 13.2 %fusion.18 = (f32[1024]{0:T(1024)S(1)}, f32[1024,512]{0,1:T(8,128)S(1)}) fusion(bf16[1024,7168]{1,0:T(8,128)(2,1)} %all-gather.6.cloned.1.call-done, bf16[512,7168]{1,0:T(8,128)(2,1)} %param.7), kind=kOutput, calls=%fused_computation.35 | convolution fusion | flops 7516716032 | bytes 24121344 | tf_op jit(solution)/shard_map/dot_general | solution.py:38
  155.0 0.1 stack_reshape.9
  155.1 0.5 exponential_reduce_fusion
  155.6 0.1 stack_reshape.10
  155.6 0.1 stack_reshape.11
  155.7 0.1 copy.17
  155.8 16.3 %all_to_all.15 = f32[64,3,16]{2,1,0:T(4,128)S(1)} all-to-all(f32[64,3,16]{2,1,0:T(4,128)S(1)} %copy.17), channel_id=1, replica_groups=mesh['pipe'=2,'vocab'=8,'dp'=8] {'vocab','dp'}, dimensions={0} | all-to-all | bytes 24576 | tf_op jit(solution)/shard_map/all_to_all | solution.py:53
  172.1 0.1 fusion.16
  172.3 12.1 %all_to_all.16 = f32[64,2,16]{2,1,0:T(2,128)S(1)} all-to-all(f32[64,2,16]{2,1,0:T(2,128)S(1)} %broadcast_in_dim.8), channel_id=1, replica_groups=mesh['pipe'=2,'vocab'=8,'dp'=8] {'vocab','dp'}, dimensions={0} | all-to-all | bytes 16384 | tf_op jit(solution)/shard_map/all_to_all | solution.py:60
  184.5 0.1 fusion.17
  184.6 0.1 sub.47
  184.7 0.5 fusion.11
  185.1 14.1 %convolution_convert_fusion = bf16[1024,7168]{1,0:T(8,128)(2,1)} fusion(bf16[1024,512]{0,1:T(8,128)(2,1)S(1)} %fusion.11, bf16[512,7168]{1,0:T(8,128)(2,1)} %param.7), kind=kOutput, calls=%fused_computation | convolution fusion | flops 7523532800 | bytes 23068672 | tf_op jit(solution)/shard_map/dot_general | solution.py:81
  199.3 0.0 reduce-scatter.3.cloned.1.call-update
  199.3 0.0 reduce-scatter.5.cloned.1.call-start
  199.3 79.6 %reduce-scatter.3.cloned.1.call-done = bf16[128,7168]{1,0:T(8,128)(2,1)} async-done(((bf16[1024,7168]{1,0:T(8,128)(2,1)}), bf16[128,7168]{1,0:T(8,128)(2,1)}) %reduce-scatter.3.cloned.1.call-update) | async-done | bytes 1835024 | tf_op jit(solution)/shard_map/reduce_scatter | solution.py:82
  279.0 0.0 reduce-scatter.5.cloned.1.call-update
  279.0 0.0 all-gather.8.cloned.1.call-start
  279.1 8.5 %fusion.4 = bf16[512,3584]{1,0:T(8,128)(2,1)} fusion(bf16[1024,512]{0,1:T(8,128)(2,1)S(1)} %fusion.11, bf16[1024,7168]{1,0:T(8,128)(2,1)} %all-gather.6.cloned.1.call-done, s32[]{:T(128)S(6)} %select_n.27), kind=kOutput, calls=%fused_computation.6 | convolution fusion | flops 3759931392 | bytes 12058628 | tf_op jit(solution)/shard_map/dot_general | solution.py:74
  287.6 3.0 collective-permute-start
  290.6 71.4 %reduce-scatter.5.cloned.1.call-done = bf16[16,7168]{1,0:T(8,128)(2,1)} async-done(((bf16[128,7168]{1,0:T(8,128)(2,1)}), bf16[16,7168]{1,0:T(8,128)(2,1)}) %reduce-scatter.5.cloned.1.call-update) | async-done | bytes 229392 | tf_op jit(solution)/shard_map/reduce_scatter | solution.py:83
  361.9 0.0 all-gather.8.cloned.1.call-update
  362.0 0.6 reshape.74
  362.6 41.8 %collective-permute-done = bf16[512,3584]{1,0:T(8,128)(2,1)} collective-permute-done((bf16[512,3584]{1,0:T(8,128)(2,1)}, bf16[512,3584]{1,0:T(8,128)(2,1)}, u32[]{:S(2)}, u32[]{:S(2)}) %collective-permute-start) | collective-permute-done | bytes 3670048 | tf_op jit(solution)/shard_map/ppermute | solution.py:79
  404.4 9.1 %add_convert_fusion = bf16[512,3584]{1,0:T(8,128)(2,1)} fusion(bf16[512,3584]{1,0:T(8,128)(2,1)} %collective-permute-done, bf16[1024,512]{0,1:T(8,128)(2,1)S(1)} %fusion.11, bf16[1024,7168]{1,0:T(8,128)(2,1)} %all-gather.6.cloned.1.call-done, s32[]{:T(128)S(6)} %select_n.25), kind=kOutput, calls=%fused_computation.1 | convolution fusion | flops 3763601408 | bytes 15728644 | tf_op jit(solution)/shard_map/dot_general | solution.py:74
  413.4 2.3 multiply_reduce_fusion
  415.7 0.0 copy-done.1
  415.7 2.4 subtract_convert_fusion
  (17 shorter events, 0.2 us)
Async XLA Ops:
  7.2 57.8 %all-gather.4.cloned.1.call-start = ((), (), s32[]{:S(2)}) async-start(), calls=%async_computation.5 | async-start | bytes 2064384 | tf_op jit(solution)/shard_map/all_gather | solution.py:32
  7.2 5.7 %copy-start.2 = (bf16[7168]{0:T(1024)(128)(2,1)S(1)}, bf16[7168]{0:T(1024)(128)(2,1)}, u32[]{:S(2)}) copy-start(bf16[7168]{0:T(1024)(128)(2,1)} %param.5) | copy-start | bytes 43012
  9.2 55.8 %copy-start.3 = (s32[128]{0:T(128)S(1)}, s32[128]{0:T(128)}, u32[]{:S(2)}) copy-start(s32[128]{0:T(128)} %param.6) | copy-start | bytes 1540
  14.8 127.0 %all-gather.6.cloned.1.call-start = ((), (), s32[]{:S(2)}) async-start(), calls=%async_computation.6 | async-start | bytes 16515072 | tf_op jit(solution)/shard_map/all_gather | solution.py:33
  65.6 9.3 %all-to-all-start = ((s32[8,1,128]{2,1,0:T(1,128)}), s32[8,1,128]{2,1,0:T(1,128)S(1)}, u32[]{:S(2)}, u32[]{:S(2)}) async-start(s32[8,1,128]{2,1,0:T(1,128)} %broadcast_in_dim.6), calls=%async_computation | async-start | bytes 8192 | tf_op jit(solution)/shard_map/all_to_all | solution.py:35
  68.9 210.1 %reduce-scatter.3.cloned.1.call-start = ((), (), s32[]{:S(2)}) async-start(), calls=%async_computation.7 | async-start | bytes 16515072 | tf_op jit(solution)/shard_map/reduce_scatter | solution.py:82
  199.3 162.6 %reduce-scatter.5.cloned.1.call-start = ((), (), s32[]{:S(2)}) async-start(), calls=%async_computation.8 | async-start | bytes 2064384 | tf_op jit(solution)/shard_map/reduce_scatter | solution.py:83
  279.0 134.4 %all-gather.8.cloned.1.call-start = ((), (), s32[]{:S(2)}) async-start(), calls=%async_computation.9 | async-start | bytes 2064384 | tf_op jit(solution)/shard_map/all_gather | solution.py:85
  287.6 116.8 %collective-permute-start = (bf16[512,3584]{1,0:T(8,128)(2,1)}, bf16[512,3584]{1,0:T(8,128)(2,1)}, u32[]{:S(2)}, u32[]{:S(2)}) collective-permute-start(bf16[512,3584]{1,0:T(8,128)(2,1)} %fusion.4), channel_id=1, source_target_pairs={{0,64},{64,0},{1,65},{65,1},{2,66},{66,2},{3,67},{67,3},{4,68},{68... | collective-permute-start | bytes 11010056 | tf_op jit(solution)/shard_map/ppermute | solution.py:79
  362.6 50.8 %copy-start = (bf16[128,7168]{1,0:T(8,128)(2,1)S(1)}, bf16[128,7168]{1,0:T(8,128)(2,1)}, u32[]{:S(2)}) copy-start(bf16[128,7168]{1,0:T(8,128)(2,1)} %param.4) | copy-start | bytes 5505028
  413.4 2.3 copy-start.1
Sparse Core Ops, SparseCore 0:
  15.0 49.9 all-gather.3
  66.6 75.1 all-gather.5
  199.4 79.5 reduce-scatter.2
  281.3 80.6 reduce-scatter.4
  363.5 25.2 all-gather.7

commit v2 on v0

v2 whole, which is shorter than its diff:
```python
import jax
import jax.numpy as jnp
from jax import lax
from jax.sharding import PartitionSpec as P

NORM_EPS = 1e-06
NX, NC, NZ, NY = 4, 2, 4, 2


def hop(array, dx=0, dc=0, dz=0, dy=0):
    pairs = []
    for x in range(NX):
        for c in range(NC):
            for z in range(NZ):
                for y in range(NY):
                    here = ((x * NC + c) * NZ + z) * NY + y
                    there = (
                        ((x + dx) % NX * NC + (c + dc) % NC) * NZ + (z + dz) % NZ
                    ) * NY + (y + dy) % NY
                    pairs.append((here, there))
    return lax.ppermute(array, ("vocab", "dp"), pairs)


def put(buffer, block, *lead):
    block = block.reshape((1,) * len(lead) + buffer.shape[len(lead):])
    start = tuple(lead) + (0,) * (buffer.ndim - len(lead))
    return lax.dynamic_update_slice(buffer, block, start)


def take(buffer, *lead):
    start = tuple(lead) + (0,) * (buffer.ndim - len(lead))
    sizes = (1,) * len(lead) + buffer.shape[len(lead):]
    return lax.dynamic_slice(buffer, start, sizes).reshape(buffer.shape[len(lead):])


def dot(a, b, contract, out=jnp.float32):
    return lax.dot_general(
        a, b, (contract, ((), ())), preferred_element_type=jnp.float32
    ).astype(out)


def on_device(hidden, gain, targets, table):
    tok_rows, width = hidden.shape
    vocab_rows = table.shape[0]
    half = width // 2
    bf16, f32 = jnp.bfloat16, jnp.float32
    vocab, dp, pipe = lax.axis_index("vocab"), lax.axis_index("dp"), lax.axis_index("pipe")
    x, c = vocab // NC, vocab % NC
    z, y = dp // NY, dp % NY
    group = NX * NC * NZ * NY
    part = tok_rows // (NX * NC)
    side = tok_rows // NC
    far = side * NZ * NY
    first = c * side + x * part
    own_col, other_col = pipe * half, (1 - pipe) * half

    gain_wide = gain.astype(f32)

    def scale(rows):
        wide = rows.astype(f32)
        inverse = lax.rsqrt(jnp.mean(wide * wide, axis=1, keepdims=True) + NORM_EPS)
        return wide, inverse, (wide * inverse * gain_wide).astype(bf16)

    hidden_mine, inverse_mine, normed_mine = scale(
        lax.dynamic_slice_in_dim(hidden, first, part)
    )
    mine1 = lax.dynamic_slice(normed_mine, (0, own_col), (part, half))
    seed = jnp.broadcast_to(mine1[None], (NZ * NY, part, half))
    near = lax.all_to_all(seed, "dp", 0, 0, tiled=True)
    _, _, normed_side = scale(lax.dynamic_slice_in_dim(hidden, c * side, side))
    mine2 = lax.dynamic_slice(normed_side, (0, other_col), (side, half))
    mine2, near, targets = lax.optimization_barrier((mine2, near, targets))
    rows1 = lax.all_gather(near.reshape(-1, half), "vocab", axis=0, tiled=True)

    partner = hop(mine2, dy=1)
    rows2 = jnp.zeros((NC, NY, NZ, side, half), bf16)
    for block, at in ((mine2, y), (partner, 1 - y)):
        gathered = put(jnp.zeros((NZ, side, half), bf16), block, z)
        for dz in (1, 3, 2):
            gathered = put(gathered, hop(block, dz=dz), (z - dz) % NZ)
        rows2 = put(rows2, gathered, c, at)
        rows2 = put(rows2, hop(gathered, dc=1), 1 - c, at)
    rows2 = rows2.reshape(-1, half)

    spread = jnp.broadcast_to(targets.reshape(1, tok_rows), (NZ * NY, tok_rows))
    wanted = lax.all_to_all(spread, "dp", 0, 0, tiled=True)
    wanted = wanted.reshape(NZ * NY, NC, NX, part).transpose(2, 1, 0, 3).reshape(-1)

    table1 = lax.dynamic_slice(table, (0, own_col), (vocab_rows, half))
    table2 = lax.dynamic_slice(table, (0, other_col), (vocab_rows, half))
    logits1 = dot(rows1, table1, ((1,), (1,)))
    logits2 = dot(rows2, table2, ((1,), (1,)))
    logits2 = logits2.reshape(NC, NY, NZ, NX, part, vocab_rows).transpose(3, 0, 2, 1, 4, 5)
    logits = logits1 + logits2.reshape(logits1.shape)

    first_row = (vocab * NZ * NY + dp) * vocab_rows
    columns = lax.broadcasted_iota(jnp.int32, (1, vocab_rows), 1) + first_row
    is_target = columns == wanted[:, None]
    picked = jnp.sum(jnp.where(is_target, logits, jnp.zeros_like(logits)), axis=1)
    local_top = jnp.max(logits, axis=1)
    local_norm = local_top + jnp.log(jnp.sum(jnp.exp(logits - local_top[:, None]), axis=1))
    picked = picked.reshape(NX * NC, NZ * NY, part).transpose(1, 0, 2).reshape(NZ * NY, tok_rows)
    stats = jnp.concatenate(
        [
            jnp.broadcast_to(local_norm[None], (group, local_norm.shape[0])),
            jnp.tile(picked, (NX * NC, 1)),
        ],
        axis=1,
    )
    stats = lax.all_to_all(stats, ("vocab", "dp"), 0, 0, tiled=True)
    norms, picks = stats[:, : local_norm.shape[0]], stats[:, local_norm.shape[0] :]
    row_top = jnp.max(norms, axis=0)
    log_norm = row_top + jnp.log(jnp.sum(jnp.exp(norms - row_top), axis=0))
    own_norm = lax.dynamic_slice_in_dim(
        log_norm.reshape(NX * NC, NZ * NY, part), dp, 1, axis=1
    ).reshape(-1)
    token_loss = (own_norm - jnp.sum(picks, axis=0)).reshape(NX, NC, part)
    token_loss = token_loss.transpose(1, 0, 2).reshape(-1)

    grad_a = (jnp.exp(logits - log_norm[:, None]) - is_target.astype(f32)).astype(bf16)
    grad_b = grad_a.reshape(NX, NC, NZ, NY, part, vocab_rows).transpose(1, 3, 2, 0, 4, 5)
    grad_b = grad_b.reshape(NC, far, vocab_rows)

    swap = [(0, 1), (1, 0)]
    early = vocab_rows * 3 // 4
    all_b = grad_b.reshape(-1, vocab_rows)
    sent_grad = dot(all_b[:, :early], rows2, ((0,), (0,)), bf16)
    late_grad = dot(all_b[:, early:], rows2, ((0,), (0,)), bf16)
    sent_grad, late_grad, grad_a, grad_b = lax.optimization_barrier(
        (sent_grad, late_grad, grad_a, grad_b)
    )
    received = lax.ppermute(sent_grad, "pipe", swap)
    sent = dot(take(grad_b, 1 - c), table2, ((1,), (0,)), bf16)
    sent, grad_a = lax.optimization_barrier((sent, grad_a))
    sent = hop(sent, dc=1)
    sums1 = dot(grad_a, table1, ((1,), (0,)), bf16)
    sums1, grad_b = lax.optimization_barrier((sums1, grad_b))
    over_vocab = lax.psum_scatter(sums1, "vocab", scatter_dimension=0, tiled=True)
    sums2 = (dot(take(grad_b, c), table2, ((1,), (0,))) + sent.astype(f32)).astype(bf16)
    sums2 = sums2.reshape(NY, NZ, side, half)
    z_blocks = [
        lax.dynamic_slice_in_dim(sums2, (z + dz) % NZ, 1, axis=1).reshape(NY, NX, part, half)
        for dz in range(NZ)
    ]
    *z_blocks, grad_a = lax.optimization_barrier((*z_blocks, grad_a))

    own_grad = dot(grad_a, rows1, ((0,), (0,)))

    total2 = z_blocks[0].astype(f32)
    for dz in (1, 3, 2):
        total2 = total2 + hop(z_blocks[dz], dz=dz).astype(f32)
    total2 = total2.astype(bf16)
    x_blocks = [
        lax.dynamic_slice_in_dim(total2, (x + dx) % NX, 1, axis=1).reshape(NY, part, half)
        for dx in range(NX)
    ]
    *x_blocks, own_grad = lax.optimization_barrier((*x_blocks, own_grad))
    mine2 = x_blocks[0].astype(f32)
    for dx in (1, 3, 2):
        mine2 = mine2 + hop(x_blocks[dx], dx=dx).astype(f32)
    mine2 = mine2.astype(bf16)
    mine2, over_vocab, received = lax.optimization_barrier((mine2, over_vocab, received))
    mine2 = take(mine2, y).astype(f32) + hop(take(mine2, 1 - y), dy=1).astype(f32)
    blocks = lax.all_to_all(over_vocab.reshape(-1, part, half), "dp", 0, 0, tiled=True)
    mine1 = jnp.sum(blocks.astype(f32), axis=0)
    mine1, mine2, late = lax.optimization_barrier((mine1, mine2, late_grad))
    late = lax.ppermute(late, "pipe", swap)

    own_first = pipe == 0
    normed_grad = jnp.concatenate(
        [jnp.where(own_first, mine1, mine2), jnp.where(own_first, mine2, mine1)], axis=1
    )
    upward = normed_grad * gain_wide
    inner_sum = jnp.sum(upward * hidden_mine, axis=1, keepdims=True)
    result = (
        inverse_mine * upward
        - hidden_mine * (inverse_mine * inverse_mine * inverse_mine) * inner_sum / width
    ).astype(bf16)
    along_x = put(jnp.zeros((NX, part, width), bf16), result, x)
    for dx in (1, 3, 2):
        along_x = put(along_x, hop(result, dx=dx), (x - dx) % NX)
    hidden_grad = put(jnp.zeros((NC, NX, part, width), bf16), along_x, c)
    hidden_grad = put(hidden_grad, hop(along_x, dc=1), 1 - c)
    received = jnp.concatenate([received, late], axis=0).astype(f32)
    table_grad = (own_grad + received).astype(bf16)
    return (hidden_grad.reshape(tok_rows, width), table_grad, token_loss)


def solution(mesh):
    placed = (P(("pipe", "dp"), None), P(), P(("pipe", "dp")), P(("vocab", "dp"), None))
    return jax.shard_map(
        on_device,
        mesh=mesh,
        in_specs=placed,
        out_specs=(P(("pipe", "dp"), None), P(("vocab", "dp"), "pipe"), P(("pipe", "dp"))),
        check_vma=False,
    )
```

time: 1070 us -> 265 us (0.25)
  waiting for transfers between devices: 696 us -> 118 us
  blocking collectives: 304 us -> 17.2 us
  starting transfers between devices: 0.34 us -> 43.4 us
  local copies, waits for them, and re-layouts: 0.6 us -> 12.1 us
    reduce_scatter x2 -> x1, waiting for transfers between devices: 375 us -> 0.02 us  [on_device(): lax.psum_scatter(sums1, 'vocab', scatter_dimension=0, tiled=True)]
    all_gather x1, waiting for transfers between devices: 269 us -> 0.01 us  [on_device(): rows1 = lax.all_gather(near.reshape(-1, half), 'vocab', axis=0, tiled=True)]
    pmax x1 -> x0, blocking collectives: 143 us -> none  [on_device(): row_top = lax.pmax(local_top, ('vocab', 'dp'))]
    psum x1 -> x0, blocking collectives: 141 us -> none  [on_device(): lax.psum((jnp.sum(jnp.exp(logits - row_top[:, None]), axis=1), picked), (...]
    ppermute x0 -> x23, waiting for transfers between devices: none -> 81.4 us  [the longest x21 69.5 us: hop(): return lax.ppermute(array, ('vocab', 'dp'), pairs)]
    psum x1 -> x0, waiting for transfers between devices: 52 us -> none  [on_device(): normed_grad = lax.psum(replica_sum, 'vocab').astype(jnp.float32)]
    all_to_all x0 -> x3, waiting for transfers between devices: none -> 36.7 us  [the longest x1 13.1 us: on_device(): wanted = lax.all_to_all(spread, 'dp', 0, 0, tiled=True)]
    ppermute x0 -> x23, starting transfers between devices: none -> 27.7 us  [the longest x21 21.6 us: hop(): return lax.ppermute(array, ('vocab', 'dp'), pairs)]
  transfers between devices with their start and end apart: 4 -> 28, of which waited for: 4 -> 18; matrix products, arithmetic and copies ran while one was open for 2% -> 14% of each run, Pallas kernels for 0% -> 0%
where the time goes in v2:
time: 265 us
  waiting for transfers between devices  118 us (45%)
  starting transfers between devices  43.4 us (16%)
  matrix products  42.9 us (16%)
  blocking collectives  17.2 us (6%)
  other arithmetic  15.9 us (6%)
  between operations  14.9 us (6%)
  local copies, waits for them, and re-layouts  12.1 us (5%)
    ppermute x21, waiting for transfers between devices, hop(): return lax.ppermute(array, ('vocab', 'dp'), pairs)  69.5 us
    dot_general x8, matrix products, dot(): lax.dot_general(a, b, (contract, ((), ())), preferred_element_type=jnp.fl...  42.9 us
    ppermute x21, starting transfers between devices, hop(): return lax.ppermute(array, ('vocab', 'dp'), pairs)  21.6 us
    all_to_all x1, blocking collectives, on_device(): stats = lax.all_to_all(stats, ('vocab', 'dp'), 0, 0, tiled=True)  17.2 us
    all_to_all x1, waiting for transfers between devices, on_device(): wanted = lax.all_to_all(spread, 'dp', 0, 0, tiled=True)  13.1 us
    all_to_all x1, waiting for transfers between devices, on_device(): lax.all_to_all(over_vocab.reshape(-1, part, half), 'dp', 0, 0, tiled=True)  12.5 us
    ppermute x1, waiting for transfers between devices, on_device(): late = lax.ppermute(late, 'pipe', swap)  11.9 us
    all_to_all x1, waiting for transfers between devices, on_device(): near = lax.all_to_all(seed, 'dp', 0, 0, tiled=True)  11.1 us
  transfers between devices with their start and end apart: 28, of which 18 were waited for; matrix products, arithmetic and copies ran while one was open for 14% of the time, Pallas kernels for 0%

profile of v2, /device:TPU:0, one launch (start us, length us, event | category | flops | bytes accessed | tf_op | source)
XLA Modules:
  0.0 264.6 jit_solution(15319591281787665911)
XLA Ops:
  8.2 1.1 multiply_reduce_fusion.2
  11.2 6.4 %all-to-all-start = ((bf16[8,16,3584]{2,1,0:T(8,128)(2,1)}), bf16[8,16,3584]{2,1,0:T(8,128)(2,1)S(1)}, u32[]{:S(2)}, u32[]{:S(2)}) async-start(bf16[8,16,3584]{2,1,0:T(8,128)(2,1)} %broadcast_in_dim.16), calls=%async_computation | async-start | bytes 1835008 | tf_op jit(solution)/shard_map/all_to_all | solution.py:69
  17.7 1.3 dynamic-slice_convert_fusion
  19.0 1.5 multiply_reduce_fusion
  20.8 11.1 %all-to-all-done = bf16[8,16,3584]{2,1,0:T(8,128)(2,1)S(1)} async-done(((bf16[8,16,3584]{2,1,0:T(8,128)(2,1)}), bf16[8,16,3584]{2,1,0:T(8,128)(2,1)S(1)}, u32[]{:S(2)}, u32[]{:S(2)}) %all-to-all-start) | async-done | bytes 917536 | tf_op jit(solution)/shard_map/all_to_all | solution.py:69
  33.4 2.7 %collective-permute-start.1 = (bf16[64,3584]{1,0:T(8,128)(2,1)S(1)}, bf16[64,3584]{1,0:T(8,128)(2,1)}, u32[]{:S(2)}, u32[]{:S(2)}) collective-permute-start(bf16[64,3584]{1,0:T(8,128)(2,1)S(1)} %fusion.20), channel_id=1, source_target_pairs={{0,6},{1,7},{2,0},{3,1},{4,2},{5,3},{6,4},{7,5},{8,14},{9,15},{10,... | collective-permute-start | bytes 1376264 | tf_op jit(solution)/shard_map/ppermute | solution.py:21
  36.7 5.4 %all-to-all-start.1 = ((s32[8,1,128]{2,1,0:T(1,128)}), s32[8,1,128]{2,1,0:T(1,128)S(1)}, u32[]{:S(2)}, u32[]{:S(2)}) async-start(s32[8,1,128]{2,1,0:T(1,128)} %broadcast_in_dim.19), calls=%async_computation.1 | async-start | bytes 8192 | tf_op jit(solution)/shard_map/all_to_all | solution.py:86
  42.3 13.1 %all-to-all-done.1 = s32[8,1,128]{2,1,0:T(1,128)S(1)} async-done(((s32[8,1,128]{2,1,0:T(1,128)}), s32[8,1,128]{2,1,0:T(1,128)S(1)}, u32[]{:S(2)}, u32[]{:S(2)}) %all-to-all-start.1) | async-done | bytes 4128 | tf_op jit(solution)/shard_map/all_to_all | solution.py:86
  56.8 1.1 bitcast_dynamic-update-slice_fusion.12
  57.8 1.1 bitcast_dynamic-update-slice_fusion.11
  59.1 1.3 collective-permute-start.5
  60.3 2.0 collective-permute-start.6
  64.1 9.1 %collective-permute-done.5 = bf16[64,3584]{1,0:T(8,128)(2,1)S(1)} collective-permute-done((bf16[64,3584]{1,0:T(8,128)(2,1)S(1)}, bf16[64,3584]{1,0:T(8,128)(2,1)S(1)}, u32[]{:S(2)}, u32[]{:S(2)}) %collective-permute-start.5) | collective-permute-done | bytes 458784 | tf_op jit(solution)/shard_map/ppermute | solution.py:21
  73.2 9.1 %collective-permute-done.6 = bf16[64,3584]{1,0:T(8,128)(2,1)S(1)} collective-permute-done((bf16[64,3584]{1,0:T(8,128)(2,1)S(1)}, bf16[64,3584]{1,0:T(8,128)(2,1)S(1)}, u32[]{:S(2)}, u32[]{:S(2)}) %collective-permute-start.6) | collective-permute-done | bytes 458784 | tf_op jit(solution)/shard_map/ppermute | solution.py:21
  82.4 1.2 collective-permute-done.7
  84.4 3.3 %collective-permute-done.8 = bf16[4,64,3584]{2,1,0:T(8,128)(2,1)S(1)} collective-permute-done((bf16[4,64,3584]{2,1,0:T(8,128)(2,1)S(1)}, bf16[4,64,3584]{2,1,0:T(8,128)(2,1)S(1)}, u32[]{:S(2)}, u32[]{:S(2)}) %collective-permute-start.8) | collective-permute-done | bytes 1835040 | tf_op jit(solution)/shard_map/ppermute | solution.py:21
  87.9 4.0 %fusion.14 = f32[4,2,4,2,16,512]{5,4,0,2,3,1:T(8,128)S(1)} fusion(bf16[2,2,4,4,16,3584]{5,4,3,2,1,0:T(8,128)(2,1)S(1)} %bitcast.109, bf16[512,7168]{1,0:T(8,128)(2,1)S(1)} %bitcast.132, s32[]{:T(128)S(6)} %select_n.192), kind=kOutput, calls=%fused_computation.29 | convolution fusion | flops 3758096384 | bytes 13107204 | tf_op jit(solution)/shard_map/dot_general | solution.py:37
  91.9 1.5 copy.25
  93.4 8.8 %fusion.35 = (f32[1024]{0:T(1024)S(1)}, f32[1024,512]{1,0:T(8,128)S(1)}) fusion(f32[4,2,4,2,16,512]{5,4,3,2,1,0:T(8,128)} %copy.25, bf16[1024,3584]{1,0:T(8,128)(2,1)} %all-gather.2.cloned.1.call-done, bf16[512,7168]{1,0:T(8,128)(2,1)} %param.7, s32[]{:T(128)S(6)} %select_n.193), kind=kOutput, calls=%fused_computation.95 | convolution fusion | flops 3759143936 | bytes 15208452 | tf_op jit(solution)/shard_map/dot_general | solution.py:37
  103.5 17.2 %all_to_all.28 = f32[64,1,1152]{2,1,0:T(1,128)S(1)} all-to-all(f32[64,1,1152]{2,1,0:T(1,128)S(1)} %all_to_all.20), channel_id=1, replica_groups=mesh['pipe'=2,'vocab'=8,'dp'=8] {'vocab','dp'}, dimensions={0} | all-to-all | bytes 589824 | tf_op jit(solution)/shard_map/all_to_all | solution.py:110
  121.5 1.1 convolution_convert_fusion.3
  122.6 4.4 %convolution_convert_fusion.2 = bf16[384,3584]{1,0:T(8,128)(2,1)} fusion(bf16[1024,3584]{1,0:T(8,128)(2,1)S(1)} %bitcast.111, bf16[1024,512]{1,0:T(8,128)(2,1)S(1)} %bitcast.120), kind=kOutput, calls=%fused_computation.4 | convolution fusion | flops 2819948544 | bytes 10878976 | tf_op jit(solution)/shard_map/dot_general | solution.py:37
  127.0 3.9 %convolution_convert_fusion.1 = bf16[512,3584]{1,0:T(8,128)(2,1)} fusion(bf16[512,7168]{1,0:T(8,128)(2,1)S(1)} %bitcast.134, s32[]{:T(128)S(6)} %select_n.192, bf16[2,512,512]{2,1,0:T(8,128)(2,1)S(1)} %bitcast.121, s32[]{:T(128)S(6)} %select_n.205), kind=kOutput, calls=%fused_computation.3 | convolution fusion | flops 1880883200 | bytes 7864328 | tf_op jit(solution)/shard_map/dot_general | solution.py:37
  130.9 6.1 %convolution_convert_fusion = bf16[1024,3584]{1,0:T(8,128)(2,1)} fusion(bf16[1024,512]{1,0:T(8,128)(2,1)S(1)} %fusion.13, bf16[512,7168]{1,0:T(8,128)(2,1)S(1)} %bitcast.134, s32[]{:T(128)S(6)} %select_n.193), kind=kOutput, calls=%fused_computation | convolution fusion | flops 3761766400 | bytes 12058628 | tf_op jit(solution)/shard_map/dot_general | solution.py:37
  137.3 3.0 %collective-permute-start.16 = (bf16[384,3584]{1,0:T(8,128)(2,1)}, bf16[384,3584]{1,0:T(8,128)(2,1)}, u32[]{:S(2)}, u32[]{:S(2)}) collective-permute-start(bf16[384,3584]{1,0:T(8,128)(2,1)} %convolution_convert_fusion.2), channel_id=1, source_target_pairs={{0,64},{64,0},{1,65},{65,1},{2,66},{66,2},{3,67},{67,3},{4,68},{68... | collective-permute-start | bytes 8257544 | tf_op jit(solution)/shard_map/ppermute | solution.py:132
  140.3 3.6 %collective-permute-done.9 = bf16[512,3584]{1,0:T(8,128)(2,1)} collective-permute-done((bf16[512,3584]{1,0:T(8,128)(2,1)}, bf16[512,3584]{1,0:T(8,128)(2,1)}, u32[]{:S(2)}, u32[]{:S(2)}) %collective-permute-start.9) | collective-permute-done | bytes 3670048 | tf_op jit(solution)/shard_map/ppermute | solution.py:21
  143.9 5.3 %add_convert_fusion.1 = bf16[512,3584]{1,0:T(8,128)(2,1)S(1)} fusion(bf16[512,3584]{1,0:T(8,128)(2,1)} %collective-permute-done.9, bf16[512,7168]{1,0:T(8,128)(2,1)} %param.7, s32[]{:T(128)S(6)} %select_n.192, bf16[2,512,512]{2,1,0:T(8,128)(2,1)S(1)} %bitcast.122, s32[]{:T(128)S(6)} %select_n.202), kind=kOutput, calls=%fused_computation.2 | convolution fusion | flops 1884553216 | bytes 11534344 | tf_op jit(solution)/shard_map/dot_general | solution.py:37
  150.5 2.3 collective-permute-start.11
  153.7 9.3 %fusion.36 = f32[512,3584]{1,0:T(8,128)} fusion(bf16[1024,512]{1,0:T(8,128)(2,1)S(1)} %fusion.13, bf16[1024,3584]{1,0:T(8,128)(2,1)} %all-gather.2.cloned.1.call-done), kind=kOutput, calls=%fused_computation.96 | convolution fusion | flops 3758096384 | bytes 15728640 | tf_op jit(solution)/shard_map/dot_general | solution.py:37
  163.0 10.9 %collective-permute-done.10 = bf16[2,4,16,3584]{3,2,1,0:T(8,128)(2,1)S(1)} collective-permute-done((bf16[2,4,16,3584]{3,2,1,0:T(8,128)(2,1)S(1)}, bf16[2,4,16,3584]{3,2,1,0:T(8,128)(2,1)S(1)}, u32[]{:S(2)}, u32[]{:S(2)}) %collective-permute-start.10) | collective-permute-done | bytes 917536 | tf_op jit(solution)/shard_map/ppermute | solution.py:21
  173.9 18.2 %collective-permute-done.11 = bf16[2,4,16,3584]{3,2,1,0:T(8,128)(2,1)S(1)} collective-permute-done((bf16[2,4,16,3584]{3,2,1,0:T(8,128)(2,1)S(1)}, bf16[2,4,16,3584]{3,2,1,0:T(8,128)(2,1)S(1)}, u32[]{:S(2)}, u32[]{:S(2)}) %collective-permute-start.11) | collective-permute-done | bytes 917536 | tf_op jit(solution)/shard_map/ppermute | solution.py:21
  193.4 1.0 collective-permute-start.13
  194.4 2.3 collective-permute-start.14
  197.7 5.6 %collective-permute-done.13 = bf16[2,16,3584]{2,1,0:T(8,128)(2,1)S(1)} collective-permute-done((bf16[2,16,3584]{2,1,0:T(8,128)(2,1)S(1)}, bf16[2,16,3584]{2,1,0:T(8,128)(2,1)S(1)}, u32[]{:S(2)}, u32[]{:S(2)}) %collective-permute-start.13) | collective-permute-done | bytes 229408 | tf_op jit(solution)/shard_map/ppermute | solution.py:21
  203.3 2.6 collective-permute-done.14
  206.7 1.0 collective-permute-start.17
  207.9 3.8 %all-to-all-start.3 = ((bf16[8,16,3584]{2,1,0:T(8,128)(2,1)}), bf16[8,16,3584]{2,1,0:T(8,128)(2,1)S(1)}, u32[]{:S(2)}, u32[]{:S(2)}) async-start(bf16[8,16,3584]{2,1,0:T(8,128)(2,1)} %bitcast.124), calls=%async_computation.4 | async-start | bytes 1835008 | tf_op jit(solution)/shard_map/all_to_all | solution.py:164
  211.7 12.5 %all-to-all-done.3 = bf16[8,16,3584]{2,1,0:T(8,128)(2,1)S(1)} async-done(((bf16[8,16,3584]{2,1,0:T(8,128)(2,1)}), bf16[8,16,3584]{2,1,0:T(8,128)(2,1)S(1)}, u32[]{:S(2)}, u32[]{:S(2)}) %all-to-all-start.3) | async-done | bytes 917536 | tf_op jit(solution)/shard_map/all_to_all | solution.py:164
  224.4 1.1 multiply_reduce_fusion.1
  225.6 1.1 bitcast_dynamic-update-slice_fusion.17
  228.4 2.3 collective-permute-start.19
  230.8 3.2 %collective-permute-start.22 = (bf16[128,3584]{1,0:T(8,128)(2,1)S(1)}, bf16[128,3584]{1,0:T(8,128)(2,1)S(1)}, u32[]{:S(2)}, u32[]{:S(2)}) collective-permute-start(bf16[128,3584]{1,0:T(8,128)(2,1)S(1)} %convolution_convert_fusion.3), channel_id=1, source_target_pairs={{0,64},{64,0},{1,65},{65,1},{2,66},{66,2},{3,67},{67,3},{4,68},{68... | collective-permute-start | bytes 2752520 | tf_op jit(solution)/shard_map/ppermute | solution.py:167
  234.0 2.0 collective-permute-done.18
  236.0 1.2 collective-permute-done.19
  237.2 1.2 collective-permute-done.20
  238.8 11.9 %collective-permute-done.22 = bf16[128,3584]{1,0:T(8,128)(2,1)S(1)} collective-permute-done((bf16[128,3584]{1,0:T(8,128)(2,1)S(1)}, bf16[128,3584]{1,0:T(8,128)(2,1)S(1)}, u32[]{:S(2)}, u32[]{:S(2)}) %collective-permute-start.22) | collective-permute-done | bytes 917536 | tf_op jit(solution)/shard_map/ppermute | solution.py:167
  250.7 5.7 %add_convert_fusion = bf16[512,3584]{1,0:T(8,128)(2,1)} fusion(f32[512,3584]{1,0:T(8,128)} %fusion.36, bf16[128,3584]{1,0:T(8,128)(2,1)S(1)} %collective-permute-done.22, bf16[384,3584]{1,0:T(8,128)(2,1)} %collective-permute-done.16), kind=kLoop, calls=%fused_computation.1 | loop fusion | flops 11010048 | bytes 14680064 | tf_op jit(solution)/shard_map/convert_element_type | solution.py:185
  256.5 1.2 copy-done.3
  (115 shorter events, 19.5 us)
Async XLA Ops:
  11.2 20.7 %all-to-all-start = ((bf16[8,16,3584]{2,1,0:T(8,128)(2,1)}), bf16[8,16,3584]{2,1,0:T(8,128)(2,1)S(1)}, u32[]{:S(2)}, u32[]{:S(2)}) async-start(bf16[8,16,3584]{2,1,0:T(8,128)(2,1)} %broadcast_in_dim.16), calls=%async_computation | async-start | bytes 1835008 | tf_op jit(solution)/shard_map/all_to_all | solution.py:69
  17.7 75.8 %all-gather.2.cloned.1.call-start = ((), (), s32[]{:S(2)}) async-start(), calls=%async_computation.5 | async-start | bytes 8257536 | tf_op jit(solution)/shard_map/all_gather | solution.py:73
  19.0 17.1 %copy-start.5 = (s32[128]{0:T(128)S(1)}, s32[128]{0:T(128)}, u32[]{:S(2)}) copy-start(s32[128]{0:T(128)} %param.6) | copy-start | bytes 1540
  31.9 4.1 %copy-start.2 = (bf16[8,16,3584]{2,1,0:T(8,128)(2,1)}, bf16[8,16,3584]{2,1,0:T(8,128)(2,1)S(1)}, u32[]{:S(2)}) copy-start(bf16[8,16,3584]{2,1,0:T(8,128)(2,1)S(1)} %all-to-all-done) | copy-start | bytes 2752516
  31.9 27.1 %collective-permute-start.4 = (bf16[64,3584]{1,0:T(8,128)(2,1)S(1)}, bf16[64,3584]{1,0:T(8,128)(2,1)S(1)}, u32[]{:S(2)}, u32[]{:S(2)}) collective-permute-start(bf16[64,3584]{1,0:T(8,128)(2,1)S(1)} %fusion.20), channel_id=1, source_target_pairs={{0,1},{1,0},{2,3},{3,2},{4,5},{5,4},{6,7},{7,6},{8,9},{9,8},{10,11... | collective-permute-start | bytes 1376264 | tf_op jit(solution)/shard_map/ppermute | solution.py:21
  32.8 24.0 %collective-permute-start = (bf16[64,3584]{1,0:T(8,128)(2,1)S(1)}, bf16[64,3584]{1,0:T(8,128)(2,1)}, u32[]{:S(2)}, u32[]{:S(2)}) collective-permute-start(bf16[64,3584]{1,0:T(8,128)(2,1)S(1)} %fusion.20), channel_id=1, source_target_pairs={{0,2},{1,3},{2,4},{3,5},{4,6},{5,7},{6,0},{7,1},{8,10},{9,11},{10,... | collective-permute-start | bytes 1376264 | tf_op jit(solution)/shard_map/ppermute | solution.py:21
  33.4 24.5 %collective-permute-start.1 = (bf16[64,3584]{1,0:T(8,128)(2,1)S(1)}, bf16[64,3584]{1,0:T(8,128)(2,1)}, u32[]{:S(2)}, u32[]{:S(2)}) collective-permute-start(bf16[64,3584]{1,0:T(8,128)(2,1)S(1)} %fusion.20), channel_id=1, source_target_pairs={{0,6},{1,7},{2,0},{3,1},{4,2},{5,3},{6,4},{7,5},{8,14},{9,15},{10,... | collective-permute-start | bytes 1376264 | tf_op jit(solution)/shard_map/ppermute | solution.py:21
  36.0 22.9 %collective-permute-start.2 = (bf16[64,3584]{1,0:T(8,128)(2,1)S(1)}, bf16[64,3584]{1,0:T(8,128)(2,1)S(1)}, u32[]{:S(2)}, u32[]{:S(2)}) collective-permute-start(bf16[64,3584]{1,0:T(8,128)(2,1)S(1)} %fusion.20), channel_id=1, source_target_pairs={{0,4},{1,5},{2,6},{3,7},{4,0},{5,1},{6,2},{7,3},{8,12},{9,13},{10,... | collective-permute-start | bytes 1376264 | tf_op jit(solution)/shard_map/ppermute | solution.py:21
  36.7 18.7 %all-to-all-start.1 = ((s32[8,1,128]{2,1,0:T(1,128)}), s32[8,1,128]{2,1,0:T(1,128)S(1)}, u32[]{:S(2)}, u32[]{:S(2)}) async-start(s32[8,1,128]{2,1,0:T(1,128)} %broadcast_in_dim.19), calls=%async_computation.1 | async-start | bytes 8192 | tf_op jit(solution)/shard_map/all_to_all | solution.py:86
  42.1 164.6 %reduce-scatter.2.cloned.1.call-start = ((), (), s32[]{:S(2)}) async-start(), calls=%async_computation.6 | async-start | bytes 8257536 | tf_op jit(solution)/shard_map/reduce_scatter | solution.py:138
  59.0 25.0 %collective-permute-start.3 = (bf16[4,64,3584]{2,1,0:T(8,128)(2,1)S(1)}, bf16[4,64,3584]{2,1,0:T(8,128)(2,1)S(1)}, u32[]{:S(2)}, u32[]{:S(2)}) collective-permute-start(bf16[4,64,3584]{2,1,0:T(8,128)(2,1)S(1)} %bitcast_dynamic-update-slice_fusion.10), channel_id=1, source_target_pairs={{0,8},{1,9},{2,10},{3,11},{4,12},{5,13},{6,14},{7,15},{8,0},{9,1},... | collective-permute-start | bytes 5505032 | tf_op jit(solution)/shard_map/ppermute | solution.py:21
  59.1 14.1 %collective-permute-start.5 = (bf16[64,3584]{1,0:T(8,128)(2,1)S(1)}, bf16[64,3584]{1,0:T(8,128)(2,1)S(1)}, u32[]{:S(2)}, u32[]{:S(2)}) collective-permute-start(bf16[64,3584]{1,0:T(8,128)(2,1)S(1)} %collective-permute-done.4), channel_id=1, source_target_pairs={{0,2},{1,3},{2,4},{3,5},{4,6},{5,7},{6,0},{7,1},{8,10},{9,11},{10,... | collective-permute-start | bytes 1376264 | tf_op jit(solution)/shard_map/ppermute | solution.py:21
  60.3 22.0 %collective-permute-start.6 = (bf16[64,3584]{1,0:T(8,128)(2,1)S(1)}, bf16[64,3584]{1,0:T(8,128)(2,1)S(1)}, u32[]{:S(2)}, u32[]{:S(2)}) collective-permute-start(bf16[64,3584]{1,0:T(8,128)(2,1)S(1)} %collective-permute-done.4), channel_id=1, source_target_pairs={{0,6},{1,7},{2,0},{3,1},{4,2},{5,3},{6,4},{7,5},{8,14},{9,15},{10,... | collective-permute-start | bytes 1376264 | tf_op jit(solution)/shard_map/ppermute | solution.py:21
  62.4 21.2 %collective-permute-start.7 = (bf16[64,3584]{1,0:T(8,128)(2,1)S(1)}, bf16[64,3584]{1,0:T(8,128)(2,1)S(1)}, u32[]{:S(2)}, u32[]{:S(2)}) collective-permute-start(bf16[64,3584]{1,0:T(8,128)(2,1)S(1)} %collective-permute-done.4), channel_id=1, source_target_pairs={{0,4},{1,5},{2,6},{3,7},{4,0},{5,1},{6,2},{7,3},{8,12},{9,13},{10,... | collective-permute-start | bytes 1376264 | tf_op jit(solution)/shard_map/ppermute | solution.py:21
  63.9 24.1 %slice-start = ((s8[7340032]{0:T(1024)(128)(4,1)}), s8[4194304]{0:T(1024)(128)(4,1)S(1)}, s32[]{:S(2)}) async-start(s8[7340032]{0:T(1024)(128)(4,1)} %bitcast.131), calls=%async_computation.7 | async-start | bytes 8388608
  83.6 4.3 %slice-start.1 = ((s8[7340032]{0:T(1024)(128)(4,1)}), s8[3145728]{0:T(1024)(128)(4,1)S(1)}, s32[]{:S(2)}) async-start(s8[7340032]{0:T(1024)(128)(4,1)} %bitcast.131), calls=%async_computation.8 | async-start | bytes 6291456
  83.7 4.0 %collective-permute-start.8 = (bf16[4,64,3584]{2,1,0:T(8,128)(2,1)S(1)}, bf16[4,64,3584]{2,1,0:T(8,128)(2,1)S(1)}, u32[]{:S(2)}, u32[]{:S(2)}) collective-permute-start(bf16[4,64,3584]{2,1,0:T(8,128)(2,1)S(1)} %bitcast_dynamic-update-slice_fusion.6), channel_id=1, source_target_pairs={{0,8},{1,9},{2,10},{3,11},{4,12},{5,13},{6,14},{7,15},{8,0},{9,1},... | collective-permute-start | bytes 5505032 | tf_op jit(solution)/shard_map/ppermute | solution.py:21
  87.9 4.0 %copy-start = (bf16[2,2,4,64,3584]{4,3,2,1,0:T(8,128)(2,1)}, bf16[2,2,4,64,3584]{4,3,2,1,0:T(8,128)(2,1)S(1)}, u32[]{:S(2)}) copy-start(bf16[2,2,4,64,3584]{4,3,2,1,0:T(8,128)(2,1)S(1)} %bitcast_dynamic-update-slice_fusion) | copy-start | bytes 22020100
  103.2 18.2 %copy-start.1 = (bf16[2,2,4,64,3584]{4,3,2,1,0:T(8,128)(2,1)S(1)}, bf16[2,2,4,64,3584]{4,3,2,1,0:T(8,128)(2,1)}, u32[]{:S(2)}) copy-start(bf16[2,2,4,64,3584]{4,3,2,1,0:T(8,128)(2,1)} %copy-done) | copy-start | bytes 22020100
  121.3 5.7 %slice-start.2 = ((s8[7340032]{0:T(1024)(128)(4,1)}), s8[4194304]{0:T(1024)(128)(4,1)S(1)}, s32[]{:S(2)}) async-start(s8[7340032]{0:T(1024)(128)(4,1)} %bitcast.133), calls=%async_computation.9 | async-start | bytes 8388608
  121.5 5.6 %slice-start.3 = ((s8[7340032]{0:T(1024)(128)(4,1)}), s8[3145728]{0:T(1024)(128)(4,1)S(1)}, s32[]{:S(2)}) async-start(s8[7340032]{0:T(1024)(128)(4,1)} %bitcast.133), calls=%async_computation.10 | async-start | bytes 6291456
  137.0 6.8 %collective-permute-start.9 = (bf16[512,3584]{1,0:T(8,128)(2,1)}, bf16[512,3584]{1,0:T(8,128)(2,1)}, u32[]{:S(2)}, u32[]{:S(2)}) collective-permute-start(bf16[512,3584]{1,0:T(8,128)(2,1)} %convolution_convert_fusion.1), channel_id=1, source_target_pairs={{0,8},{1,9},{2,10},{3,11},{4,12},{5,13},{6,14},{7,15},{8,0},{9,1},... | collective-permute-start | bytes 11010056 | tf_op jit(solution)/shard_map/ppermute | solution.py:21
  137.3 69.4 %collective-permute-start.16 = (bf16[384,3584]{1,0:T(8,128)(2,1)}, bf16[384,3584]{1,0:T(8,128)(2,1)}, u32[]{:S(2)}, u32[]{:S(2)}) collective-permute-start(bf16[384,3584]{1,0:T(8,128)(2,1)} %convolution_convert_fusion.2), channel_id=1, source_target_pairs={{0,64},{64,0},{1,65},{65,1},{2,66},{66,2},{3,67},{67,3},{4,68},{68... | collective-permute-start | bytes 8257544 | tf_op jit(solution)/shard_map/ppermute | solution.py:132
  149.5 24.4 %collective-permute-start.10 = (bf16[2,4,16,3584]{3,2,1,0:T(8,128)(2,1)S(1)}, bf16[2,4,16,3584]{3,2,1,0:T(8,128)(2,1)S(1)}, u32[]{:S(2)}, u32[]{:S(2)}) collective-permute-start(bf16[2,4,16,3584]{3,2,1,0:T(8,128)(2,1)S(1)} %bitcast.127), channel_id=1, source_target_pairs={{0,2},{1,3},{2,4},{3,5},{4,6},{5,7},{6,0},{7,1},{8,10},{9,11},{10,... | collective-permute-start | bytes 2752520 | tf_op jit(solution)/shard_map/ppermute | solution.py:21
  150.5 41.6 %collective-permute-start.11 = (bf16[2,4,16,3584]{3,2,1,0:T(8,128)(2,1)S(1)}, bf16[2,4,16,3584]{3,2,1,0:T(8,128)(2,1)S(1)}, u32[]{:S(2)}, u32[]{:S(2)}) collective-permute-start(bf16[2,4,16,3584]{3,2,1,0:T(8,128)(2,1)S(1)} %bitcast.126), channel_id=1, source_target_pairs={{0,6},{1,7},{2,0},{3,1},{4,2},{5,3},{6,4},{7,5},{8,14},{9,15},{10,... | collective-permute-start | bytes 2752520 | tf_op jit(solution)/shard_map/ppermute | solution.py:21
  152.8 40.1 %collective-permute-start.12 = (bf16[2,4,16,3584]{3,2,1,0:T(8,128)(2,1)S(1)}, bf16[2,4,16,3584]{3,2,1,0:T(8,128)(2,1)S(1)}, u32[]{:S(2)}, u32[]{:S(2)}) collective-permute-start(bf16[2,4,16,3584]{3,2,1,0:T(8,128)(2,1)S(1)} %bitcast.125), channel_id=1, source_target_pairs={{0,4},{1,5},{2,6},{3,7},{4,0},{5,1},{6,2},{7,3},{8,12},{9,13},{10,... | collective-permute-start | bytes 2752520 | tf_op jit(solution)/shard_map/ppermute | solution.py:21
  163.0 34.7 %copy-start.4 = (bf16[7168]{0:T(1024)(128)(2,1)S(1)}, bf16[7168]{0:T(1024)(128)(2,1)}, u32[]{:S(2)}) copy-start(bf16[7168]{0:T(1024)(128)(2,1)} %param.5) | copy-start | bytes 43012
  193.4 9.9 %collective-permute-start.13 = (bf16[2,16,3584]{2,1,0:T(8,128)(2,1)S(1)}, bf16[2,16,3584]{2,1,0:T(8,128)(2,1)S(1)}, u32[]{:S(2)}, u32[]{:S(2)}) collective-permute-start(bf16[2,16,3584]{2,1,0:T(8,128)(2,1)S(1)} %get-tuple-element.44), channel_id=1, source_target_pairs={{0,16},{1,17},{2,18},{3,19},{4,20},{5,21},{6,22},{7,23},{8,24},{9,... | collective-permute-start | bytes 688136 | tf_op jit(solution)/shard_map/ppermute | solution.py:21
  194.4 11.4 %collective-permute-start.14 = (bf16[2,16,3584]{2,1,0:T(8,128)(2,1)S(1)}, bf16[2,16,3584]{2,1,0:T(8,128)(2,1)S(1)}, u32[]{:S(2)}, u32[]{:S(2)}) collective-permute-start(bf16[2,16,3584]{2,1,0:T(8,128)(2,1)S(1)} %get-tuple-element.45), channel_id=1, source_target_pairs={{0,48},{1,49},{2,50},{3,51},{4,52},{5,53},{6,54},{7,55},{8,56},{9,... | collective-permute-start | bytes 688136 | tf_op jit(solution)/shard_map/ppermute | solution.py:21
  196.7 9.8 %collective-permute-start.15 = (bf16[2,16,3584]{2,1,0:T(8,128)(2,1)S(1)}, bf16[2,16,3584]{2,1,0:T(8,128)(2,1)S(1)}, u32[]{:S(2)}, u32[]{:S(2)}) collective-permute-start(bf16[2,16,3584]{2,1,0:T(8,128)(2,1)S(1)} %get-tuple-element.46), channel_id=1, source_target_pairs={{0,32},{1,33},{2,34},{3,35},{4,36},{5,37},{6,38},{7,39},{8,40},{9,... | collective-permute-start | bytes 688136 | tf_op jit(solution)/shard_map/ppermute | solution.py:21
  206.7 4.9 %collective-permute-start.17 = (bf16[16,3584]{1,0:T(8,128)(2,1)S(1)}, bf16[16,3584]{1,0:T(8,128)(2,1)S(1)}, u32[]{:S(2)}, u32[]{:S(2)}) collective-permute-start(bf16[16,3584]{1,0:T(8,128)(2,1)S(1)} %dynamic-slice_bitcast_fusion.4), channel_id=1, source_target_pairs={{0,1},{1,0},{2,3},{3,2},{4,5},{5,4},{6,7},{7,6},{8,9},{9,8},{10,11... | collective-permute-start | bytes 344072 | tf_op jit(solution)/shard_map/ppermute | solution.py:21
  207.9 16.3 %all-to-all-start.3 = ((bf16[8,16,3584]{2,1,0:T(8,128)(2,1)}), bf16[8,16,3584]{2,1,0:T(8,128)(2,1)S(1)}, u32[]{:S(2)}, u32[]{:S(2)}) async-start(bf16[8,16,3584]{2,1,0:T(8,128)(2,1)} %bitcast.124), calls=%async_computation.4 | async-start | bytes 1835008 | tf_op jit(solution)/shard_map/all_to_all | solution.py:164
  226.7 9.3 %collective-permute-start.18 = (bf16[16,7168]{1,0:T(8,128)(2,1)S(1)}, bf16[16,7168]{1,0:T(8,128)(2,1)S(1)}, u32[]{:S(2)}, u32[]{:S(2)}) collective-permute-start(bf16[16,7168]{1,0:T(8,128)(2,1)S(1)} %get-tuple-element.60), channel_id=1, source_target_pairs={{0,16},{1,17},{2,18},{3,19},{4,20},{5,21},{6,22},{7,23},{8,24},{9,... | collective-permute-start | bytes 688136 | tf_op jit(solution)/shard_map/ppermute | solution.py:21
  228.4 8.8 %collective-permute-start.19 = (bf16[16,7168]{1,0:T(8,128)(2,1)S(1)}, bf16[16,7168]{1,0:T(8,128)(2,1)S(1)}, u32[]{:S(2)}, u32[]{:S(2)}) collective-permute-start(bf16[16,7168]{1,0:T(8,128)(2,1)S(1)} %get-tuple-element.60), channel_id=1, source_target_pairs={{0,48},{1,49},{2,50},{3,51},{4,52},{5,53},{6,54},{7,55},{8,56},{9,... | collective-permute-start | bytes 688136 | tf_op jit(solution)/shard_map/ppermute | solution.py:21
  230.7 7.7 %collective-permute-start.20 = (bf16[16,7168]{1,0:T(8,128)(2,1)S(1)}, bf16[16,7168]{1,0:T(8,128)(2,1)S(1)}, u32[]{:S(2)}, u32[]{:S(2)}) collective-permute-start(bf16[16,7168]{1,0:T(8,128)(2,1)S(1)} %get-tuple-element.60), channel_id=1, source_target_pairs={{0,32},{1,33},{2,34},{3,35},{4,36},{5,37},{6,38},{7,39},{8,40},{9,... | collective-permute-start | bytes 688136 | tf_op jit(solution)/shard_map/ppermute | solution.py:21
  230.8 19.9 %collective-permute-start.22 = (bf16[128,3584]{1,0:T(8,128)(2,1)S(1)}, bf16[128,3584]{1,0:T(8,128)(2,1)S(1)}, u32[]{:S(2)}, u32[]{:S(2)}) collective-permute-start(bf16[128,3584]{1,0:T(8,128)(2,1)S(1)} %convolution_convert_fusion.3), channel_id=1, source_target_pairs={{0,64},{64,0},{1,65},{65,1},{2,66},{66,2},{3,67},{67,3},{4,68},{68... | collective-permute-start | bytes 2752520 | tf_op jit(solution)/shard_map/ppermute | solution.py:167
  238.4 17.9 %collective-permute-start.21 = (bf16[4,16,7168]{2,1,0:T(8,128)(2,1)S(1)}, bf16[4,16,7168]{2,1,0:T(8,128)(2,1)S(1)}, u32[]{:S(2)}, u32[]{:S(2)}) collective-permute-start(bf16[4,16,7168]{2,1,0:T(8,128)(2,1)S(1)} %bitcast_dynamic-update-slice_fusion.14), channel_id=1, source_target_pairs={{0,8},{1,9},{2,10},{3,11},{4,12},{5,13},{6,14},{7,15},{8,0},{9,1},... | collective-permute-start | bytes 2752520 | tf_op jit(solution)/shard_map/ppermute | solution.py:21
  256.5 1.2 copy-start.3
Sparse Core Ops, SparseCore 0:
  36.2 46.8 all-gather.1
  137.2 44.8 reduce-scatter.1

commit v3 on v2

--- a/solution.py
+++ b/solution.py
@@ -1,10 +1,13 @@
 import jax
 import jax.numpy as jnp
 from jax import lax
+from jax.experimental import pallas as pl
+from jax.experimental.pallas import tpu as pltpu
 from jax.sharding import PartitionSpec as P
 
 NORM_EPS = 1e-06
 NX, NC, NZ, NY = 4, 2, 4, 2
+DIGIT = 256
 
 
 def hop(array, dx=0, dc=0, dz=0, dy=0):
@@ -37,6 +40,44 @@
     return lax.dot_general(
         a, b, (contract, ((), ())), preferred_element_type=jnp.float32
     ).astype(out)
+
+
+def backward_kernel(place, hidden, gain, mine1, mine2, far, result):
+    part, width = hidden.shape
+    own = mine1[...]
+    other = mine2[...] + far[...].astype(jnp.float32)
+    first = place[1] == 0
+    grad = jnp.concatenate(
+        [jnp.where(first, own, other), jnp.where(first, other, own)], axis=1
+    )
+    wide = hidden[...].astype(jnp.float32)
+    inverse = lax.rsqrt(jnp.mean(wide * wide, axis=1, keepdims=True) + NORM_EPS)
+    upward = grad * gain[...].astype(jnp.float32)
+    inner_sum = jnp.sum(upward * wide, axis=1, keepdims=True)
+    result[...] = (
+        inverse * upward - wide * (inverse * inverse * inverse) * inner_sum / width
+    ).astype(jnp.bfloat16)
+
+
+def backward_call(place, hidden, gain, mine1, mine2, far, part):
+    width = hidden.shape[1]
+    whole = lambda a: pl.BlockSpec(a.shape, lambda i, p: (0, 0))
+    return pl.pallas_call(
+        backward_kernel,
+        grid_spec=pltpu.PrefetchScalarGridSpec(
+            num_scalar_prefetch=1,
+            grid=(1,),
+            in_specs=[
+                pl.BlockSpec((part, width), lambda i, p: (p[0], 0)),
+                pl.BlockSpec((1, width), lambda i, p: (0, 0)),
+                whole(mine1), whole(mine2), whole(far),
+            ],
+            out_specs=pl.BlockSpec((part, width), lambda i, p: (0, 0)),
+        ),
+        out_shape=jax.ShapeDtypeStruct((part, width), jnp.bfloat16),
+        compiler_params=pltpu.CompilerParams(vmem_limit_bytes=32 << 20),
+        name="backward",
+    )(place, hidden, gain.reshape(1, width), mine1, mine2, far)
 
 
 def on_device(hidden, gain, targets, table):
@@ -55,43 +96,53 @@
     own_col, other_col = pipe * half, (1 - pipe) * half
 
     gain_wide = gain.astype(f32)
+    place = jnp.stack([c * NX + x, pipe]).astype(jnp.int32)
 
     def scale(rows):
         wide = rows.astype(f32)
         inverse = lax.rsqrt(jnp.mean(wide * wide, axis=1, keepdims=True) + NORM_EPS)
-        return wide, inverse, (wide * inverse * gain_wide).astype(bf16)
-
-    hidden_mine, inverse_mine, normed_mine = scale(
-        lax.dynamic_slice_in_dim(hidden, first, part)
-    )
+        return (wide * inverse * gain_wide).astype(bf16)
+
+    normed_mine = scale(lax.dynamic_slice_in_dim(hidden, first, part))
     mine1 = lax.dynamic_slice(normed_mine, (0, own_col), (part, half))
-    seed = jnp.broadcast_to(mine1[None], (NZ * NY, part, half))
+    digits = jnp.stack([targets // DIGIT, targets % DIGIT]).astype(bf16)
+    digits = jnp.pad(digits, ((0, part - 2), (0, 0)))
+    seed = jnp.concatenate([mine1, digits], axis=1)
+    seed = jnp.broadcast_to(seed[None], (NZ * NY, part, half + tok_rows))
     near = lax.all_to_all(seed, "dp", 0, 0, tiled=True)
-    _, _, normed_side = scale(lax.dynamic_slice_in_dim(hidden, c * side, side))
+    normed_side = scale(lax.dynamic_slice_in_dim(hidden, c * side, side))
     mine2 = lax.dynamic_slice(normed_side, (0, other_col), (side, half))
-    mine2, near, targets = lax.optimization_barrier((mine2, near, targets))
-    rows1 = lax.all_gather(near.reshape(-1, half), "vocab", axis=0, tiled=True)
+    mine2, near = lax.optimization_barrier((mine2, near))
+    rows1 = lax.all_gather(near[:, :, :half].reshape(-1, half), "vocab", axis=0, tiled=True)
 
     partner = hop(mine2, dy=1)
     rows2 = jnp.zeros((NC, NY, NZ, side, half), bf16)
-    for block, at in ((mine2, y), (partner, 1 - y)):
-        gathered = put(jnp.zeros((NZ, side, half), bf16), block, z)
-        for dz in (1, 3, 2):
-            gathered = put(gathered, hop(block, dz=dz), (z - dz) % NZ)
-        rows2 = put(rows2, gathered, c, at)
-        rows2 = put(rows2, hop(gathered, dc=1), 1 - c, at)
+    own_rows = put(jnp.zeros((NZ, side, half), bf16), mine2, z)
+    far_rows = put(jnp.zeros((NZ, side, half), bf16), partner, z)
+    near1, near3, near2 = (hop(mine2, dz=dz) for dz in (1, 3, 2))
+    far2, far1, far3 = hop(partner, dz=2), hop(near1, dy=1), hop(near3, dy=1)
+    near2, far1 = lax.optimization_barrier((near2, far1))
+    for dz, near_block, far_block in ((1, near1, far1), (3, near3, far3), (2, near2, far2)):
+        own_rows = put(own_rows, near_block, (z - dz) % NZ)
+        far_rows = put(far_rows, far_block, (z - dz) % NZ)
+    for block, at in ((own_rows, y), (far_rows, 1 - y)):
+        rows2 = put(rows2, block, c, at)
+        rows2 = put(rows2, hop(block, dc=1), 1 - c, at)
     rows2 = rows2.reshape(-1, half)
 
-    spread = jnp.broadcast_to(targets.reshape(1, tok_rows), (NZ * NY, tok_rows))
-    wanted = lax.all_to_all(spread, "dp", 0, 0, tiled=True)
+    wanted = near[:, :2, half:].astype(jnp.int32)
+    wanted = wanted[:, 0] * DIGIT + wanted[:, 1]
     wanted = wanted.reshape(NZ * NY, NC, NX, part).transpose(2, 1, 0, 3).reshape(-1)
 
     table1 = lax.dynamic_slice(table, (0, own_col), (vocab_rows, half))
     table2 = lax.dynamic_slice(table, (0, other_col), (vocab_rows, half))
+    table1, table2, wanted = lax.optimization_barrier((table1, table2, wanted))
     logits1 = dot(rows1, table1, ((1,), (1,)))
     logits2 = dot(rows2, table2, ((1,), (1,)))
     logits2 = logits2.reshape(NC, NY, NZ, NX, part, vocab_rows).transpose(3, 0, 2, 1, 4, 5)
-    logits = logits1 + logits2.reshape(logits1.shape)
+    logits2 = logits2.reshape(logits1.shape)
+    logits1, logits2 = lax.optimization_barrier((logits1, logits2))
+    logits = logits1 + logits2
 
     first_row = (vocab * NZ * NY + dp) * vocab_rows
     columns = lax.broadcasted_iota(jnp.int32, (1, vocab_rows), 1) + first_row
@@ -121,30 +172,29 @@
     grad_b = grad_a.reshape(NX, NC, NZ, NY, part, vocab_rows).transpose(1, 3, 2, 0, 4, 5)
     grad_b = grad_b.reshape(NC, far, vocab_rows)
 
+    sums1 = dot(grad_a, table1, ((1,), (0,)), bf16)
+    sums1, grad_a, grad_b = lax.optimization_barrier((sums1, grad_a, grad_b))
+    over_vocab = lax.psum_scatter(sums1, "vocab", scatter_dimension=0, tiled=True)
+    sent = dot(take(grad_b, 1 - c), table2, ((1,), (0,)), bf16)
+    sent, grad_b = lax.optimization_barrier((sent, grad_b))
+    sent = hop(sent, dc=1)
+
     swap = [(0, 1), (1, 0)]
     early = vocab_rows * 3 // 4
     all_b = grad_b.reshape(-1, vocab_rows)
     sent_grad = dot(all_b[:, :early], rows2, ((0,), (0,)), bf16)
-    late_grad = dot(all_b[:, early:], rows2, ((0,), (0,)), bf16)
-    sent_grad, late_grad, grad_a, grad_b = lax.optimization_barrier(
-        (sent_grad, late_grad, grad_a, grad_b)
-    )
+    sent_grad, grad_b = lax.optimization_barrier((sent_grad, grad_b))
     received = lax.ppermute(sent_grad, "pipe", swap)
-    sent = dot(take(grad_b, 1 - c), table2, ((1,), (0,)), bf16)
-    sent, grad_a = lax.optimization_barrier((sent, grad_a))
-    sent = hop(sent, dc=1)
-    sums1 = dot(grad_a, table1, ((1,), (0,)), bf16)
-    sums1, grad_b = lax.optimization_barrier((sums1, grad_b))
-    over_vocab = lax.psum_scatter(sums1, "vocab", scatter_dimension=0, tiled=True)
+
     sums2 = (dot(take(grad_b, c), table2, ((1,), (0,))) + sent.astype(f32)).astype(bf16)
     sums2 = sums2.reshape(NY, NZ, side, half)
     z_blocks = [
         lax.dynamic_slice_in_dim(sums2, (z + dz) % NZ, 1, axis=1).reshape(NY, NX, part, half)
         for dz in range(NZ)
     ]
-    *z_blocks, grad_a = lax.optimization_barrier((*z_blocks, grad_a))
-
-    own_grad = dot(grad_a, rows1, ((0,), (0,)))
+    *z_blocks, grad_a, grad_b = lax.optimization_barrier((*z_blocks, grad_a, grad_b))
+    late_grad = dot(grad_b.reshape(-1, vocab_rows)[:, early:], rows2, ((0,), (0,)), bf16)
+    own_grad = dot(grad_a, rows1, ((0,), (0,)), bf16)
 
     total2 = z_blocks[0].astype(f32)
     for dz in (1, 3, 2):
@@ -154,35 +204,36 @@
         lax.dynamic_slice_in_dim(total2, (x + dx) % NX, 1, axis=1).reshape(NY, part, half)
         for dx in range(NX)
     ]
-    *x_blocks, own_grad = lax.optimization_barrier((*x_blocks, own_grad))
+    *x_blocks, own_grad, late_grad, over_vocab = lax.optimization_barrier(
+        (*x_blocks, own_grad, late_grad, over_vocab)
+    )
     mine2 = x_blocks[0].astype(f32)
     for dx in (1, 3, 2):
         mine2 = mine2 + hop(x_blocks[dx], dx=dx).astype(f32)
     mine2 = mine2.astype(bf16)
-    mine2, over_vocab, received = lax.optimization_barrier((mine2, over_vocab, received))
-    mine2 = take(mine2, y).astype(f32) + hop(take(mine2, 1 - y), dy=1).astype(f32)
     blocks = lax.all_to_all(over_vocab.reshape(-1, part, half), "dp", 0, 0, tiled=True)
     mine1 = jnp.sum(blocks.astype(f32), axis=0)
-    mine1, mine2, late = lax.optimization_barrier((mine1, mine2, late_grad))
+    mine1, mine2, received = lax.optimization_barrier((mine1, mine2, received))
+    far = hop(take(mine2, 1 - y), dy=1)
+    mine2 = take(mine2, y).astype(f32)
+    far, late, received = lax.optimization_barrier((far, late_grad, received))
     late = lax.ppermute(late, "pipe", swap)
 
-    own_first = pipe == 0
-    normed_grad = jnp.concatenate(
-        [jnp.where(own_first, mine1, mine2), jnp.where(own_first, mine2, mine1)], axis=1
-    )
-    upward = normed_grad * gain_wide
-    inner_sum = jnp.sum(upward * hidden_mine, axis=1, keepdims=True)
-    result = (
-        inverse_mine * upward
-        - hidden_mine * (inverse_mine * inverse_mine * inverse_mine) * inner_sum / width
-    ).astype(bf16)
+    result = backward_call(place, hidden, gain, mine1, mine2, far, part)
     along_x = put(jnp.zeros((NX, part, width), bf16), result, x)
     for dx in (1, 3, 2):
         along_x = put(along_x, hop(result, dx=dx), (x - dx) % NX)
     hidden_grad = put(jnp.zeros((NC, NX, part, width), bf16), along_x, c)
     hidden_grad = put(hidden_grad, hop(along_x, dc=1), 1 - c)
-    received = jnp.concatenate([received, late], axis=0).astype(f32)
-    table_grad = (own_grad + received).astype(bf16)
+    own_wide = own_grad.astype(f32)
+    table_grad = lax.dynamic_update_slice(
+        jnp.zeros((vocab_rows, half), bf16),
+        (own_wide[:early] + received.astype(f32)).astype(bf16),
+        (0, 0),
+    )
+    table_grad = lax.dynamic_update_slice(
+        table_grad, (own_wide[early:] + late.astype(f32)).astype(bf16), (early, 0)
+    )
     return (hidden_grad.reshape(tok_rows, width), table_grad, token_loss)
 
 

time: 265 us -> 252 us (0.951)
  waiting for transfers between devices: 118 us -> 90.4 us
  local copies, waits for them, and re-layouts: 12.1 us -> 30.5 us
  starting transfers between devices: 43.4 us -> 36.2 us
    all_to_all x1 -> x0, waiting for transfers between devices: 13.1 us -> none  [on_device(): wanted = lax.all_to_all(spread, 'dp', 0, 0, tiled=True)]
    dynamic_slice x0 -> x1, local copies, waits for them, and re-layouts: none -> 6.65 us  [on_device(): table2 = lax.dynamic_slice(table, (0, other_col), (vocab_rows, half))]
    dynamic_update_slice x17 -> x18, local copies, waits for them, and re-layouts: 3.35 us -> 9.99 us  [put(): return lax.dynamic_update_slice(buffer, block, start)]
    all_to_all x1, waiting for transfers between devices: 11.1 us -> 4.85 us  [on_device(): near = lax.all_to_all(seed, 'dp', 0, 0, tiled=True)]
    ppermute x21, waiting for transfers between devices: 69.5 us -> 63.5 us  [hop(): return lax.ppermute(array, ('vocab', 'dp'), pairs)]
    all_to_all x1 -> x0, starting transfers between devices: 5.41 us -> none  [on_device(): wanted = lax.all_to_all(spread, 'dp', 0, 0, tiled=True)]
    all_to_all x1, waiting for transfers between devices: 12.5 us -> 7.18 us  [on_device(): lax.all_to_all(over_vocab.reshape(-1, part, half), 'dp', 0, 0, tiled=True)]
    convert_element_type x4 -> x6, other arithmetic: 5.92 us -> 7.28 us  [the longest x1 3.06 us: on_device(): own_wide = own_grad.astype(f32)]
  transfers between devices with their start and end apart: 28 -> 27, of which waited for: 18 -> 14; matrix products, arithmetic and copies ran while one was open for 14% -> 26% of each run, Pallas kernels for 0% -> 0%
where the time goes in v3:
time: 252 us
  waiting for transfers between devices  90.4 us (36%)
  matrix products  43.6 us (17%)
  starting transfers between devices  36.2 us (14%)
  local copies, waits for them, and re-layouts  30.5 us (12%)
  other arithmetic  17.7 us (7%)
  blocking collectives  17.7 us (7%)
  between operations  14.8 us (6%)
    ppermute x21, waiting for transfers between devices, hop(): return lax.ppermute(array, ('vocab', 'dp'), pairs)  63.5 us
    dot_general x8, matrix products, dot(): lax.dot_general(a, b, (contract, ((), ())), preferred_element_type=jnp.fl...  43.6 us
    ppermute x21, starting transfers between devices, hop(): return lax.ppermute(array, ('vocab', 'dp'), pairs)  21.4 us
    all_to_all x1, blocking collectives, on_device(): stats = lax.all_to_all(stats, ('vocab', 'dp'), 0, 0, tiled=True)  17.7 us
    ppermute x1, waiting for transfers between devices, on_device(): late = lax.ppermute(late, 'pipe', swap)  12.9 us
    dynamic_update_slice x18, local copies, waits for them, and re-layouts, put(): return lax.dynamic_update_slice(buffer, block, start)  9.99 us
    all_to_all x1, waiting for transfers between devices, on_device(): lax.all_to_all(over_vocab.reshape(-1, part, half), 'dp', 0, 0, tiled=True)  7.18 us
    dynamic_slice x1, local copies, waits for them, and re-layouts, on_device(): table2 = lax.dynamic_slice(table, (0, other_col), (vocab_rows, half))  6.65 us
  transfers between devices with their start and end apart: 27, of which 14 were waited for; matrix products, arithmetic and copies ran while one was open for 26% of the time, Pallas kernels for 0%

profile of v3, /device:TPU:0, one launch (start us, length us, event | category | flops | bytes accessed | tf_op | source)
XLA Modules:
  0.0 251.7 jit_solution(1014888268179137722)
XLA Ops:
  8.3 1.1 multiply_reduce_fusion.1
  12.1 6.4 %all-to-all-start = ((bf16[8,16,3712]{2,1,0:T(8,128)(2,1)}), bf16[8,16,3712]{2,1,0:T(8,128)(2,1)S(1)}, u32[]{:S(2)}, u32[]{:S(2)}) async-start(bf16[8,16,3712]{2,1,0:T(8,128)(2,1)} %broadcast_in_dim.14), calls=%async_computation | async-start | bytes 1900544 | tf_op jit(solution)/shard_map/all_to_all | solution.py:112
  18.6 1.4 dynamic-slice_convert_fusion
  20.4 6.7 %constant_dynamic-slice_fusion.5 = (bf16[512,3584]{1,0:T(8,128)(2,1)}, bf16[512,3584]{1,0:T(8,128)(2,1)}) fusion(bf16[512,7168]{1,0:T(8,128)(2,1)} %param.7, s32[]{:T(128)S(6)} %select_n.189, s32[]{:T(128)S(6)} %select_n.191), kind=kLoop, calls=%fused_computation.78 | loop fusion | bytes 14680072 | tf_op jit(solution)/shard_map/dynamic_slice | solution.py:138
  27.0 1.3 fusion.11
  28.3 4.9 %all-to-all-done = bf16[8,16,3712]{2,1,0:T(8,128)(2,1)S(1)} async-done(((bf16[8,16,3712]{2,1,0:T(8,128)(2,1)}), bf16[8,16,3712]{2,1,0:T(8,128)(2,1)S(1)}, u32[]{:S(2)}, u32[]{:S(2)}) %all-to-all-start) | async-done | bytes 950304 | tf_op jit(solution)/shard_map/all_to_all | solution.py:112
  33.2 2.3 collective-permute-start.2
  35.5 1.2 collective-permute-start.5
  38.4 1.4 broadcast.83.clone
  40.7 14.4 %collective-permute-done = bf16[64,3584]{1,0:T(8,128)(2,1)} collective-permute-done((bf16[64,3584]{1,0:T(8,128)(2,1)S(1)}, bf16[64,3584]{1,0:T(8,128)(2,1)}, u32[]{:S(2)}, u32[]{:S(2)}) %collective-permute-start) | collective-permute-done | bytes 458784 | tf_op jit(solution)/shard_map/ppermute | solution.py:24
  55.7 1.4 collective-permute-start.6
  57.2 2.0 collective-permute-start.7
  60.3 1.8 bitcast_dynamic-update-slice_fusion.12
  62.1 1.8 bitcast_dynamic-update-slice_fusion.11
  64.0 3.3 %collective-permute-done.3 = bf16[64,3584]{1,0:T(8,128)(2,1)S(1)} collective-permute-done((bf16[64,3584]{1,0:T(8,128)(2,1)}, bf16[64,3584]{1,0:T(8,128)(2,1)S(1)}, u32[]{:S(2)}, u32[]{:S(2)}) %collective-permute-start.3) | collective-permute-done | bytes 458784 | tf_op jit(solution)/shard_map/ppermute | solution.py:24
  67.2 1.8 bitcast_dynamic-update-slice_fusion.10
  69.1 3.0 %collective-permute-done.6 = bf16[64,3584]{1,0:T(8,128)(2,1)S(1)} collective-permute-done((bf16[64,3584]{1,0:T(8,128)(2,1)}, bf16[64,3584]{1,0:T(8,128)(2,1)S(1)}, u32[]{:S(2)}, u32[]{:S(2)}) %collective-permute-start.6) | collective-permute-done | bytes 458784 | tf_op jit(solution)/shard_map/ppermute | solution.py:24
  73.0 1.7 bitcast_dynamic-update-slice_fusion.3
  77.4 4.0 %fusion.7 = f32[4,2,4,2,16,512]{5,4,0,2,3,1:T(8,128)S(1)} fusion(bf16[2,2,4,4,16,3584]{5,4,3,2,1,0:T(8,128)(2,1)S(1)} %bitcast.120, bf16[512,3584]{1,0:T(8,128)(2,1)S(1)} %copy-done.5), kind=kOutput, calls=%fused_computation.26 | convolution fusion | flops 3758096384 | bytes 13107200 | tf_op jit(solution)/shard_map/dot_general | solution.py:40
  81.3 1.5 copy.35
  82.8 1.9 all-gather.2.cloned.1.call-done
  84.7 7.5 %fusion.33 = f32[1024,512]{1,0:T(8,128)S(1)} fusion(bf16[1024,3584]{1,0:T(8,128)(2,1)} %all-gather.2.cloned.1.call-done, bf16[512,3584]{1,0:T(8,128)(2,1)} %get-tuple-element.39), kind=kOutput, calls=%fused_computation.105 | convolution fusion | flops 3758096384 | bytes 13107200 | tf_op jit(solution)/shard_map/dot_general | solution.py:40
  92.5 1.3 copy-done.2
  95.0 17.7 %all_to_all.22 = f32[64,1,1152]{2,1,0:T(1,128)S(1)} all-to-all(f32[64,1,1152]{2,1,0:T(1,128)S(1)} %all_to_all.15), channel_id=1, replica_groups=mesh['pipe'=2,'vocab'=8,'dp'=8] {'vocab','dp'}, dimensions={0} | all-to-all | bytes 589824 | tf_op jit(solution)/shard_map/all_to_all | solution.py:161
  113.4 6.1 %convolution_convert_fusion = bf16[1024,3584]{1,0:T(8,128)(2,1)} fusion(bf16[1024,512]{1,0:T(8,128)(2,1)S(1)} %fusion.5, bf16[512,3584]{1,0:T(8,128)(2,1)S(1)} %copy-done.7), kind=kOutput, calls=%fused_computation | convolution fusion | flops 3761766400 | bytes 12058624 | tf_op jit(solution)/shard_map/dot_general | solution.py:40
  120.6 6.1 %convolution_convert_fusion.2 = bf16[512,3584]{1,0:T(8,128)(2,1)} fusion(bf16[512,3584]{1,0:T(8,128)(2,1)} %get-tuple-element.43, bf16[2,512,512]{2,1,0:T(8,128)(2,1)} %bitcast.133, s32[]{:T(128)S(6)} %select_n.205), kind=kOutput, calls=%fused_computation.3 | convolution fusion | flops 1880883200 | bytes 7864324 | tf_op jit(solution)/shard_map/dot_general | solution.py:40
  126.8 8.1 %convolution_convert_fusion.3 = bf16[384,3584]{1,0:T(8,128)(2,1)} fusion(bf16[1024,3584]{1,0:T(8,128)(2,1)} %bitcast.121, bf16[1024,512]{1,0:T(8,128)(2,1)} %bitcast.134), kind=kOutput, calls=%fused_computation.4 | convolution fusion | flops 2819948544 | bytes 10878976 | tf_op jit(solution)/shard_map/dot_general | solution.py:40
  134.9 2.9 %collective-permute-start.16 = (bf16[384,3584]{1,0:T(8,128)(2,1)}, bf16[384,3584]{1,0:T(8,128)(2,1)}, u32[]{:S(2)}, u32[]{:S(2)}) collective-permute-start(bf16[384,3584]{1,0:T(8,128)(2,1)} %convolution_convert_fusion.3), channel_id=1, source_target_pairs={{0,64},{64,0},{1,65},{65,1},{2,66},{66,2},{3,67},{67,3},{4,68},{68... | collective-permute-start | bytes 8257544 | tf_op jit(solution)/shard_map/ppermute | solution.py:187
  137.8 4.2 %add_convert_fusion = bf16[512,3584]{1,0:T(8,128)(2,1)S(1)} fusion(bf16[512,3584]{1,0:T(8,128)(2,1)} %collective-permute-done.9, bf16[512,3584]{1,0:T(8,128)(2,1)S(1)} %copy-done.6, bf16[2,512,512]{2,1,0:T(8,128)(2,1)S(1)} %bitcast.135, s32[]{:T(128)S(6)} %select_n.202), kind=kOutput, calls=%fused_computation.1 | convolution fusion | flops 1884553216 | bytes 11534340 | tf_op jit(solution)/shard_map/dot_general | solution.py:40
  143.4 2.2 collective-permute-start.11
  146.2 2.1 convolution_convert_fusion.4
  148.3 5.5 %convolution_convert_fusion.1 = bf16[512,3584]{1,0:T(8,128)(2,1)} fusion(bf16[1024,512]{1,0:T(8,128)(2,1)S(1)} %fusion.5, bf16[1024,3584]{1,0:T(8,128)(2,1)S(1)} %bitcast.146), kind=kOutput, calls=%fused_computation.2 | convolution fusion | flops 3759931392 | bytes 12058624 | tf_op jit(solution)/shard_map/dot_general | solution.py:40
  153.8 31.7 %collective-permute-done.10 = bf16[2,4,16,3584]{3,2,1,0:T(8,128)(2,1)S(1)} collective-permute-done((bf16[2,4,16,3584]{3,2,1,0:T(8,128)(2,1)S(1)}, bf16[2,4,16,3584]{3,2,1,0:T(8,128)(2,1)S(1)}, u32[]{:S(2)}, u32[]{:S(2)}) %collective-permute-start.10) | collective-permute-done | bytes 917536 | tf_op jit(solution)/shard_map/ppermute | solution.py:24
  188.0 2.2 collective-permute-start.14
  191.4 4.2 %all-to-all-start.2 = ((bf16[8,16,3584]{2,1,0:T(8,128)(2,1)}), bf16[8,16,3584]{2,1,0:T(8,128)(2,1)S(1)}, u32[]{:S(2)}, u32[]{:S(2)}) async-start(bf16[8,16,3584]{2,1,0:T(8,128)(2,1)} %bitcast.138), calls=%async_computation.3 | async-start | bytes 1835008 | tf_op jit(solution)/shard_map/all_to_all | solution.py:214
  195.7 1.1 collective-permute-done.13
  196.8 2.6 %collective-permute-done.14 = bf16[2,16,3584]{2,1,0:T(8,128)(2,1)} collective-permute-done((bf16[2,16,3584]{2,1,0:T(8,128)(2,1)}, bf16[2,16,3584]{2,1,0:T(8,128)(2,1)}, u32[]{:S(2)}, u32[]{:S(2)}) %collective-permute-start.14) | collective-permute-done | bytes 229408 | tf_op jit(solution)/shard_map/ppermute | solution.py:24
  200.2 1.3 add_convert_fusion.2
  201.4 7.2 %all-to-all-done.2 = bf16[8,16,3584]{2,1,0:T(8,128)(2,1)S(1)} async-done(((bf16[8,16,3584]{2,1,0:T(8,128)(2,1)}), bf16[8,16,3584]{2,1,0:T(8,128)(2,1)S(1)}, u32[]{:S(2)}, u32[]{:S(2)}) %all-to-all-start.2) | async-done | bytes 917536 | tf_op jit(solution)/shard_map/all_to_all | solution.py:214
  208.8 1.7 collective-permute-start.17
  211.1 3.1 %convert_element_type.129 = f32[512,3584]{1,0:T(8,128)S(1)} convert(bf16[512,3584]{1,0:T(8,128)(2,1)} %convolution_convert_fusion.1) | non-fusion elementwise | flops 1835008 | bytes 11010048 | tf_op jit(solution)/shard_map/convert_element_type | solution.py:228
  215.7 2.6 %collective-permute-start.19 = (bf16[16,7168]{1,0:T(8,128)(2,1)S(1)}, bf16[16,7168]{1,0:T(8,128)(2,1)S(1)}, u32[]{:S(2)}, u32[]{:S(2)}) collective-permute-start(bf16[16,7168]{1,0:T(8,128)(2,1)S(1)} %backward.1), channel_id=1, source_target_pairs={{0,48},{1,49},{2,50},{3,51},{4,52},{5,53},{6,54},{7,55},{8,56},{9,... | collective-permute-start | bytes 688136 | tf_op jit(solution)/shard_map/ppermute | solution.py:24
  219.0 1.2 collective-permute-start.22
  220.3 2.7 %fusion = bf16[384,3584]{1,0:T(8,128)(2,1)S(1)} fusion(f32[512,3584]{1,0:T(8,128)S(1)} %convert_element_type.129, bf16[384,3584]{1,0:T(8,128)(2,1)} %collective-permute-done.16), kind=kLoop, calls=%fused_computation.6 | loop fusion | flops 4128768 | bytes 11010048 | tf_op jit(solution)/shard_map/convert_element_type | solution.py:231
  222.9 5.0 %collective-permute-done.18 = bf16[16,7168]{1,0:T(8,128)(2,1)S(1)} collective-permute-done((bf16[16,7168]{1,0:T(8,128)(2,1)S(1)}, bf16[16,7168]{1,0:T(8,128)(2,1)S(1)}, u32[]{:S(2)}, u32[]{:S(2)}) %collective-permute-start.18) | collective-permute-done | bytes 229408 | tf_op jit(solution)/shard_map/ppermute | solution.py:24
  228.4 12.9 %collective-permute-done.22 = bf16[128,3584]{1,0:T(8,128)(2,1)S(1)} collective-permute-done((bf16[128,3584]{1,0:T(8,128)(2,1)S(1)}, bf16[128,3584]{1,0:T(8,128)(2,1)S(1)}, u32[]{:S(2)}, u32[]{:S(2)}) %collective-permute-start.22) | collective-permute-done | bytes 917536 | tf_op jit(solution)/shard_map/ppermute | solution.py:220
  241.5 2.1 pad_maximum_fusion
  243.7 1.2 copy-done.9
  (132 shorter events, 25.4 us)
Async XLA Ops:
  7.2 11.4 %copy-start = (bf16[128,7168]{1,0:T(8,128)(2,1)S(1)}, bf16[128,7168]{1,0:T(8,128)(2,1)}, u32[]{:S(2)}) copy-start(bf16[128,7168]{1,0:T(8,128)(2,1)} %hidden.1) | copy-start | bytes 5505028
  12.1 21.1 %all-to-all-start = ((bf16[8,16,3712]{2,1,0:T(8,128)(2,1)}), bf16[8,16,3712]{2,1,0:T(8,128)(2,1)S(1)}, u32[]{:S(2)}, u32[]{:S(2)}) async-start(bf16[8,16,3712]{2,1,0:T(8,128)(2,1)} %broadcast_in_dim.14), calls=%async_computation | async-start | bytes 1900544 | tf_op jit(solution)/shard_map/all_to_all | solution.py:112
  18.6 66.2 %all-gather.2.cloned.1.call-start = ((), (), s32[]{:S(2)}) async-start(), calls=%async_computation.4 | async-start | bytes 8257536 | tf_op jit(solution)/shard_map/all_gather | solution.py:116
  33.2 21.9 %collective-permute-start = (bf16[64,3584]{1,0:T(8,128)(2,1)S(1)}, bf16[64,3584]{1,0:T(8,128)(2,1)}, u32[]{:S(2)}, u32[]{:S(2)}) collective-permute-start(bf16[64,3584]{1,0:T(8,128)(2,1)S(1)} %fusion.11), channel_id=1, source_target_pairs={{0,2},{1,3},{2,4},{3,5},{4,6},{5,7},{6,0},{7,1},{8,10},{9,11},{10,... | collective-permute-start | bytes 1376264 | tf_op jit(solution)/shard_map/ppermute | solution.py:24
  33.2 30.8 %collective-permute-start.2 = (bf16[64,3584]{1,0:T(8,128)(2,1)S(1)}, bf16[64,3584]{1,0:T(8,128)(2,1)}, u32[]{:S(2)}, u32[]{:S(2)}) collective-permute-start(bf16[64,3584]{1,0:T(8,128)(2,1)S(1)} %fusion.11), channel_id=1, source_target_pairs={{0,4},{1,5},{2,6},{3,7},{4,0},{5,1},{6,2},{7,3},{8,12},{9,13},{10,... | collective-permute-start | bytes 1376264 | tf_op jit(solution)/shard_map/ppermute | solution.py:24
  35.5 21.6 %collective-permute-start.5 = (bf16[64,3584]{1,0:T(8,128)(2,1)S(1)}, bf16[64,3584]{1,0:T(8,128)(2,1)}, u32[]{:S(2)}, u32[]{:S(2)}) collective-permute-start(bf16[64,3584]{1,0:T(8,128)(2,1)S(1)} %fusion.11), channel_id=1, source_target_pairs={{0,1},{1,0},{2,3},{3,2},{4,5},{5,4},{6,7},{7,6},{8,9},{9,8},{10,11... | collective-permute-start | bytes 1376264 | tf_op jit(solution)/shard_map/ppermute | solution.py:24
  36.7 19.1 %collective-permute-start.1 = (bf16[64,3584]{1,0:T(8,128)(2,1)S(1)}, bf16[64,3584]{1,0:T(8,128)(2,1)}, u32[]{:S(2)}, u32[]{:S(2)}) collective-permute-start(bf16[64,3584]{1,0:T(8,128)(2,1)S(1)} %fusion.11), channel_id=1, source_target_pairs={{0,6},{1,7},{2,0},{3,1},{4,2},{5,3},{6,4},{7,5},{8,14},{9,15},{10,... | collective-permute-start | bytes 1376264 | tf_op jit(solution)/shard_map/ppermute | solution.py:24
  38.3 148.6 %reduce-scatter.2.cloned.1.call-start = ((), (), s32[]{:S(2)}) async-start(), calls=%async_computation.5 | async-start | bytes 8257536 | tf_op jit(solution)/shard_map/reduce_scatter | solution.py:177
  55.1 12.1 %collective-permute-start.3 = (bf16[64,3584]{1,0:T(8,128)(2,1)}, bf16[64,3584]{1,0:T(8,128)(2,1)S(1)}, u32[]{:S(2)}, u32[]{:S(2)}) collective-permute-start(bf16[64,3584]{1,0:T(8,128)(2,1)} %collective-permute-done), channel_id=1, source_target_pairs={{0,1},{1,0},{2,3},{3,2},{4,5},{5,4},{6,7},{7,6},{8,9},{9,8},{10,11... | collective-permute-start | bytes 1376264 | tf_op jit(solution)/shard_map/ppermute | solution.py:24
  55.7 16.4 %collective-permute-start.6 = (bf16[64,3584]{1,0:T(8,128)(2,1)}, bf16[64,3584]{1,0:T(8,128)(2,1)S(1)}, u32[]{:S(2)}, u32[]{:S(2)}) collective-permute-start(bf16[64,3584]{1,0:T(8,128)(2,1)} %collective-permute-done.1), channel_id=1, source_target_pairs={{0,1},{1,0},{2,3},{3,2},{4,5},{5,4},{6,7},{7,6},{8,9},{9,8},{10,11... | collective-permute-start | bytes 1376264 | tf_op jit(solution)/shard_map/ppermute | solution.py:24
  57.2 15.0 %collective-permute-start.7 = (bf16[64,3584]{1,0:T(8,128)(2,1)}, bf16[64,3584]{1,0:T(8,128)(2,1)S(1)}, u32[]{:S(2)}, u32[]{:S(2)}) collective-permute-start(bf16[64,3584]{1,0:T(8,128)(2,1)} %collective-permute-done.5), channel_id=1, source_target_pairs={{0,4},{1,5},{2,6},{3,7},{4,0},{5,1},{6,2},{7,3},{8,12},{9,13},{10,... | collective-permute-start | bytes 1376264 | tf_op jit(solution)/shard_map/ppermute | solution.py:24
  69.0 5.7 %collective-permute-start.4 = (bf16[4,64,3584]{2,1,0:T(8,128)(2,1)}, bf16[4,64,3584]{2,1,0:T(8,128)(2,1)S(1)}, u32[]{:S(2)}, u32[]{:S(2)}) collective-permute-start(bf16[4,64,3584]{2,1,0:T(8,128)(2,1)} %bitcast_dynamic-update-slice_fusion.10), channel_id=1, source_target_pairs={{0,8},{1,9},{2,10},{3,11},{4,12},{5,13},{6,14},{7,15},{8,0},{9,1},... | collective-permute-start | bytes 5505032 | tf_op jit(solution)/shard_map/ppermute | solution.py:24
  72.2 3.9 %collective-permute-start.8 = (bf16[4,64,3584]{2,1,0:T(8,128)(2,1)S(1)}, bf16[4,64,3584]{2,1,0:T(8,128)(2,1)S(1)}, u32[]{:S(2)}, u32[]{:S(2)}) collective-permute-start(bf16[4,64,3584]{2,1,0:T(8,128)(2,1)S(1)} %bitcast_dynamic-update-slice_fusion.6), channel_id=1, source_target_pairs={{0,8},{1,9},{2,10},{3,11},{4,12},{5,13},{6,14},{7,15},{8,0},{9,1},... | collective-permute-start | bytes 5505032 | tf_op jit(solution)/shard_map/ppermute | solution.py:24
  75.2 2.2 copy-start.5
  76.3 5.0 %copy-start.1 = (bf16[2,2,4,64,3584]{4,3,2,1,0:T(8,128)(2,1)}, bf16[2,2,4,64,3584]{4,3,2,1,0:T(8,128)(2,1)S(1)}, u32[]{:S(2)}) copy-start(bf16[2,2,4,64,3584]{4,3,2,1,0:T(8,128)(2,1)S(1)} %bitcast_dynamic-update-slice_fusion) | copy-start | bytes 22020100
  84.7 7.5 %copy-start.4 = (f32[4,2,4,2,16,512]{5,4,3,2,1,0:T(8,128)S(1)}, f32[4,2,4,2,16,512]{5,4,3,2,1,0:T(8,128)}, u32[]{:S(2)}) copy-start(f32[4,2,4,2,16,512]{5,4,3,2,1,0:T(8,128)} %copy.35) | copy-start | bytes 6291460
  92.5 1.3 copy-start.2
  94.8 18.1 %copy-start.3 = (f32[1024,512]{1,0:T(8,128)S(1)}, f32[1024,512]{1,0:T(8,128)}, u32[]{:S(2)}) copy-start(f32[1024,512]{1,0:T(8,128)} %copy-done.2) | copy-start | bytes 6291460
  94.8 18.6 %copy-start.7 = (bf16[512,3584]{1,0:T(8,128)(2,1)S(1)}, bf16[512,3584]{1,0:T(8,128)(2,1)}, u32[]{:S(2)}) copy-start(bf16[512,3584]{1,0:T(8,128)(2,1)} %get-tuple-element.39) | copy-start | bytes 11010052
  126.7 11.1 %collective-permute-start.9 = (bf16[512,3584]{1,0:T(8,128)(2,1)}, bf16[512,3584]{1,0:T(8,128)(2,1)}, u32[]{:S(2)}, u32[]{:S(2)}) collective-permute-start(bf16[512,3584]{1,0:T(8,128)(2,1)} %convolution_convert_fusion.2), channel_id=1, source_target_pairs={{0,8},{1,9},{2,10},{3,11},{4,12},{5,13},{6,14},{7,15},{8,0},{9,1},... | collective-permute-start | bytes 11010056 | tf_op jit(solution)/shard_map/ppermute | solution.py:24
  126.8 11.0 %copy-start.6 = (bf16[512,3584]{1,0:T(8,128)(2,1)S(1)}, bf16[512,3584]{1,0:T(8,128)(2,1)}, u32[]{:S(2)}) copy-start(bf16[512,3584]{1,0:T(8,128)(2,1)} %get-tuple-element.43) | copy-start | bytes 11010052
  126.8 11.0 %copy-start.8 = (bf16[4,2,4,2,16,512]{5,4,0,2,3,1:T(8,128)(2,1)S(1)}, bf16[4,2,4,2,16,512]{5,4,0,2,3,1:T(8,128)(2,1)}, u32[]{:S(2)}) copy-start(bf16[4,2,4,2,16,512]{5,4,0,2,3,1:T(8,128)(2,1)} %copy.37) | copy-start | bytes 3145732
  126.8 19.4 %slice-start = ((s8[7340032]{0:T(1024)(128)(4,1)}), s8[4194304]{0:T(1024)(128)(4,1)S(1)}, s32[]{:S(2)}) async-start(s8[7340032]{0:T(1024)(128)(4,1)} %bitcast.122), calls=%async_computation.6 | async-start | bytes 8388608
  134.9 11.3 %slice-start.1 = ((s8[7340032]{0:T(1024)(128)(4,1)}), s8[3145728]{0:T(1024)(128)(4,1)S(1)}, s32[]{:S(2)}) async-start(s8[7340032]{0:T(1024)(128)(4,1)} %bitcast.122), calls=%async_computation.7 | async-start | bytes 6291456
  134.9 73.8 %collective-permute-start.16 = (bf16[384,3584]{1,0:T(8,128)(2,1)}, bf16[384,3584]{1,0:T(8,128)(2,1)}, u32[]{:S(2)}, u32[]{:S(2)}) collective-permute-start(bf16[384,3584]{1,0:T(8,128)(2,1)} %convolution_convert_fusion.3), channel_id=1, source_target_pairs={{0,64},{64,0},{1,65},{65,1},{2,66},{66,2},{3,67},{67,3},{4,68},{68... | collective-permute-start | bytes 8257544 | tf_op jit(solution)/shard_map/ppermute | solution.py:187
  142.1 6.3 %slice-start.2 = ((s8[7340032]{0:T(1024)(128)(4,1)}), s8[4194304]{0:T(1024)(128)(4,1)S(1)}, s32[]{:S(2)}) async-start(s8[7340032]{0:T(1024)(128)(4,1)} %bitcast.145), calls=%async_computation.8 | async-start | bytes 8388608
  142.3 43.3 %collective-permute-start.10 = (bf16[2,4,16,3584]{3,2,1,0:T(8,128)(2,1)S(1)}, bf16[2,4,16,3584]{3,2,1,0:T(8,128)(2,1)S(1)}, u32[]{:S(2)}, u32[]{:S(2)}) collective-permute-start(bf16[2,4,16,3584]{3,2,1,0:T(8,128)(2,1)S(1)} %bitcast.141), channel_id=1, source_target_pairs={{0,2},{1,3},{2,4},{3,5},{4,6},{5,7},{6,0},{7,1},{8,10},{9,11},{10,... | collective-permute-start | bytes 2752520 | tf_op jit(solution)/shard_map/ppermute | solution.py:24
  143.4 42.1 %collective-permute-start.11 = (bf16[2,4,16,3584]{3,2,1,0:T(8,128)(2,1)S(1)}, bf16[2,4,16,3584]{3,2,1,0:T(8,128)(2,1)S(1)}, u32[]{:S(2)}, u32[]{:S(2)}) collective-permute-start(bf16[2,4,16,3584]{3,2,1,0:T(8,128)(2,1)S(1)} %bitcast.140), channel_id=1, source_target_pairs={{0,6},{1,7},{2,0},{3,1},{4,2},{5,3},{6,4},{7,5},{8,14},{9,15},{10,... | collective-permute-start | bytes 2752520 | tf_op jit(solution)/shard_map/ppermute | solution.py:24
  145.6 40.0 %collective-permute-start.12 = (bf16[2,4,16,3584]{3,2,1,0:T(8,128)(2,1)S(1)}, bf16[2,4,16,3584]{3,2,1,0:T(8,128)(2,1)S(1)}, u32[]{:S(2)}, u32[]{:S(2)}) collective-permute-start(bf16[2,4,16,3584]{3,2,1,0:T(8,128)(2,1)S(1)} %bitcast.139), channel_id=1, source_target_pairs={{0,4},{1,5},{2,6},{3,7},{4,0},{5,1},{6,2},{7,3},{8,12},{9,13},{10,... | collective-permute-start | bytes 2752520 | tf_op jit(solution)/shard_map/ppermute | solution.py:24
  146.2 2.1 slice-start.3
  153.8 37.3 %copy-start.11 = (bf16[7168]{0:T(1024)(128)(2,1)S(1)}, bf16[7168]{0:T(1024)(128)(2,1)}, u32[]{:S(2)}) copy-start(bf16[7168]{0:T(1024)(128)(2,1)} %param.5) | copy-start | bytes 43012
  186.9 9.9 %collective-permute-start.13 = (bf16[2,16,3584]{2,1,0:T(8,128)(2,1)}, bf16[2,16,3584]{2,1,0:T(8,128)(2,1)}, u32[]{:S(2)}, u32[]{:S(2)}) collective-permute-start(bf16[2,16,3584]{2,1,0:T(8,128)(2,1)} %get-tuple-element.61), channel_id=1, source_target_pairs={{0,16},{1,17},{2,18},{3,19},{4,20},{5,21},{6,22},{7,23},{8,24},{9,... | collective-permute-start | bytes 688136 | tf_op jit(solution)/shard_map/ppermute | solution.py:24
  188.0 11.5 %collective-permute-start.14 = (bf16[2,16,3584]{2,1,0:T(8,128)(2,1)}, bf16[2,16,3584]{2,1,0:T(8,128)(2,1)}, u32[]{:S(2)}, u32[]{:S(2)}) collective-permute-start(bf16[2,16,3584]{2,1,0:T(8,128)(2,1)} %get-tuple-element.62), channel_id=1, source_target_pairs={{0,48},{1,49},{2,50},{3,51},{4,52},{5,53},{6,54},{7,55},{8,56},{9,... | collective-permute-start | bytes 688136 | tf_op jit(solution)/shard_map/ppermute | solution.py:24
  190.2 10.0 %collective-permute-start.15 = (bf16[2,16,3584]{2,1,0:T(8,128)(2,1)S(1)}, bf16[2,16,3584]{2,1,0:T(8,128)(2,1)}, u32[]{:S(2)}, u32[]{:S(2)}) collective-permute-start(bf16[2,16,3584]{2,1,0:T(8,128)(2,1)S(1)} %get-tuple-element.63), channel_id=1, source_target_pairs={{0,32},{1,33},{2,34},{3,35},{4,36},{5,37},{6,38},{7,39},{8,40},{9,... | collective-permute-start | bytes 688136 | tf_op jit(solution)/shard_map/ppermute | solution.py:24
  191.4 17.2 %all-to-all-start.2 = ((bf16[8,16,3584]{2,1,0:T(8,128)(2,1)}), bf16[8,16,3584]{2,1,0:T(8,128)(2,1)S(1)}, u32[]{:S(2)}, u32[]{:S(2)}) async-start(bf16[8,16,3584]{2,1,0:T(8,128)(2,1)} %bitcast.138), calls=%async_computation.3 | async-start | bytes 1835008 | tf_op jit(solution)/shard_map/all_to_all | solution.py:214
  208.8 5.3 %collective-permute-start.17 = (bf16[16,3584]{1,0:T(8,128)(2,1)S(1)}, bf16[16,3584]{1,0:T(8,128)(2,1)S(1)}, u32[]{:S(2)}, u32[]{:S(2)}) collective-permute-start(bf16[16,3584]{1,0:T(8,128)(2,1)S(1)} %get-tuple-element.87), channel_id=1, source_target_pairs={{0,1},{1,0},{2,3},{3,2},{4,5},{5,4},{6,7},{7,6},{8,9},{9,8},{10,11... | collective-permute-start | bytes 344072 | tf_op jit(solution)/shard_map/ppermute | solution.py:24
  211.1 7.9 %copy-start.10 = (bf16[128,3584]{1,0:T(8,128)(2,1)S(1)}, bf16[128,3584]{1,0:T(8,128)(2,1)}, u32[]{:S(2)}) copy-start(bf16[128,3584]{1,0:T(8,128)(2,1)} %convolution_convert_fusion.4) | copy-start | bytes 2752516
  215.0 12.9 %collective-permute-start.18 = (bf16[16,7168]{1,0:T(8,128)(2,1)S(1)}, bf16[16,7168]{1,0:T(8,128)(2,1)S(1)}, u32[]{:S(2)}, u32[]{:S(2)}) collective-permute-start(bf16[16,7168]{1,0:T(8,128)(2,1)S(1)} %backward.1), channel_id=1, source_target_pairs={{0,16},{1,17},{2,18},{3,19},{4,20},{5,21},{6,22},{7,23},{8,24},{9,... | collective-permute-start | bytes 688136 | tf_op jit(solution)/shard_map/ppermute | solution.py:24
  215.7 12.3 %collective-permute-start.19 = (bf16[16,7168]{1,0:T(8,128)(2,1)S(1)}, bf16[16,7168]{1,0:T(8,128)(2,1)S(1)}, u32[]{:S(2)}, u32[]{:S(2)}) collective-permute-start(bf16[16,7168]{1,0:T(8,128)(2,1)S(1)} %backward.1), channel_id=1, source_target_pairs={{0,48},{1,49},{2,50},{3,51},{4,52},{5,53},{6,54},{7,55},{8,56},{9,... | collective-permute-start | bytes 688136 | tf_op jit(solution)/shard_map/ppermute | solution.py:24
  218.3 9.7 %collective-permute-start.20 = (bf16[16,7168]{1,0:T(8,128)(2,1)S(1)}, bf16[16,7168]{1,0:T(8,128)(2,1)S(1)}, u32[]{:S(2)}, u32[]{:S(2)}) collective-permute-start(bf16[16,7168]{1,0:T(8,128)(2,1)S(1)} %backward.1), channel_id=1, source_target_pairs={{0,32},{1,33},{2,34},{3,35},{4,36},{5,37},{6,38},{7,39},{8,40},{9,... | collective-permute-start | bytes 688136 | tf_op jit(solution)/shard_map/ppermute | solution.py:24
  219.0 22.4 %collective-permute-start.22 = (bf16[128,3584]{1,0:T(8,128)(2,1)S(1)}, bf16[128,3584]{1,0:T(8,128)(2,1)S(1)}, u32[]{:S(2)}, u32[]{:S(2)}) collective-permute-start(bf16[128,3584]{1,0:T(8,128)(2,1)S(1)} %copy-done.10), channel_id=1, source_target_pairs={{0,64},{64,0},{1,65},{65,1},{2,66},{66,2},{3,67},{67,3},{4,68},{68... | collective-permute-start | bytes 2752520 | tf_op jit(solution)/shard_map/ppermute | solution.py:220
  228.1 15.5 %collective-permute-start.21 = (bf16[4,16,7168]{2,1,0:T(8,128)(2,1)S(1)}, bf16[4,16,7168]{2,1,0:T(8,128)(2,1)S(1)}, u32[]{:S(2)}, u32[]{:S(2)}) collective-permute-start(bf16[4,16,7168]{2,1,0:T(8,128)(2,1)S(1)} %bitcast_dynamic-update-slice_fusion.14), channel_id=1, source_target_pairs={{0,8},{1,9},{2,10},{3,11},{4,12},{5,13},{6,14},{7,15},{8,0},{9,1},... | collective-permute-start | bytes 2752520 | tf_op jit(solution)/shard_map/ppermute | solution.py:24
  243.7 1.2 copy-start.9
Sparse Core Ops, SparseCore 0:
  38.4 46.2 all-gather.1
  120.7 45.8 reduce-scatter.1

commit v4 on v3

--- a/solution.py
+++ b/solution.py
@@ -176,15 +176,18 @@
     sums1, grad_a, grad_b = lax.optimization_barrier((sums1, grad_a, grad_b))
     over_vocab = lax.psum_scatter(sums1, "vocab", scatter_dimension=0, tiled=True)
     sent = dot(take(grad_b, 1 - c), table2, ((1,), (0,)), bf16)
-    sent, grad_b = lax.optimization_barrier((sent, grad_b))
+    start, early = half // 14, half * 6 // 7
+    first_grad = dot(grad_b.reshape(-1, vocab_rows), rows2[:, :start], ((0,), (0,)), bf16)
+    sent, first_grad, grad_b = lax.optimization_barrier((sent, first_grad, grad_b))
+    swap = [(0, 1), (1, 0)]
+    first_grad = lax.ppermute(first_grad, "pipe", swap)
     sent = hop(sent, dc=1)
 
-    swap = [(0, 1), (1, 0)]
-    early = vocab_rows * 3 // 4
     all_b = grad_b.reshape(-1, vocab_rows)
-    sent_grad = dot(all_b[:, :early], rows2, ((0,), (0,)), bf16)
+    sent_grad = dot(all_b, rows2[:, start:early], ((0,), (0,)), bf16)
     sent_grad, grad_b = lax.optimization_barrier((sent_grad, grad_b))
     received = lax.ppermute(sent_grad, "pipe", swap)
+    first_grad, grad_b = lax.optimization_barrier((first_grad, grad_b))
 
     sums2 = (dot(take(grad_b, c), table2, ((1,), (0,))) + sent.astype(f32)).astype(bf16)
     sums2 = sums2.reshape(NY, NZ, side, half)
@@ -193,7 +196,7 @@
         for dz in range(NZ)
     ]
     *z_blocks, grad_a, grad_b = lax.optimization_barrier((*z_blocks, grad_a, grad_b))
-    late_grad = dot(grad_b.reshape(-1, vocab_rows)[:, early:], rows2, ((0,), (0,)), bf16)
+    late_grad = dot(grad_b.reshape(-1, vocab_rows), rows2[:, early:], ((0,), (0,)), bf16)
     own_grad = dot(grad_a, rows1, ((0,), (0,)), bf16)
 
     total2 = z_blocks[0].astype(f32)
@@ -225,14 +228,16 @@
         along_x = put(along_x, hop(result, dx=dx), (x - dx) % NX)
     hidden_grad = put(jnp.zeros((NC, NX, part, width), bf16), along_x, c)
     hidden_grad = put(hidden_grad, hop(along_x, dc=1), 1 - c)
-    own_wide = own_grad.astype(f32)
     table_grad = lax.dynamic_update_slice(
         jnp.zeros((vocab_rows, half), bf16),
-        (own_wide[:early] + received.astype(f32)).astype(bf16),
-        (0, 0),
+        (own_grad[:, start:early].astype(f32) + received.astype(f32)).astype(bf16),
+        (0, start),
     )
     table_grad = lax.dynamic_update_slice(
-        table_grad, (own_wide[early:] + late.astype(f32)).astype(bf16), (early, 0)
+        table_grad, (own_grad[:, :start].astype(f32) + first_grad.astype(f32)).astype(bf16), (0, 0)
+    )
+    table_grad = lax.dynamic_update_slice(
+        table_grad, (own_grad[:, early:].astype(f32) + late.astype(f32)).astype(bf16), (0, early)
     )
     return (hidden_grad.reshape(tok_rows, width), table_grad, token_loss)
 

time: 252 us -> 248 us (0.984)
  waiting for transfers between devices: 90.4 us -> 82.9 us
  matrix products: 43.6 us -> 47 us
    ppermute x1, waiting for transfers between devices: 12.9 us -> 3.48 us  [on_device(): late = lax.ppermute(late, 'pipe', swap)]
    dot_general x8 -> x9, matrix products: 43.6 us -> 47 us  [dot(): lax.dot_general(a, b, (contract, ((), ())), preferred_element_type=jnp.fl...]
    all_to_all x1, waiting for transfers between devices: 7.18 us -> 10.3 us  [on_device(): lax.all_to_all(over_vocab.reshape(-1, part, half), 'dp', 0, 0, tiled=True)]
    ppermute x0 -> x1, starting transfers between devices: none -> 2.72 us  [on_device(): first_grad = lax.ppermute(first_grad, 'pipe', swap)]
    convert_element_type x3 -> x1, other arithmetic: 5.86 us -> 3.35 us  [on_device(): (own_grad[:, start:early].astype(f32) + received.astype(f32)).astype(bf16)]
  transfers between devices with their start and end apart: 27 -> 28, of which waited for: 14 -> 13; matrix products, arithmetic and copies ran while one was open for 26% -> 27% of each run, Pallas kernels for 0% -> 0%
where the time goes in v4:
time: 248 us; the launch traced here: 247 us
  waiting for transfers between devices  82.9 us (33%)
  matrix products  47 us (19%)
  starting transfers between devices  36.5 us (15%)
  local copies, waits for them, and re-layouts  31.6 us (13%)
  blocking collectives  17.7 us (7%)
  other arithmetic  15.3 us (6%)
  between operations  14.8 us (6%)
    ppermute x21, waiting for transfers between devices, hop(): return lax.ppermute(array, ('vocab', 'dp'), pairs)  62 us
    dot_general x9, matrix products, dot(): lax.dot_general(a, b, (contract, ((), ())), preferred_element_type=jnp.fl...  47 us
    ppermute x21, starting transfers between devices, hop(): return lax.ppermute(array, ('vocab', 'dp'), pairs)  19.8 us
    all_to_all x1, blocking collectives, on_device(): stats = lax.all_to_all(stats, ('vocab', 'dp'), 0, 0, tiled=True)  17.7 us
    all_to_all x1, waiting for transfers between devices, on_device(): lax.all_to_all(over_vocab.reshape(-1, part, half), 'dp', 0, 0, tiled=True)  10.3 us
    dynamic_update_slice x18, local copies, waits for them, and re-layouts, put(): return lax.dynamic_update_slice(buffer, block, start)  9.99 us
    dynamic_slice x1, local copies, waits for them, and re-layouts, on_device(): table2 = lax.dynamic_slice(table, (0, other_col), (vocab_rows, half))  6.64 us
    all_to_all x1, starting transfers between devices, on_device(): near = lax.all_to_all(seed, 'dp', 0, 0, tiled=True)  6.41 us
  transfers between devices with their start and end apart: 28, of which 13 were waited for; matrix products, arithmetic and copies ran while one was open for 27% of the time, Pallas kernels for 0%

profile of v4, /device:TPU:0, one launch (start us, length us, event | category | flops | bytes accessed | tf_op | source)
XLA Modules:
  0.0 246.5 jit_solution(17096804380177665213)
XLA Ops:
  7.2 1.1 dynamic-slice_convert_fusion.1
  8.3 1.1 multiply_reduce_fusion.1
  12.1 6.4 %all-to-all-start = ((bf16[8,16,3712]{2,1,0:T(8,128)(2,1)}), bf16[8,16,3712]{2,1,0:T(8,128)(2,1)S(1)}, u32[]{:S(2)}, u32[]{:S(2)}) async-start(bf16[8,16,3712]{2,1,0:T(8,128)(2,1)} %broadcast_in_dim.14), calls=%async_computation | async-start | bytes 1900544 | tf_op jit(solution)/shard_map/all_to_all | solution.py:112
  18.6 1.4 dynamic-slice_convert_fusion
  20.3 6.6 %constant_dynamic-slice_fusion.5 = (bf16[512,3584]{1,0:T(8,128)(2,1)}, bf16[512,3584]{1,0:T(8,128)(2,1)}) fusion(bf16[512,7168]{1,0:T(8,128)(2,1)} %param.7, s32[]{:T(128)S(6)} %select_n.189, s32[]{:T(128)S(6)} %select_n.191), kind=kLoop, calls=%fused_computation.81 | loop fusion | bytes 14680072 | tf_op jit(solution)/shard_map/dynamic_slice | solution.py:138
  27.0 1.3 fusion.15
  28.3 4.9 %all-to-all-done = bf16[8,16,3712]{2,1,0:T(8,128)(2,1)S(1)} async-done(((bf16[8,16,3712]{2,1,0:T(8,128)(2,1)}), bf16[8,16,3712]{2,1,0:T(8,128)(2,1)S(1)}, u32[]{:S(2)}, u32[]{:S(2)}) %all-to-all-start) | async-done | bytes 950304 | tf_op jit(solution)/shard_map/all_to_all | solution.py:112
  33.2 2.3 collective-permute-start.2
  35.5 1.2 collective-permute-start.5
  38.3 1.4 broadcast.85.clone
  40.7 14.4 %collective-permute-done = bf16[64,3584]{1,0:T(8,128)(2,1)} collective-permute-done((bf16[64,3584]{1,0:T(8,128)(2,1)S(1)}, bf16[64,3584]{1,0:T(8,128)(2,1)}, u32[]{:S(2)}, u32[]{:S(2)}) %collective-permute-start) | collective-permute-done | bytes 458784 | tf_op jit(solution)/shard_map/ppermute | solution.py:24
  55.7 1.4 collective-permute-start.6
  57.1 2.0 collective-permute-start.7
  60.3 1.8 bitcast_dynamic-update-slice_fusion.12
  62.1 1.8 bitcast_dynamic-update-slice_fusion.11
  63.9 3.3 %collective-permute-done.3 = bf16[64,3584]{1,0:T(8,128)(2,1)S(1)} collective-permute-done((bf16[64,3584]{1,0:T(8,128)(2,1)}, bf16[64,3584]{1,0:T(8,128)(2,1)S(1)}, u32[]{:S(2)}, u32[]{:S(2)}) %collective-permute-start.3) | collective-permute-done | bytes 458784 | tf_op jit(solution)/shard_map/ppermute | solution.py:24
  67.2 1.8 bitcast_dynamic-update-slice_fusion.10
  69.1 3.0 %collective-permute-done.6 = bf16[64,3584]{1,0:T(8,128)(2,1)S(1)} collective-permute-done((bf16[64,3584]{1,0:T(8,128)(2,1)}, bf16[64,3584]{1,0:T(8,128)(2,1)S(1)}, u32[]{:S(2)}, u32[]{:S(2)}) %collective-permute-start.6) | collective-permute-done | bytes 458784 | tf_op jit(solution)/shard_map/ppermute | solution.py:24
  73.0 1.7 bitcast_dynamic-update-slice_fusion.3
  77.0 4.0 %fusion.10 = f32[4,2,4,2,16,512]{5,4,0,2,3,1:T(8,128)S(1)} fusion(bf16[2,2,4,4,16,3584]{5,4,3,2,1,0:T(8,128)(2,1)S(1)} %bitcast.123, bf16[512,3584]{1,0:T(8,128)(2,1)S(1)} %copy-done.6), kind=kOutput, calls=%fused_computation.23 | convolution fusion | flops 3758096384 | bytes 13107200 | tf_op jit(solution)/shard_map/dot_general | solution.py:40
  81.0 1.5 copy.35
  82.4 2.3 all-gather.2.cloned.1.call-done
  84.7 7.5 %fusion.38 = f32[1024,512]{1,0:T(8,128)S(1)} fusion(bf16[1024,3584]{1,0:T(8,128)(2,1)} %all-gather.2.cloned.1.call-done, bf16[512,3584]{1,0:T(8,128)(2,1)} %get-tuple-element.42), kind=kOutput, calls=%fused_computation.108 | convolution fusion | flops 3758096384 | bytes 13107200 | tf_op jit(solution)/shard_map/dot_general | solution.py:40
  92.5 1.3 copy-done.1
  95.0 17.7 %all_to_all.22 = f32[64,1,1152]{2,1,0:T(1,128)S(1)} all-to-all(f32[64,1,1152]{2,1,0:T(1,128)S(1)} %all_to_all.15), channel_id=1, replica_groups=mesh['pipe'=2,'vocab'=8,'dp'=8] {'vocab','dp'}, dimensions={0} | all-to-all | bytes 589824 | tf_op jit(solution)/shard_map/all_to_all | solution.py:161
  113.4 6.0 %convolution_convert_fusion = bf16[1024,3584]{1,0:T(8,128)(2,1)} fusion(bf16[1024,512]{1,0:T(8,128)(2,1)S(1)} %fusion.9, bf16[512,3584]{1,0:T(8,128)(2,1)S(1)} %copy-done.8), kind=kOutput, calls=%fused_computation | convolution fusion | flops 3761766400 | bytes 12058624 | tf_op jit(solution)/shard_map/dot_general | solution.py:40
  120.5 2.5 %convolution_convert_fusion.4 = bf16[512,256]{1,0:T(8,128)(2,1)} fusion(bf16[1024,512]{1,0:T(8,128)(2,1)} %bitcast.135, bf16[1024,3584]{1,0:T(8,128)(2,1)} %bitcast.124), kind=kOutput, calls=%fused_computation.25 | convolution fusion | flops 268566528 | bytes 1835008 | tf_op jit(solution)/shard_map/dot_general | solution.py:40
  123.0 6.1 %convolution_convert_fusion.2 = bf16[512,3584]{1,0:T(8,128)(2,1)} fusion(bf16[512,3584]{1,0:T(8,128)(2,1)} %get-tuple-element.46, bf16[2,512,512]{2,1,0:T(8,128)(2,1)} %bitcast.136, s32[]{:T(128)S(6)} %select_n.205), kind=kOutput, calls=%fused_computation.3 | convolution fusion | flops 1880883200 | bytes 7864324 | tf_op jit(solution)/shard_map/dot_general | solution.py:40
  129.3 2.7 %collective-permute-start.9 = (bf16[512,256]{1,0:T(8,128)(2,1)}, bf16[512,256]{1,0:T(8,128)(2,1)S(1)}, u32[]{:S(2)}, u32[]{:S(2)}) collective-permute-start(bf16[512,256]{1,0:T(8,128)(2,1)} %convolution_convert_fusion.4), channel_id=1, source_target_pairs={{0,64},{64,0},{1,65},{65,1},{2,66},{66,2},{3,67},{67,3},{4,68},{68... | collective-permute-start | bytes 786440 | tf_op jit(solution)/shard_map/ppermute | solution.py:183
  132.0 8.0 %fusion.2 = bf16[512,2816]{1,0:T(8,128)(2,1)} fusion(bf16[1024,512]{1,0:T(8,128)(2,1)} %bitcast.137, bf16[1024,3584]{1,0:T(8,128)(2,1)} %bitcast.125), kind=kOutput, calls=%fused_computation.7 | convolution fusion | flops 2954231808 | bytes 9699328 | tf_op jit(solution)/shard_map/dot_general | solution.py:40
  140.8 4.5 %add_convert_fusion = bf16[512,3584]{1,0:T(8,128)(2,1)S(1)} fusion(bf16[512,3584]{1,0:T(8,128)(2,1)} %collective-permute-done.10, bf16[512,3584]{1,0:T(8,128)(2,1)S(1)} %copy-done.7, bf16[2,512,512]{2,1,0:T(8,128)(2,1)S(1)} %bitcast.138, s32[]{:T(128)S(6)} %select_n.202), kind=kOutput, calls=%fused_computation.1 | convolution fusion | flops 1884553216 | bytes 11534340 | tf_op jit(solution)/shard_map/dot_general | solution.py:40
  146.2 2.6 %collective-permute-start.12 = (bf16[2,4,16,3584]{3,2,1,0:T(8,128)(2,1)S(1)}, bf16[2,4,16,3584]{3,2,1,0:T(8,128)(2,1)S(1)}, u32[]{:S(2)}, u32[]{:S(2)}) collective-permute-start(bf16[2,4,16,3584]{3,2,1,0:T(8,128)(2,1)S(1)} %bitcast.142), channel_id=1, source_target_pairs={{0,6},{1,7},{2,0},{3,1},{4,2},{5,3},{6,4},{7,5},{8,14},{9,15},{10,... | collective-permute-start | bytes 2752520 | tf_op jit(solution)/shard_map/ppermute | solution.py:24
  148.9 2.8 %convolution_convert_fusion.3 = bf16[512,512]{1,0:T(8,128)(2,1)} fusion(bf16[1024,512]{1,0:T(8,128)(2,1)S(1)} %bitcast.139, bf16[1024,3584]{1,0:T(8,128)(2,1)} %bitcast.126), kind=kOutput, calls=%fused_computation.24 | convolution fusion | flops 537133056 | bytes 2621440 | tf_op jit(solution)/shard_map/dot_general | solution.py:40
  151.7 5.5 %convolution_convert_fusion.1 = bf16[512,3584]{1,0:T(8,128)(2,1)} fusion(bf16[1024,512]{1,0:T(8,128)(2,1)S(1)} %fusion.9, bf16[1024,3584]{1,0:T(8,128)(2,1)S(1)} %bitcast.148), kind=kOutput, calls=%fused_computation.2 | convolution fusion | flops 3759931392 | bytes 12058624 | tf_op jit(solution)/shard_map/dot_general | solution.py:40
  157.3 31.5 %collective-permute-done.11 = bf16[2,4,16,3584]{3,2,1,0:T(8,128)(2,1)S(1)} collective-permute-done((bf16[2,4,16,3584]{3,2,1,0:T(8,128)(2,1)S(1)}, bf16[2,4,16,3584]{3,2,1,0:T(8,128)(2,1)S(1)}, u32[]{:S(2)}, u32[]{:S(2)}) %collective-permute-start.11) | collective-permute-done | bytes 917536 | tf_op jit(solution)/shard_map/ppermute | solution.py:24
  190.7 2.6 %collective-permute-start.15 = (bf16[2,16,3584]{2,1,0:T(8,128)(2,1)}, bf16[2,16,3584]{2,1,0:T(8,128)(2,1)}, u32[]{:S(2)}, u32[]{:S(2)}) collective-permute-start(bf16[2,16,3584]{2,1,0:T(8,128)(2,1)} %get-tuple-element.67), channel_id=1, source_target_pairs={{0,48},{1,49},{2,50},{3,51},{4,52},{5,53},{6,54},{7,55},{8,56},{9,... | collective-permute-start | bytes 688136 | tf_op jit(solution)/shard_map/ppermute | solution.py:24
  193.9 4.2 %all-to-all-start.2 = ((bf16[8,16,3584]{2,1,0:T(8,128)(2,1)}), bf16[8,16,3584]{2,1,0:T(8,128)(2,1)S(1)}, u32[]{:S(2)}, u32[]{:S(2)}) async-start(bf16[8,16,3584]{2,1,0:T(8,128)(2,1)} %bitcast.140), calls=%async_computation.3 | async-start | bytes 1835008 | tf_op jit(solution)/shard_map/all_to_all | solution.py:217
  198.1 4.4 %collective-permute-done.14 = bf16[2,16,3584]{2,1,0:T(8,128)(2,1)} collective-permute-done((bf16[2,16,3584]{2,1,0:T(8,128)(2,1)}, bf16[2,16,3584]{2,1,0:T(8,128)(2,1)}, u32[]{:S(2)}, u32[]{:S(2)}) %collective-permute-start.14) | collective-permute-done | bytes 229408 | tf_op jit(solution)/shard_map/ppermute | solution.py:24
  202.6 1.3 add_convert_fusion.5
  203.8 10.3 %all-to-all-done.2 = bf16[8,16,3584]{2,1,0:T(8,128)(2,1)S(1)} async-done(((bf16[8,16,3584]{2,1,0:T(8,128)(2,1)}), bf16[8,16,3584]{2,1,0:T(8,128)(2,1)S(1)}, u32[]{:S(2)}, u32[]{:S(2)}) %all-to-all-start.2) | async-done | bytes 917536 | tf_op jit(solution)/shard_map/all_to_all | solution.py:217
  214.3 1.3 collective-permute-start.18
  216.2 2.9 %collective-permute-done.18.far = bf16[16,3584]{1,0:T(8,128)(2,1)S(1)} collective-permute-done((bf16[16,3584]{1,0:T(8,128)(2,1)S(1)}, bf16[16,3584]{1,0:T(8,128)(2,1)S(1)}, u32[]{:S(2)}, u32[]{:S(2)}) %collective-permute-start.18) | collective-permute-done | bytes 114720 | tf_op jit(solution)/shard_map/ppermute | solution.py:24
  220.8 2.5 %collective-permute-start.20 = (bf16[16,7168]{1,0:T(8,128)(2,1)S(1)}, bf16[16,7168]{1,0:T(8,128)(2,1)S(1)}, u32[]{:S(2)}, u32[]{:S(2)}) collective-permute-start(bf16[16,7168]{1,0:T(8,128)(2,1)S(1)} %backward.1), channel_id=1, source_target_pairs={{0,48},{1,49},{2,50},{3,51},{4,52},{5,53},{6,54},{7,55},{8,56},{9,... | collective-permute-start | bytes 688136 | tf_op jit(solution)/shard_map/ppermute | solution.py:24
  223.9 2.5 %collective-permute-start.23 = (bf16[512,512]{1,0:T(8,128)(2,1)}, bf16[512,512]{1,0:T(8,128)(2,1)S(1)}, u32[]{:S(2)}, u32[]{:S(2)}) collective-permute-start(bf16[512,512]{1,0:T(8,128)(2,1)} %convolution_convert_fusion.3), channel_id=1, source_target_pairs={{0,64},{64,0},{1,65},{65,1},{2,66},{66,2},{3,67},{67,3},{4,68},{68... | collective-permute-start | bytes 1572872 | tf_op jit(solution)/shard_map/ppermute | solution.py:223
  226.4 3.3 %add_convert_fusion.1 = bf16[512,2816]{1,0:T(8,128)(2,1)S(1)} fusion(bf16[512,2816]{1,0:T(8,128)(2,1)} %collective-permute-done.17, bf16[512,3584]{1,0:T(8,128)(2,1)} %convolution_convert_fusion.1), kind=kLoop, calls=%fused_computation.6 | loop fusion | flops 5767168 | bytes 8650752 | tf_op jit(solution)/shard_map/convert_element_type | solution.py:233
  232.6 3.5 %collective-permute-done.23 = bf16[512,512]{1,0:T(8,128)(2,1)S(1)} collective-permute-done((bf16[512,512]{1,0:T(8,128)(2,1)}, bf16[512,512]{1,0:T(8,128)(2,1)S(1)}, u32[]{:S(2)}, u32[]{:S(2)}) %collective-permute-start.23) | collective-permute-done | bytes 524320 | tf_op jit(solution)/shard_map/ppermute | solution.py:223
  236.1 1.2 fusion.16
  237.4 1.7 copy-done.5
  (130 shorter events, 24.5 us)
Async XLA Ops:
  7.2 11.4 %copy-start = (bf16[128,7168]{1,0:T(8,128)(2,1)S(1)}, bf16[128,7168]{1,0:T(8,128)(2,1)}, u32[]{:S(2)}) copy-start(bf16[128,7168]{1,0:T(8,128)(2,1)} %hidden.1) | copy-start | bytes 5505028
  12.1 21.1 %all-to-all-start = ((bf16[8,16,3712]{2,1,0:T(8,128)(2,1)}), bf16[8,16,3712]{2,1,0:T(8,128)(2,1)S(1)}, u32[]{:S(2)}, u32[]{:S(2)}) async-start(bf16[8,16,3712]{2,1,0:T(8,128)(2,1)} %broadcast_in_dim.14), calls=%async_computation | async-start | bytes 1900544 | tf_op jit(solution)/shard_map/all_to_all | solution.py:112
  18.5 66.2 %all-gather.2.cloned.1.call-start = ((), (), s32[]{:S(2)}) async-start(), calls=%async_computation.4 | async-start | bytes 8257536 | tf_op jit(solution)/shard_map/all_gather | solution.py:116
  33.2 21.9 %collective-permute-start = (bf16[64,3584]{1,0:T(8,128)(2,1)S(1)}, bf16[64,3584]{1,0:T(8,128)(2,1)}, u32[]{:S(2)}, u32[]{:S(2)}) collective-permute-start(bf16[64,3584]{1,0:T(8,128)(2,1)S(1)} %fusion.15), channel_id=1, source_target_pairs={{0,2},{1,3},{2,4},{3,5},{4,6},{5,7},{6,0},{7,1},{8,10},{9,11},{10,... | collective-permute-start | bytes 1376264 | tf_op jit(solution)/shard_map/ppermute | solution.py:24
  33.2 30.8 %collective-permute-start.2 = (bf16[64,3584]{1,0:T(8,128)(2,1)S(1)}, bf16[64,3584]{1,0:T(8,128)(2,1)}, u32[]{:S(2)}, u32[]{:S(2)}) collective-permute-start(bf16[64,3584]{1,0:T(8,128)(2,1)S(1)} %fusion.15), channel_id=1, source_target_pairs={{0,4},{1,5},{2,6},{3,7},{4,0},{5,1},{6,2},{7,3},{8,12},{9,13},{10,... | collective-permute-start | bytes 1376264 | tf_op jit(solution)/shard_map/ppermute | solution.py:24
  35.5 21.6 %collective-permute-start.5 = (bf16[64,3584]{1,0:T(8,128)(2,1)S(1)}, bf16[64,3584]{1,0:T(8,128)(2,1)}, u32[]{:S(2)}, u32[]{:S(2)}) collective-permute-start(bf16[64,3584]{1,0:T(8,128)(2,1)S(1)} %fusion.15), channel_id=1, source_target_pairs={{0,1},{1,0},{2,3},{3,2},{4,5},{5,4},{6,7},{7,6},{8,9},{9,8},{10,11... | collective-permute-start | bytes 1376264 | tf_op jit(solution)/shard_map/ppermute | solution.py:24
  36.7 19.1 %collective-permute-start.1 = (bf16[64,3584]{1,0:T(8,128)(2,1)S(1)}, bf16[64,3584]{1,0:T(8,128)(2,1)}, u32[]{:S(2)}, u32[]{:S(2)}) collective-permute-start(bf16[64,3584]{1,0:T(8,128)(2,1)S(1)} %fusion.15), channel_id=1, source_target_pairs={{0,6},{1,7},{2,0},{3,1},{4,2},{5,3},{6,4},{7,5},{8,14},{9,15},{10,... | collective-permute-start | bytes 1376264 | tf_op jit(solution)/shard_map/ppermute | solution.py:24
  38.3 151.8 %reduce-scatter.2.cloned.1.call-start = ((), (), s32[]{:S(2)}) async-start(), calls=%async_computation.5 | async-start | bytes 8257536 | tf_op jit(solution)/shard_map/reduce_scatter | solution.py:177
  55.1 12.1 %collective-permute-start.3 = (bf16[64,3584]{1,0:T(8,128)(2,1)}, bf16[64,3584]{1,0:T(8,128)(2,1)S(1)}, u32[]{:S(2)}, u32[]{:S(2)}) collective-permute-start(bf16[64,3584]{1,0:T(8,128)(2,1)} %collective-permute-done), channel_id=1, source_target_pairs={{0,1},{1,0},{2,3},{3,2},{4,5},{5,4},{6,7},{7,6},{8,9},{9,8},{10,11... | collective-permute-start | bytes 1376264 | tf_op jit(solution)/shard_map/ppermute | solution.py:24
  55.7 16.4 %collective-permute-start.6 = (bf16[64,3584]{1,0:T(8,128)(2,1)}, bf16[64,3584]{1,0:T(8,128)(2,1)S(1)}, u32[]{:S(2)}, u32[]{:S(2)}) collective-permute-start(bf16[64,3584]{1,0:T(8,128)(2,1)} %collective-permute-done.1), channel_id=1, source_target_pairs={{0,1},{1,0},{2,3},{3,2},{4,5},{5,4},{6,7},{7,6},{8,9},{9,8},{10,11... | collective-permute-start | bytes 1376264 | tf_op jit(solution)/shard_map/ppermute | solution.py:24
  57.1 15.0 %collective-permute-start.7 = (bf16[64,3584]{1,0:T(8,128)(2,1)}, bf16[64,3584]{1,0:T(8,128)(2,1)S(1)}, u32[]{:S(2)}, u32[]{:S(2)}) collective-permute-start(bf16[64,3584]{1,0:T(8,128)(2,1)} %collective-permute-done.5), channel_id=1, source_target_pairs={{0,4},{1,5},{2,6},{3,7},{4,0},{5,1},{6,2},{7,3},{8,12},{9,13},{10,... | collective-permute-start | bytes 1376264 | tf_op jit(solution)/shard_map/ppermute | solution.py:24
  69.0 5.7 %collective-permute-start.4 = (bf16[4,64,3584]{2,1,0:T(8,128)(2,1)}, bf16[4,64,3584]{2,1,0:T(8,128)(2,1)S(1)}, u32[]{:S(2)}, u32[]{:S(2)}) collective-permute-start(bf16[4,64,3584]{2,1,0:T(8,128)(2,1)} %bitcast_dynamic-update-slice_fusion.10), channel_id=1, source_target_pairs={{0,8},{1,9},{2,10},{3,11},{4,12},{5,13},{6,14},{7,15},{8,0},{9,1},... | collective-permute-start | bytes 5505032 | tf_op jit(solution)/shard_map/ppermute | solution.py:24
  72.2 3.9 %collective-permute-start.8 = (bf16[4,64,3584]{2,1,0:T(8,128)(2,1)S(1)}, bf16[4,64,3584]{2,1,0:T(8,128)(2,1)S(1)}, u32[]{:S(2)}, u32[]{:S(2)}) collective-permute-start(bf16[4,64,3584]{2,1,0:T(8,128)(2,1)S(1)} %bitcast_dynamic-update-slice_fusion.6), channel_id=1, source_target_pairs={{0,8},{1,9},{2,10},{3,11},{4,12},{5,13},{6,14},{7,15},{8,0},{9,1},... | collective-permute-start | bytes 5505032 | tf_op jit(solution)/shard_map/ppermute | solution.py:24
  74.9 2.0 copy-start.6
  76.3 4.7 %copy-start.4 = (bf16[2,2,4,64,3584]{4,3,2,1,0:T(8,128)(2,1)}, bf16[2,2,4,64,3584]{4,3,2,1,0:T(8,128)(2,1)S(1)}, u32[]{:S(2)}) copy-start(bf16[2,2,4,64,3584]{4,3,2,1,0:T(8,128)(2,1)S(1)} %bitcast_dynamic-update-slice_fusion) | copy-start | bytes 22020100
  84.7 7.5 %copy-start.3 = (f32[4,2,4,2,16,512]{5,4,3,2,1,0:T(8,128)S(1)}, f32[4,2,4,2,16,512]{5,4,3,2,1,0:T(8,128)}, u32[]{:S(2)}) copy-start(f32[4,2,4,2,16,512]{5,4,3,2,1,0:T(8,128)} %copy.35) | copy-start | bytes 6291460
  92.5 1.3 copy-start.1
  94.7 18.1 %copy-start.2 = (f32[1024,512]{1,0:T(8,128)S(1)}, f32[1024,512]{1,0:T(8,128)}, u32[]{:S(2)}) copy-start(f32[1024,512]{1,0:T(8,128)} %copy-done.1) | copy-start | bytes 6291460
  94.8 18.6 %copy-start.8 = (bf16[512,3584]{1,0:T(8,128)(2,1)S(1)}, bf16[512,3584]{1,0:T(8,128)(2,1)}, u32[]{:S(2)}) copy-start(bf16[512,3584]{1,0:T(8,128)(2,1)} %get-tuple-element.42) | copy-start | bytes 11010052
  129.2 11.6 %collective-permute-start.10 = (bf16[512,3584]{1,0:T(8,128)(2,1)}, bf16[512,3584]{1,0:T(8,128)(2,1)}, u32[]{:S(2)}, u32[]{:S(2)}) collective-permute-start(bf16[512,3584]{1,0:T(8,128)(2,1)} %convolution_convert_fusion.2), channel_id=1, source_target_pairs={{0,8},{1,9},{2,10},{3,11},{4,12},{5,13},{6,14},{7,15},{8,0},{9,1},... | collective-permute-start | bytes 11010056 | tf_op jit(solution)/shard_map/ppermute | solution.py:24
  129.3 11.5 %collective-permute-start.9 = (bf16[512,256]{1,0:T(8,128)(2,1)}, bf16[512,256]{1,0:T(8,128)(2,1)S(1)}, u32[]{:S(2)}, u32[]{:S(2)}) collective-permute-start(bf16[512,256]{1,0:T(8,128)(2,1)} %convolution_convert_fusion.4), channel_id=1, source_target_pairs={{0,64},{64,0},{1,65},{65,1},{2,66},{66,2},{3,67},{67,3},{4,68},{68... | collective-permute-start | bytes 786440 | tf_op jit(solution)/shard_map/ppermute | solution.py:183
  132.0 8.7 %copy-start.7 = (bf16[512,3584]{1,0:T(8,128)(2,1)S(1)}, bf16[512,3584]{1,0:T(8,128)(2,1)}, u32[]{:S(2)}) copy-start(bf16[512,3584]{1,0:T(8,128)(2,1)} %get-tuple-element.46) | copy-start | bytes 11010052
  132.0 8.7 %copy-start.10 = (bf16[4,2,4,2,16,512]{5,4,0,2,3,1:T(8,128)(2,1)S(1)}, bf16[4,2,4,2,16,512]{5,4,0,2,3,1:T(8,128)(2,1)}, u32[]{:S(2)}) copy-start(bf16[4,2,4,2,16,512]{5,4,0,2,3,1:T(8,128)(2,1)} %copy.37) | copy-start | bytes 3145732
  132.0 19.7 %slice-start = ((s8[7340032]{0:T(1024)(128)(4,1)}), s8[4194304]{0:T(1024)(128)(4,1)S(1)}, s32[]{:S(2)}) async-start(s8[7340032]{0:T(1024)(128)(4,1)} %bitcast.147), calls=%async_computation.6 | async-start | bytes 8388608
  140.0 11.7 %slice-start.1 = ((s8[7340032]{0:T(1024)(128)(4,1)}), s8[3145728]{0:T(1024)(128)(4,1)S(1)}, s32[]{:S(2)}) async-start(s8[7340032]{0:T(1024)(128)(4,1)} %bitcast.147), calls=%async_computation.7 | async-start | bytes 6291456
  140.0 74.3 %collective-permute-start.17 = (bf16[512,2816]{1,0:T(8,128)(2,1)}, bf16[512,2816]{1,0:T(8,128)(2,1)}, u32[]{:S(2)}, u32[]{:S(2)}) collective-permute-start(bf16[512,2816]{1,0:T(8,128)(2,1)} %fusion.2), channel_id=1, source_target_pairs={{0,64},{64,0},{1,65},{65,1},{2,66},{66,2},{3,67},{67,3},{4,68},{68... | collective-permute-start | bytes 8650760 | tf_op jit(solution)/shard_map/ppermute | solution.py:189
  145.5 43.2 %collective-permute-start.11 = (bf16[2,4,16,3584]{3,2,1,0:T(8,128)(2,1)S(1)}, bf16[2,4,16,3584]{3,2,1,0:T(8,128)(2,1)S(1)}, u32[]{:S(2)}, u32[]{:S(2)}) collective-permute-start(bf16[2,4,16,3584]{3,2,1,0:T(8,128)(2,1)S(1)} %bitcast.143), channel_id=1, source_target_pairs={{0,2},{1,3},{2,4},{3,5},{4,6},{5,7},{6,0},{7,1},{8,10},{9,11},{10,... | collective-permute-start | bytes 2752520 | tf_op jit(solution)/shard_map/ppermute | solution.py:24
  146.2 42.5 %collective-permute-start.12 = (bf16[2,4,16,3584]{3,2,1,0:T(8,128)(2,1)S(1)}, bf16[2,4,16,3584]{3,2,1,0:T(8,128)(2,1)S(1)}, u32[]{:S(2)}, u32[]{:S(2)}) collective-permute-start(bf16[2,4,16,3584]{3,2,1,0:T(8,128)(2,1)S(1)} %bitcast.142), channel_id=1, source_target_pairs={{0,6},{1,7},{2,0},{3,1},{4,2},{5,3},{6,4},{7,5},{8,14},{9,15},{10,... | collective-permute-start | bytes 2752520 | tf_op jit(solution)/shard_map/ppermute | solution.py:24
  148.8 39.9 %collective-permute-start.13 = (bf16[2,4,16,3584]{3,2,1,0:T(8,128)(2,1)S(1)}, bf16[2,4,16,3584]{3,2,1,0:T(8,128)(2,1)S(1)}, u32[]{:S(2)}, u32[]{:S(2)}) collective-permute-start(bf16[2,4,16,3584]{3,2,1,0:T(8,128)(2,1)S(1)} %bitcast.141), channel_id=1, source_target_pairs={{0,4},{1,5},{2,6},{3,7},{4,0},{5,1},{6,2},{7,3},{8,12},{9,13},{10,... | collective-permute-start | bytes 2752520 | tf_op jit(solution)/shard_map/ppermute | solution.py:24
  157.3 36.3 %copy-start.11 = (bf16[7168]{0:T(1024)(128)(2,1)S(1)}, bf16[7168]{0:T(1024)(128)(2,1)}, u32[]{:S(2)}) copy-start(bf16[7168]{0:T(1024)(128)(2,1)} %param.5) | copy-start | bytes 43012
  190.1 12.5 %collective-permute-start.14 = (bf16[2,16,3584]{2,1,0:T(8,128)(2,1)}, bf16[2,16,3584]{2,1,0:T(8,128)(2,1)}, u32[]{:S(2)}, u32[]{:S(2)}) collective-permute-start(bf16[2,16,3584]{2,1,0:T(8,128)(2,1)} %get-tuple-element.66), channel_id=1, source_target_pairs={{0,16},{1,17},{2,18},{3,19},{4,20},{5,21},{6,22},{7,23},{8,24},{9,... | collective-permute-start | bytes 688136 | tf_op jit(solution)/shard_map/ppermute | solution.py:24
  190.7 11.9 %collective-permute-start.15 = (bf16[2,16,3584]{2,1,0:T(8,128)(2,1)}, bf16[2,16,3584]{2,1,0:T(8,128)(2,1)}, u32[]{:S(2)}, u32[]{:S(2)}) collective-permute-start(bf16[2,16,3584]{2,1,0:T(8,128)(2,1)} %get-tuple-element.67), channel_id=1, source_target_pairs={{0,48},{1,49},{2,50},{3,51},{4,52},{5,53},{6,54},{7,55},{8,56},{9,... | collective-permute-start | bytes 688136 | tf_op jit(solution)/shard_map/ppermute | solution.py:24
  193.3 9.2 %collective-permute-start.16 = (bf16[2,16,3584]{2,1,0:T(8,128)(2,1)}, bf16[2,16,3584]{2,1,0:T(8,128)(2,1)}, u32[]{:S(2)}, u32[]{:S(2)}) collective-permute-start(bf16[2,16,3584]{2,1,0:T(8,128)(2,1)} %get-tuple-element.68), channel_id=1, source_target_pairs={{0,32},{1,33},{2,34},{3,35},{4,36},{5,37},{6,38},{7,39},{8,40},{9,... | collective-permute-start | bytes 688136 | tf_op jit(solution)/shard_map/ppermute | solution.py:24
  193.9 20.2 %all-to-all-start.2 = ((bf16[8,16,3584]{2,1,0:T(8,128)(2,1)}), bf16[8,16,3584]{2,1,0:T(8,128)(2,1)S(1)}, u32[]{:S(2)}, u32[]{:S(2)}) async-start(bf16[8,16,3584]{2,1,0:T(8,128)(2,1)} %bitcast.140), calls=%async_computation.3 | async-start | bytes 1835008 | tf_op jit(solution)/shard_map/all_to_all | solution.py:217
  214.3 4.9 %collective-permute-start.18 = (bf16[16,3584]{1,0:T(8,128)(2,1)S(1)}, bf16[16,3584]{1,0:T(8,128)(2,1)S(1)}, u32[]{:S(2)}, u32[]{:S(2)}) collective-permute-start(bf16[16,3584]{1,0:T(8,128)(2,1)S(1)} %get-tuple-element.93), channel_id=1, source_target_pairs={{0,1},{1,0},{2,3},{3,2},{4,5},{5,4},{6,7},{7,6},{8,9},{9,8},{10,11... | collective-permute-start | bytes 344072 | tf_op jit(solution)/shard_map/ppermute | solution.py:24
  220.0 12.1 %collective-permute-start.19 = (bf16[16,7168]{1,0:T(8,128)(2,1)S(1)}, bf16[16,7168]{1,0:T(8,128)(2,1)S(1)}, u32[]{:S(2)}, u32[]{:S(2)}) collective-permute-start(bf16[16,7168]{1,0:T(8,128)(2,1)S(1)} %backward.1), channel_id=1, source_target_pairs={{0,16},{1,17},{2,18},{3,19},{4,20},{5,21},{6,22},{7,23},{8,24},{9,... | collective-permute-start | bytes 688136 | tf_op jit(solution)/shard_map/ppermute | solution.py:24
  220.8 11.3 %collective-permute-start.20 = (bf16[16,7168]{1,0:T(8,128)(2,1)S(1)}, bf16[16,7168]{1,0:T(8,128)(2,1)S(1)}, u32[]{:S(2)}, u32[]{:S(2)}) collective-permute-start(bf16[16,7168]{1,0:T(8,128)(2,1)S(1)} %backward.1), channel_id=1, source_target_pairs={{0,48},{1,49},{2,50},{3,51},{4,52},{5,53},{6,54},{7,55},{8,56},{9,... | collective-permute-start | bytes 688136 | tf_op jit(solution)/shard_map/ppermute | solution.py:24
  223.3 8.8 %collective-permute-start.21 = (bf16[16,7168]{1,0:T(8,128)(2,1)S(1)}, bf16[16,7168]{1,0:T(8,128)(2,1)S(1)}, u32[]{:S(2)}, u32[]{:S(2)}) collective-permute-start(bf16[16,7168]{1,0:T(8,128)(2,1)S(1)} %backward.1), channel_id=1, source_target_pairs={{0,32},{1,33},{2,34},{3,35},{4,36},{5,37},{6,38},{7,39},{8,40},{9,... | collective-permute-start | bytes 688136 | tf_op jit(solution)/shard_map/ppermute | solution.py:24
  223.9 12.1 %collective-permute-start.23 = (bf16[512,512]{1,0:T(8,128)(2,1)}, bf16[512,512]{1,0:T(8,128)(2,1)S(1)}, u32[]{:S(2)}, u32[]{:S(2)}) collective-permute-start(bf16[512,512]{1,0:T(8,128)(2,1)} %convolution_convert_fusion.3), channel_id=1, source_target_pairs={{0,64},{64,0},{1,65},{65,1},{2,66},{66,2},{3,67},{67,3},{4,68},{68... | collective-permute-start | bytes 1572872 | tf_op jit(solution)/shard_map/ppermute | solution.py:223
  232.2 5.0 %collective-permute-start.22 = (bf16[4,16,7168]{2,1,0:T(8,128)(2,1)S(1)}, bf16[4,16,7168]{2,1,0:T(8,128)(2,1)S(1)}, u32[]{:S(2)}, u32[]{:S(2)}) collective-permute-start(bf16[4,16,7168]{2,1,0:T(8,128)(2,1)S(1)} %bitcast_dynamic-update-slice_fusion.14), channel_id=1, source_target_pairs={{0,8},{1,9},{2,10},{3,11},{4,12},{5,13},{6,14},{7,15},{8,0},{9,1},... | collective-permute-start | bytes 2752520 | tf_op jit(solution)/shard_map/ppermute | solution.py:24
  237.2 1.8 copy-start.5
  237.3 2.3 copy-start.9
Sparse Core Ops, SparseCore 0:
  38.4 46.2 all-gather.1
  120.6 44.6 reduce-scatter.1

commit v5 on v4

--- a/solution.py
+++ b/solution.py
@@ -176,7 +176,7 @@
     sums1, grad_a, grad_b = lax.optimization_barrier((sums1, grad_a, grad_b))
     over_vocab = lax.psum_scatter(sums1, "vocab", scatter_dimension=0, tiled=True)
     sent = dot(take(grad_b, 1 - c), table2, ((1,), (0,)), bf16)
-    start, early = half // 14, half * 6 // 7
+    start, early = half // 14, half * 11 // 14
     first_grad = dot(grad_b.reshape(-1, vocab_rows), rows2[:, :start], ((0,), (0,)), bf16)
     sent, first_grad, grad_b = lax.optimization_barrier((sent, first_grad, grad_b))
     swap = [(0, 1), (1, 0)]

time: 248 us -> 247 us (level)
    all_to_all x1, waiting for transfers between devices: 10.3 us -> 6.53 us  [on_device(): lax.all_to_all(over_vocab.reshape(-1, part, half), 'dp', 0, 0, tiled=True)]
    ppermute x1, waiting for transfers between devices: 3.48 us -> 6.52 us  [on_device(): late = lax.ppermute(late, 'pipe', swap)]
  transfers between devices with their start and end apart: 28 -> 28, of which waited for: 13 -> 12; matrix products, arithmetic and copies ran while one was open for 27% -> 28% of each run, Pallas kernels for 0% -> 0%
where the time goes in v5:
time: 247 us; the launch traced here: 246 us
  waiting for transfers between devices  80.8 us (33%)
  matrix products  47 us (19%)
  starting transfers between devices  37.5 us (15%)
  local copies, waits for them, and re-layouts  31.9 us (13%)
  blocking collectives  17.7 us (7%)
  other arithmetic  15.2 us (6%)
  between operations  14.8 us (6%)
    ppermute x21, waiting for transfers between devices, hop(): return lax.ppermute(array, ('vocab', 'dp'), pairs)  60.9 us
    dot_general x9, matrix products, dot(): lax.dot_general(a, b, (contract, ((), ())), preferred_element_type=jnp.fl...  47 us
    ppermute x21, starting transfers between devices, hop(): return lax.ppermute(array, ('vocab', 'dp'), pairs)  20.4 us
    all_to_all x1, blocking collectives, on_device(): stats = lax.all_to_all(stats, ('vocab', 'dp'), 0, 0, tiled=True)  17.7 us
    dynamic_update_slice x18, local copies, waits for them, and re-layouts, put(): return lax.dynamic_update_slice(buffer, block, start)  9.99 us
    dynamic_slice x1, local copies, waits for them, and re-layouts, on_device(): table2 = lax.dynamic_slice(table, (0, other_col), (vocab_rows, half))  6.65 us
    all_to_all x1, waiting for transfers between devices, on_device(): lax.all_to_all(over_vocab.reshape(-1, part, half), 'dp', 0, 0, tiled=True)  6.53 us
    ppermute x1, waiting for transfers between devices, on_device(): late = lax.ppermute(late, 'pipe', swap)  6.52 us
  transfers between devices with their start and end apart: 28, of which 12 were waited for; matrix products, arithmetic and copies ran while one was open for 28% of the time, Pallas kernels for 0%

profile of v5, /device:TPU:0, one launch (start us, length us, event | category | flops | bytes accessed | tf_op | source)
XLA Modules:
  0.0 245.8 jit_solution(18184683817861630727)
XLA Ops:
  7.2 1.1 dynamic-slice_convert_fusion.1
  8.3 1.1 multiply_reduce_fusion.1
  12.1 6.4 %all-to-all-start = ((bf16[8,16,3712]{2,1,0:T(8,128)(2,1)}), bf16[8,16,3712]{2,1,0:T(8,128)(2,1)S(1)}, u32[]{:S(2)}, u32[]{:S(2)}) async-start(bf16[8,16,3712]{2,1,0:T(8,128)(2,1)} %broadcast_in_dim.14), calls=%async_computation | async-start | bytes 1900544 | tf_op jit(solution)/shard_map/all_to_all | solution.py:112
  18.6 1.4 dynamic-slice_convert_fusion
  20.3 6.6 %constant_dynamic-slice_fusion.5 = (bf16[512,3584]{1,0:T(8,128)(2,1)}, bf16[512,3584]{1,0:T(8,128)(2,1)}) fusion(bf16[512,7168]{1,0:T(8,128)(2,1)} %param.7, s32[]{:T(128)S(6)} %select_n.189, s32[]{:T(128)S(6)} %select_n.191), kind=kLoop, calls=%fused_computation.82 | loop fusion | bytes 14680072 | tf_op jit(solution)/shard_map/dynamic_slice | solution.py:138
  27.0 1.3 fusion.19
  28.3 4.9 %all-to-all-done = bf16[8,16,3712]{2,1,0:T(8,128)(2,1)S(1)} async-done(((bf16[8,16,3712]{2,1,0:T(8,128)(2,1)}), bf16[8,16,3712]{2,1,0:T(8,128)(2,1)S(1)}, u32[]{:S(2)}, u32[]{:S(2)}) %all-to-all-start) | async-done | bytes 950304 | tf_op jit(solution)/shard_map/all_to_all | solution.py:112
  33.2 2.3 collective-permute-start.2
  35.5 1.2 collective-permute-start.5
  38.3 1.4 broadcast.85.clone
  40.7 14.4 %collective-permute-done = bf16[64,3584]{1,0:T(8,128)(2,1)} collective-permute-done((bf16[64,3584]{1,0:T(8,128)(2,1)S(1)}, bf16[64,3584]{1,0:T(8,128)(2,1)}, u32[]{:S(2)}, u32[]{:S(2)}) %collective-permute-start) | collective-permute-done | bytes 458784 | tf_op jit(solution)/shard_map/ppermute | solution.py:24
  55.7 1.4 collective-permute-start.6
  57.1 2.0 collective-permute-start.7
  60.3 1.8 bitcast_dynamic-update-slice_fusion.12
  62.1 1.8 bitcast_dynamic-update-slice_fusion.11
  63.9 3.3 %collective-permute-done.3 = bf16[64,3584]{1,0:T(8,128)(2,1)S(1)} collective-permute-done((bf16[64,3584]{1,0:T(8,128)(2,1)}, bf16[64,3584]{1,0:T(8,128)(2,1)S(1)}, u32[]{:S(2)}, u32[]{:S(2)}) %collective-permute-start.3) | collective-permute-done | bytes 458784 | tf_op jit(solution)/shard_map/ppermute | solution.py:24
  67.2 1.8 bitcast_dynamic-update-slice_fusion.10
  69.1 3.0 %collective-permute-done.6 = bf16[64,3584]{1,0:T(8,128)(2,1)S(1)} collective-permute-done((bf16[64,3584]{1,0:T(8,128)(2,1)}, bf16[64,3584]{1,0:T(8,128)(2,1)S(1)}, u32[]{:S(2)}, u32[]{:S(2)}) %collective-permute-start.6) | collective-permute-done | bytes 458784 | tf_op jit(solution)/shard_map/ppermute | solution.py:24
  73.0 1.7 bitcast_dynamic-update-slice_fusion.3
  77.3 4.0 %fusion.10 = f32[4,2,4,2,16,512]{5,4,0,2,3,1:T(8,128)S(1)} fusion(bf16[2,2,4,4,16,3584]{5,4,3,2,1,0:T(8,128)(2,1)S(1)} %bitcast.123, bf16[512,3584]{1,0:T(8,128)(2,1)S(1)} %copy-done.6), kind=kOutput, calls=%fused_computation.23 | convolution fusion | flops 3758096384 | bytes 13107200 | tf_op jit(solution)/shard_map/dot_general | solution.py:40
  81.3 1.5 copy.35
  82.8 1.9 all-gather.2.cloned.1.call-done
  84.7 7.5 %fusion.42 = f32[1024,512]{1,0:T(8,128)S(1)} fusion(bf16[1024,3584]{1,0:T(8,128)(2,1)} %all-gather.2.cloned.1.call-done, bf16[512,3584]{1,0:T(8,128)(2,1)} %get-tuple-element.42), kind=kOutput, calls=%fused_computation.109 | convolution fusion | flops 3758096384 | bytes 13107200 | tf_op jit(solution)/shard_map/dot_general | solution.py:40
  92.5 1.3 copy-done.1
  95.0 17.7 %all_to_all.22 = f32[64,1,1152]{2,1,0:T(1,128)S(1)} all-to-all(f32[64,1,1152]{2,1,0:T(1,128)S(1)} %all_to_all.15), channel_id=1, replica_groups=mesh['pipe'=2,'vocab'=8,'dp'=8] {'vocab','dp'}, dimensions={0} | all-to-all | bytes 589824 | tf_op jit(solution)/shard_map/all_to_all | solution.py:161
  113.4 6.1 %convolution_convert_fusion = bf16[1024,3584]{1,0:T(8,128)(2,1)} fusion(bf16[1024,512]{1,0:T(8,128)(2,1)S(1)} %fusion.9, bf16[512,3584]{1,0:T(8,128)(2,1)S(1)} %copy-done.8), kind=kOutput, calls=%fused_computation | convolution fusion | flops 3761766400 | bytes 12058624 | tf_op jit(solution)/shard_map/dot_general | solution.py:40
  120.6 2.7 %convolution_convert_fusion.3 = bf16[512,256]{1,0:T(8,128)(2,1)} fusion(bf16[1024,512]{1,0:T(8,128)(2,1)} %bitcast.135, bf16[1024,3584]{1,0:T(8,128)(2,1)} %bitcast.124), kind=kOutput, calls=%fused_computation.28 | convolution fusion | flops 268566528 | bytes 1835008 | tf_op jit(solution)/shard_map/dot_general | solution.py:40
  123.3 6.0 %convolution_convert_fusion.2 = bf16[512,3584]{1,0:T(8,128)(2,1)} fusion(bf16[512,3584]{1,0:T(8,128)(2,1)} %get-tuple-element.46, bf16[2,512,512]{2,1,0:T(8,128)(2,1)S(1)} %bitcast.137, s32[]{:T(128)S(6)} %select_n.205), kind=kOutput, calls=%fused_computation.3 | convolution fusion | flops 1880883200 | bytes 7864324 | tf_op jit(solution)/shard_map/dot_general | solution.py:40
  129.3 2.7 %collective-permute-start.9 = (bf16[512,256]{1,0:T(8,128)(2,1)}, bf16[512,256]{1,0:T(8,128)(2,1)S(1)}, u32[]{:S(2)}, u32[]{:S(2)}) collective-permute-start(bf16[512,256]{1,0:T(8,128)(2,1)} %convolution_convert_fusion.3), channel_id=1, source_target_pairs={{0,64},{64,0},{1,65},{65,1},{2,66},{66,2},{3,67},{67,3},{4,68},{68... | collective-permute-start | bytes 786440 | tf_op jit(solution)/shard_map/ppermute | solution.py:183
  132.1 7.5 %fusion.2 = bf16[512,2560]{1,0:T(8,128)(2,1)} fusion(bf16[1024,512]{1,0:T(8,128)(2,1)} %bitcast.136, bf16[1024,3584]{1,0:T(8,128)(2,1)} %bitcast.125), kind=kOutput, calls=%fused_computation.7 | convolution fusion | flops 2685665280 | bytes 8912896 | tf_op jit(solution)/shard_map/dot_general | solution.py:40
  140.3 4.3 %add_convert_fusion = bf16[512,3584]{1,0:T(8,128)(2,1)S(1)} fusion(bf16[512,3584]{1,0:T(8,128)(2,1)} %collective-permute-done.10, bf16[512,3584]{1,0:T(8,128)(2,1)S(1)} %copy-done.7, bf16[2,512,512]{2,1,0:T(8,128)(2,1)S(1)} %bitcast.138, s32[]{:T(128)S(6)} %select_n.202), kind=kOutput, calls=%fused_computation.1 | convolution fusion | flops 1884553216 | bytes 11534340 | tf_op jit(solution)/shard_map/dot_general | solution.py:40
  145.4 2.7 %collective-permute-start.12 = (bf16[2,4,16,3584]{3,2,1,0:T(8,128)(2,1)S(1)}, bf16[2,4,16,3584]{3,2,1,0:T(8,128)(2,1)S(1)}, u32[]{:S(2)}, u32[]{:S(2)}) collective-permute-start(bf16[2,4,16,3584]{3,2,1,0:T(8,128)(2,1)S(1)} %bitcast.142), channel_id=1, source_target_pairs={{0,6},{1,7},{2,0},{3,1},{4,2},{5,3},{6,4},{7,5},{8,14},{9,15},{10,... | collective-permute-start | bytes 2752520 | tf_op jit(solution)/shard_map/ppermute | solution.py:24
  148.3 3.5 %fusion.15 = bf16[512,768]{1,0:T(8,128)(2,1)} fusion(bf16[1024,512]{1,0:T(8,128)(2,1)S(1)} %bitcast.139, bf16[1024,3584]{1,0:T(8,128)(2,1)} %bitcast.126), kind=kOutput, calls=%fused_computation.27 | convolution fusion | flops 805699584 | bytes 3407872 | tf_op jit(solution)/shard_map/dot_general | solution.py:40
  151.8 5.5 %convolution_convert_fusion.1 = bf16[512,3584]{1,0:T(8,128)(2,1)} fusion(bf16[1024,512]{1,0:T(8,128)(2,1)S(1)} %fusion.9, bf16[1024,3584]{1,0:T(8,128)(2,1)S(1)} %bitcast.148), kind=kOutput, calls=%fused_computation.2 | convolution fusion | flops 3759931392 | bytes 12058624 | tf_op jit(solution)/shard_map/dot_general | solution.py:40
  157.3 30.6 %collective-permute-done.11 = bf16[2,4,16,3584]{3,2,1,0:T(8,128)(2,1)S(1)} collective-permute-done((bf16[2,4,16,3584]{3,2,1,0:T(8,128)(2,1)S(1)}, bf16[2,4,16,3584]{3,2,1,0:T(8,128)(2,1)S(1)}, u32[]{:S(2)}, u32[]{:S(2)}) %collective-permute-start.11) | collective-permute-done | bytes 917536 | tf_op jit(solution)/shard_map/ppermute | solution.py:24
  189.9 2.6 %collective-permute-start.15 = (bf16[2,16,3584]{2,1,0:T(8,128)(2,1)}, bf16[2,16,3584]{2,1,0:T(8,128)(2,1)}, u32[]{:S(2)}, u32[]{:S(2)}) collective-permute-start(bf16[2,16,3584]{2,1,0:T(8,128)(2,1)} %get-tuple-element.67), channel_id=1, source_target_pairs={{0,48},{1,49},{2,50},{3,51},{4,52},{5,53},{6,54},{7,55},{8,56},{9,... | collective-permute-start | bytes 688136 | tf_op jit(solution)/shard_map/ppermute | solution.py:24
  193.2 4.4 %all-to-all-start.2 = ((bf16[8,16,3584]{2,1,0:T(8,128)(2,1)}), bf16[8,16,3584]{2,1,0:T(8,128)(2,1)S(1)}, u32[]{:S(2)}, u32[]{:S(2)}) async-start(bf16[8,16,3584]{2,1,0:T(8,128)(2,1)} %bitcast.140), calls=%async_computation.3 | async-start | bytes 1835008 | tf_op jit(solution)/shard_map/all_to_all | solution.py:217
  197.6 4.2 %collective-permute-done.14 = bf16[2,16,3584]{2,1,0:T(8,128)(2,1)} collective-permute-done((bf16[2,16,3584]{2,1,0:T(8,128)(2,1)}, bf16[2,16,3584]{2,1,0:T(8,128)(2,1)}, u32[]{:S(2)}, u32[]{:S(2)}) %collective-permute-start.14) | collective-permute-done | bytes 229408 | tf_op jit(solution)/shard_map/ppermute | solution.py:24
  201.8 1.3 add_convert_fusion.5
  203.1 6.5 %all-to-all-done.2 = bf16[8,16,3584]{2,1,0:T(8,128)(2,1)S(1)} async-done(((bf16[8,16,3584]{2,1,0:T(8,128)(2,1)}), bf16[8,16,3584]{2,1,0:T(8,128)(2,1)S(1)}, u32[]{:S(2)}, u32[]{:S(2)}) %all-to-all-start.2) | async-done | bytes 917536 | tf_op jit(solution)/shard_map/all_to_all | solution.py:217
  210.9 3.8 %collective-permute-done.18.far = bf16[16,3584]{1,0:T(8,128)(2,1)S(1)} collective-permute-done((bf16[16,3584]{1,0:T(8,128)(2,1)S(1)}, bf16[16,3584]{1,0:T(8,128)(2,1)S(1)}, u32[]{:S(2)}, u32[]{:S(2)}) %collective-permute-start.18) | collective-permute-done | bytes 114720 | tf_op jit(solution)/shard_map/ppermute | solution.py:24
  216.2 2.7 %collective-permute-start.20 = (bf16[16,7168]{1,0:T(8,128)(2,1)S(1)}, bf16[16,7168]{1,0:T(8,128)(2,1)S(1)}, u32[]{:S(2)}, u32[]{:S(2)}) collective-permute-start(bf16[16,7168]{1,0:T(8,128)(2,1)S(1)} %backward.1), channel_id=1, source_target_pairs={{0,48},{1,49},{2,50},{3,51},{4,52},{5,53},{6,54},{7,55},{8,56},{9,... | collective-permute-start | bytes 688136 | tf_op jit(solution)/shard_map/ppermute | solution.py:24
  218.8 2.0 collective-permute-start.21
  220.9 2.8 %collective-permute-start.23 = (bf16[512,768]{1,0:T(8,128)(2,1)S(1)}, bf16[512,768]{1,0:T(8,128)(2,1)S(1)}, u32[]{:S(2)}, u32[]{:S(2)}) collective-permute-start(bf16[512,768]{1,0:T(8,128)(2,1)S(1)} %copy-done.13), channel_id=1, source_target_pairs={{0,64},{64,0},{1,65},{65,1},{2,66},{66,2},{3,67},{67,3},{4,68},{68... | collective-permute-start | bytes 2359304 | tf_op jit(solution)/shard_map/ppermute | solution.py:223
  223.6 3.2 %add_convert_fusion.1 = bf16[512,2560]{1,0:T(8,128)(2,1)S(1)} fusion(bf16[512,2560]{1,0:T(8,128)(2,1)} %collective-permute-done.17, bf16[512,3584]{1,0:T(8,128)(2,1)} %convolution_convert_fusion.1), kind=kLoop, calls=%fused_computation.6 | loop fusion | flops 5242880 | bytes 7864320 | tf_op jit(solution)/shard_map/convert_element_type | solution.py:233
  228.6 6.5 %collective-permute-done.23 = bf16[512,768]{1,0:T(8,128)(2,1)S(1)} collective-permute-done((bf16[512,768]{1,0:T(8,128)(2,1)S(1)}, bf16[512,768]{1,0:T(8,128)(2,1)S(1)}, u32[]{:S(2)}, u32[]{:S(2)}) %collective-permute-start.23) | collective-permute-done | bytes 786464 | tf_op jit(solution)/shard_map/ppermute | solution.py:223
  235.2 1.3 fusion.20
  236.6 1.7 copy-done.5
  (134 shorter events, 23.6 us)
Async XLA Ops:
  7.2 11.4 %copy-start = (bf16[128,7168]{1,0:T(8,128)(2,1)S(1)}, bf16[128,7168]{1,0:T(8,128)(2,1)}, u32[]{:S(2)}) copy-start(bf16[128,7168]{1,0:T(8,128)(2,1)} %hidden.1) | copy-start | bytes 5505028
  12.1 21.1 %all-to-all-start = ((bf16[8,16,3712]{2,1,0:T(8,128)(2,1)}), bf16[8,16,3712]{2,1,0:T(8,128)(2,1)S(1)}, u32[]{:S(2)}, u32[]{:S(2)}) async-start(bf16[8,16,3712]{2,1,0:T(8,128)(2,1)} %broadcast_in_dim.14), calls=%async_computation | async-start | bytes 1900544 | tf_op jit(solution)/shard_map/all_to_all | solution.py:112
  18.5 66.2 %all-gather.2.cloned.1.call-start = ((), (), s32[]{:S(2)}) async-start(), calls=%async_computation.4 | async-start | bytes 8257536 | tf_op jit(solution)/shard_map/all_gather | solution.py:116
  33.2 21.9 %collective-permute-start = (bf16[64,3584]{1,0:T(8,128)(2,1)S(1)}, bf16[64,3584]{1,0:T(8,128)(2,1)}, u32[]{:S(2)}, u32[]{:S(2)}) collective-permute-start(bf16[64,3584]{1,0:T(8,128)(2,1)S(1)} %fusion.19), channel_id=1, source_target_pairs={{0,2},{1,3},{2,4},{3,5},{4,6},{5,7},{6,0},{7,1},{8,10},{9,11},{10,... | collective-permute-start | bytes 1376264 | tf_op jit(solution)/shard_map/ppermute | solution.py:24
  33.2 30.8 %collective-permute-start.2 = (bf16[64,3584]{1,0:T(8,128)(2,1)S(1)}, bf16[64,3584]{1,0:T(8,128)(2,1)}, u32[]{:S(2)}, u32[]{:S(2)}) collective-permute-start(bf16[64,3584]{1,0:T(8,128)(2,1)S(1)} %fusion.19), channel_id=1, source_target_pairs={{0,4},{1,5},{2,6},{3,7},{4,0},{5,1},{6,2},{7,3},{8,12},{9,13},{10,... | collective-permute-start | bytes 1376264 | tf_op jit(solution)/shard_map/ppermute | solution.py:24
  35.5 21.6 %collective-permute-start.5 = (bf16[64,3584]{1,0:T(8,128)(2,1)S(1)}, bf16[64,3584]{1,0:T(8,128)(2,1)}, u32[]{:S(2)}, u32[]{:S(2)}) collective-permute-start(bf16[64,3584]{1,0:T(8,128)(2,1)S(1)} %fusion.19), channel_id=1, source_target_pairs={{0,1},{1,0},{2,3},{3,2},{4,5},{5,4},{6,7},{7,6},{8,9},{9,8},{10,11... | collective-permute-start | bytes 1376264 | tf_op jit(solution)/shard_map/ppermute | solution.py:24
  36.7 19.1 %collective-permute-start.1 = (bf16[64,3584]{1,0:T(8,128)(2,1)S(1)}, bf16[64,3584]{1,0:T(8,128)(2,1)}, u32[]{:S(2)}, u32[]{:S(2)}) collective-permute-start(bf16[64,3584]{1,0:T(8,128)(2,1)S(1)} %fusion.19), channel_id=1, source_target_pairs={{0,6},{1,7},{2,0},{3,1},{4,2},{5,3},{6,4},{7,5},{8,14},{9,15},{10,... | collective-permute-start | bytes 1376264 | tf_op jit(solution)/shard_map/ppermute | solution.py:24
  38.3 151.1 %reduce-scatter.2.cloned.1.call-start = ((), (), s32[]{:S(2)}) async-start(), calls=%async_computation.5 | async-start | bytes 8257536 | tf_op jit(solution)/shard_map/reduce_scatter | solution.py:177
  55.1 12.1 %collective-permute-start.3 = (bf16[64,3584]{1,0:T(8,128)(2,1)}, bf16[64,3584]{1,0:T(8,128)(2,1)S(1)}, u32[]{:S(2)}, u32[]{:S(2)}) collective-permute-start(bf16[64,3584]{1,0:T(8,128)(2,1)} %collective-permute-done), channel_id=1, source_target_pairs={{0,1},{1,0},{2,3},{3,2},{4,5},{5,4},{6,7},{7,6},{8,9},{9,8},{10,11... | collective-permute-start | bytes 1376264 | tf_op jit(solution)/shard_map/ppermute | solution.py:24
  55.7 16.4 %collective-permute-start.6 = (bf16[64,3584]{1,0:T(8,128)(2,1)}, bf16[64,3584]{1,0:T(8,128)(2,1)S(1)}, u32[]{:S(2)}, u32[]{:S(2)}) collective-permute-start(bf16[64,3584]{1,0:T(8,128)(2,1)} %collective-permute-done.1), channel_id=1, source_target_pairs={{0,1},{1,0},{2,3},{3,2},{4,5},{5,4},{6,7},{7,6},{8,9},{9,8},{10,11... | collective-permute-start | bytes 1376264 | tf_op jit(solution)/shard_map/ppermute | solution.py:24
  57.1 15.0 %collective-permute-start.7 = (bf16[64,3584]{1,0:T(8,128)(2,1)}, bf16[64,3584]{1,0:T(8,128)(2,1)S(1)}, u32[]{:S(2)}, u32[]{:S(2)}) collective-permute-start(bf16[64,3584]{1,0:T(8,128)(2,1)} %collective-permute-done.5), channel_id=1, source_target_pairs={{0,4},{1,5},{2,6},{3,7},{4,0},{5,1},{6,2},{7,3},{8,12},{9,13},{10,... | collective-permute-start | bytes 1376264 | tf_op jit(solution)/shard_map/ppermute | solution.py:24
  69.0 5.7 %collective-permute-start.4 = (bf16[4,64,3584]{2,1,0:T(8,128)(2,1)}, bf16[4,64,3584]{2,1,0:T(8,128)(2,1)S(1)}, u32[]{:S(2)}, u32[]{:S(2)}) collective-permute-start(bf16[4,64,3584]{2,1,0:T(8,128)(2,1)} %bitcast_dynamic-update-slice_fusion.10), channel_id=1, source_target_pairs={{0,8},{1,9},{2,10},{3,11},{4,12},{5,13},{6,14},{7,15},{8,0},{9,1},... | collective-permute-start | bytes 5505032 | tf_op jit(solution)/shard_map/ppermute | solution.py:24
  72.2 3.9 %collective-permute-start.8 = (bf16[4,64,3584]{2,1,0:T(8,128)(2,1)S(1)}, bf16[4,64,3584]{2,1,0:T(8,128)(2,1)S(1)}, u32[]{:S(2)}, u32[]{:S(2)}) collective-permute-start(bf16[4,64,3584]{2,1,0:T(8,128)(2,1)S(1)} %bitcast_dynamic-update-slice_fusion.6), channel_id=1, source_target_pairs={{0,8},{1,9},{2,10},{3,11},{4,12},{5,13},{6,14},{7,15},{8,0},{9,1},... | collective-permute-start | bytes 5505032 | tf_op jit(solution)/shard_map/ppermute | solution.py:24
  75.2 2.2 copy-start.6
  76.3 5.0 %copy-start.4 = (bf16[2,2,4,64,3584]{4,3,2,1,0:T(8,128)(2,1)}, bf16[2,2,4,64,3584]{4,3,2,1,0:T(8,128)(2,1)S(1)}, u32[]{:S(2)}) copy-start(bf16[2,2,4,64,3584]{4,3,2,1,0:T(8,128)(2,1)S(1)} %bitcast_dynamic-update-slice_fusion) | copy-start | bytes 22020100
  84.7 7.5 %copy-start.3 = (f32[4,2,4,2,16,512]{5,4,3,2,1,0:T(8,128)S(1)}, f32[4,2,4,2,16,512]{5,4,3,2,1,0:T(8,128)}, u32[]{:S(2)}) copy-start(f32[4,2,4,2,16,512]{5,4,3,2,1,0:T(8,128)} %copy.35) | copy-start | bytes 6291460
  92.5 1.3 copy-start.1
  94.7 18.1 %copy-start.2 = (f32[1024,512]{1,0:T(8,128)S(1)}, f32[1024,512]{1,0:T(8,128)}, u32[]{:S(2)}) copy-start(f32[1024,512]{1,0:T(8,128)} %copy-done.1) | copy-start | bytes 6291460
  94.8 18.6 %copy-start.8 = (bf16[512,3584]{1,0:T(8,128)(2,1)S(1)}, bf16[512,3584]{1,0:T(8,128)(2,1)}, u32[]{:S(2)}) copy-start(bf16[512,3584]{1,0:T(8,128)(2,1)} %get-tuple-element.42) | copy-start | bytes 11010052
  120.6 2.7 %copy-start.10 = (bf16[4,2,4,2,16,512]{5,4,0,2,3,1:T(8,128)(2,1)S(1)}, bf16[4,2,4,2,16,512]{5,4,0,2,3,1:T(8,128)(2,1)}, u32[]{:S(2)}) copy-start(bf16[4,2,4,2,16,512]{5,4,0,2,3,1:T(8,128)(2,1)} %copy.37) | copy-start | bytes 3145732
  129.2 11.1 %collective-permute-start.10 = (bf16[512,3584]{1,0:T(8,128)(2,1)}, bf16[512,3584]{1,0:T(8,128)(2,1)}, u32[]{:S(2)}, u32[]{:S(2)}) collective-permute-start(bf16[512,3584]{1,0:T(8,128)(2,1)} %convolution_convert_fusion.2), channel_id=1, source_target_pairs={{0,8},{1,9},{2,10},{3,11},{4,12},{5,13},{6,14},{7,15},{8,0},{9,1},... | collective-permute-start | bytes 11010056 | tf_op jit(solution)/shard_map/ppermute | solution.py:24
  129.3 10.9 %collective-permute-start.9 = (bf16[512,256]{1,0:T(8,128)(2,1)}, bf16[512,256]{1,0:T(8,128)(2,1)S(1)}, u32[]{:S(2)}, u32[]{:S(2)}) collective-permute-start(bf16[512,256]{1,0:T(8,128)(2,1)} %convolution_convert_fusion.3), channel_id=1, source_target_pairs={{0,64},{64,0},{1,65},{65,1},{2,66},{66,2},{3,67},{67,3},{4,68},{68... | collective-permute-start | bytes 786440 | tf_op jit(solution)/shard_map/ppermute | solution.py:183
  132.1 8.2 %copy-start.7 = (bf16[512,3584]{1,0:T(8,128)(2,1)S(1)}, bf16[512,3584]{1,0:T(8,128)(2,1)}, u32[]{:S(2)}) copy-start(bf16[512,3584]{1,0:T(8,128)(2,1)} %get-tuple-element.46) | copy-start | bytes 11010052
  132.1 8.2 %copy-start.11 = (bf16[4,2,4,2,16,512]{5,4,0,2,3,1:T(8,128)(2,1)S(1)}, bf16[4,2,4,2,16,512]{5,4,0,2,3,1:T(8,128)(2,1)}, u32[]{:S(2)}) copy-start(bf16[4,2,4,2,16,512]{5,4,0,2,3,1:T(8,128)(2,1)} %copy.37) | copy-start | bytes 3145732
  139.5 70.2 %collective-permute-start.17 = (bf16[512,2560]{1,0:T(8,128)(2,1)}, bf16[512,2560]{1,0:T(8,128)(2,1)}, u32[]{:S(2)}, u32[]{:S(2)}) collective-permute-start(bf16[512,2560]{1,0:T(8,128)(2,1)} %fusion.2), channel_id=1, source_target_pairs={{0,64},{64,0},{1,65},{65,1},{2,66},{66,2},{3,67},{67,3},{4,68},{68... | collective-permute-start | bytes 7864328 | tf_op jit(solution)/shard_map/ppermute | solution.py:189
  144.6 7.2 %slice-start = ((s8[7340032]{0:T(1024)(128)(4,1)}), s8[4194304]{0:T(1024)(128)(4,1)S(1)}, s32[]{:S(2)}) async-start(s8[7340032]{0:T(1024)(128)(4,1)} %bitcast.147), calls=%async_computation.6 | async-start | bytes 8388608
  144.8 43.1 %collective-permute-start.11 = (bf16[2,4,16,3584]{3,2,1,0:T(8,128)(2,1)S(1)}, bf16[2,4,16,3584]{3,2,1,0:T(8,128)(2,1)S(1)}, u32[]{:S(2)}, u32[]{:S(2)}) collective-permute-start(bf16[2,4,16,3584]{3,2,1,0:T(8,128)(2,1)S(1)} %bitcast.143), channel_id=1, source_target_pairs={{0,2},{1,3},{2,4},{3,5},{4,6},{5,7},{6,0},{7,1},{8,10},{9,11},{10,... | collective-permute-start | bytes 2752520 | tf_op jit(solution)/shard_map/ppermute | solution.py:24
  145.4 42.5 %collective-permute-start.12 = (bf16[2,4,16,3584]{3,2,1,0:T(8,128)(2,1)S(1)}, bf16[2,4,16,3584]{3,2,1,0:T(8,128)(2,1)S(1)}, u32[]{:S(2)}, u32[]{:S(2)}) collective-permute-start(bf16[2,4,16,3584]{3,2,1,0:T(8,128)(2,1)S(1)} %bitcast.142), channel_id=1, source_target_pairs={{0,6},{1,7},{2,0},{3,1},{4,2},{5,3},{6,4},{7,5},{8,14},{9,15},{10,... | collective-permute-start | bytes 2752520 | tf_op jit(solution)/shard_map/ppermute | solution.py:24
  148.1 39.8 %collective-permute-start.13 = (bf16[2,4,16,3584]{3,2,1,0:T(8,128)(2,1)S(1)}, bf16[2,4,16,3584]{3,2,1,0:T(8,128)(2,1)S(1)}, u32[]{:S(2)}, u32[]{:S(2)}) collective-permute-start(bf16[2,4,16,3584]{3,2,1,0:T(8,128)(2,1)S(1)} %bitcast.141), channel_id=1, source_target_pairs={{0,4},{1,5},{2,6},{3,7},{4,0},{5,1},{6,2},{7,3},{8,12},{9,13},{10,... | collective-permute-start | bytes 2752520 | tf_op jit(solution)/shard_map/ppermute | solution.py:24
  148.3 3.5 %slice-start.1 = ((s8[7340032]{0:T(1024)(128)(4,1)}), s8[3145728]{0:T(1024)(128)(4,1)S(1)}, s32[]{:S(2)}) async-start(s8[7340032]{0:T(1024)(128)(4,1)} %bitcast.147), calls=%async_computation.7 | async-start | bytes 6291456
  157.3 35.6 %copy-start.12 = (bf16[7168]{0:T(1024)(128)(2,1)S(1)}, bf16[7168]{0:T(1024)(128)(2,1)}, u32[]{:S(2)}) copy-start(bf16[7168]{0:T(1024)(128)(2,1)} %param.5) | copy-start | bytes 43012
  189.3 12.5 %collective-permute-start.14 = (bf16[2,16,3584]{2,1,0:T(8,128)(2,1)}, bf16[2,16,3584]{2,1,0:T(8,128)(2,1)}, u32[]{:S(2)}, u32[]{:S(2)}) collective-permute-start(bf16[2,16,3584]{2,1,0:T(8,128)(2,1)} %get-tuple-element.66), channel_id=1, source_target_pairs={{0,16},{1,17},{2,18},{3,19},{4,20},{5,21},{6,22},{7,23},{8,24},{9,... | collective-permute-start | bytes 688136 | tf_op jit(solution)/shard_map/ppermute | solution.py:24
  189.9 11.9 %collective-permute-start.15 = (bf16[2,16,3584]{2,1,0:T(8,128)(2,1)}, bf16[2,16,3584]{2,1,0:T(8,128)(2,1)}, u32[]{:S(2)}, u32[]{:S(2)}) collective-permute-start(bf16[2,16,3584]{2,1,0:T(8,128)(2,1)} %get-tuple-element.67), channel_id=1, source_target_pairs={{0,48},{1,49},{2,50},{3,51},{4,52},{5,53},{6,54},{7,55},{8,56},{9,... | collective-permute-start | bytes 688136 | tf_op jit(solution)/shard_map/ppermute | solution.py:24
  192.6 9.2 %collective-permute-start.16 = (bf16[2,16,3584]{2,1,0:T(8,128)(2,1)}, bf16[2,16,3584]{2,1,0:T(8,128)(2,1)}, u32[]{:S(2)}, u32[]{:S(2)}) collective-permute-start(bf16[2,16,3584]{2,1,0:T(8,128)(2,1)} %get-tuple-element.68), channel_id=1, source_target_pairs={{0,32},{1,33},{2,34},{3,35},{4,36},{5,37},{6,38},{7,39},{8,40},{9,... | collective-permute-start | bytes 688136 | tf_op jit(solution)/shard_map/ppermute | solution.py:24
  193.2 16.4 %all-to-all-start.2 = ((bf16[8,16,3584]{2,1,0:T(8,128)(2,1)}), bf16[8,16,3584]{2,1,0:T(8,128)(2,1)S(1)}, u32[]{:S(2)}, u32[]{:S(2)}) async-start(bf16[8,16,3584]{2,1,0:T(8,128)(2,1)} %bitcast.140), calls=%async_computation.3 | async-start | bytes 1835008 | tf_op jit(solution)/shard_map/all_to_all | solution.py:217
  209.8 4.9 %collective-permute-start.18 = (bf16[16,3584]{1,0:T(8,128)(2,1)S(1)}, bf16[16,3584]{1,0:T(8,128)(2,1)S(1)}, u32[]{:S(2)}, u32[]{:S(2)}) collective-permute-start(bf16[16,3584]{1,0:T(8,128)(2,1)S(1)} %get-tuple-element.93), channel_id=1, source_target_pairs={{0,1},{1,0},{2,3},{3,2},{4,5},{5,4},{6,7},{7,6},{8,9},{9,8},{10,11... | collective-permute-start | bytes 344072 | tf_op jit(solution)/shard_map/ppermute | solution.py:24
  210.9 10.0 %copy-start.13 = (bf16[512,768]{1,0:T(8,128)(2,1)S(1)}, bf16[512,768]{1,0:T(8,128)(2,1)}, u32[]{:S(2)}) copy-start(bf16[512,768]{1,0:T(8,128)(2,1)} %fusion.15) | copy-start | bytes 2359300
  215.5 12.6 %collective-permute-start.19 = (bf16[16,7168]{1,0:T(8,128)(2,1)S(1)}, bf16[16,7168]{1,0:T(8,128)(2,1)S(1)}, u32[]{:S(2)}, u32[]{:S(2)}) collective-permute-start(bf16[16,7168]{1,0:T(8,128)(2,1)S(1)} %backward.1), channel_id=1, source_target_pairs={{0,16},{1,17},{2,18},{3,19},{4,20},{5,21},{6,22},{7,23},{8,24},{9,... | collective-permute-start | bytes 688136 | tf_op jit(solution)/shard_map/ppermute | solution.py:24
  216.2 12.0 %collective-permute-start.20 = (bf16[16,7168]{1,0:T(8,128)(2,1)S(1)}, bf16[16,7168]{1,0:T(8,128)(2,1)S(1)}, u32[]{:S(2)}, u32[]{:S(2)}) collective-permute-start(bf16[16,7168]{1,0:T(8,128)(2,1)S(1)} %backward.1), channel_id=1, source_target_pairs={{0,48},{1,49},{2,50},{3,51},{4,52},{5,53},{6,54},{7,55},{8,56},{9,... | collective-permute-start | bytes 688136 | tf_op jit(solution)/shard_map/ppermute | solution.py:24
  218.8 9.4 %collective-permute-start.21 = (bf16[16,7168]{1,0:T(8,128)(2,1)S(1)}, bf16[16,7168]{1,0:T(8,128)(2,1)S(1)}, u32[]{:S(2)}, u32[]{:S(2)}) collective-permute-start(bf16[16,7168]{1,0:T(8,128)(2,1)S(1)} %backward.1), channel_id=1, source_target_pairs={{0,32},{1,33},{2,34},{3,35},{4,36},{5,37},{6,38},{7,39},{8,40},{9,... | collective-permute-start | bytes 688136 | tf_op jit(solution)/shard_map/ppermute | solution.py:24
  220.9 14.3 %collective-permute-start.23 = (bf16[512,768]{1,0:T(8,128)(2,1)S(1)}, bf16[512,768]{1,0:T(8,128)(2,1)S(1)}, u32[]{:S(2)}, u32[]{:S(2)}) collective-permute-start(bf16[512,768]{1,0:T(8,128)(2,1)S(1)} %copy-done.13), channel_id=1, source_target_pairs={{0,64},{64,0},{1,65},{65,1},{2,66},{66,2},{3,67},{67,3},{4,68},{68... | collective-permute-start | bytes 2359304 | tf_op jit(solution)/shard_map/ppermute | solution.py:223
  228.3 8.2 %collective-permute-start.22 = (bf16[4,16,7168]{2,1,0:T(8,128)(2,1)S(1)}, bf16[4,16,7168]{2,1,0:T(8,128)(2,1)S(1)}, u32[]{:S(2)}, u32[]{:S(2)}) collective-permute-start(bf16[4,16,7168]{2,1,0:T(8,128)(2,1)S(1)} %bitcast_dynamic-update-slice_fusion.14), channel_id=1, source_target_pairs={{0,8},{1,9},{2,10},{3,11},{4,12},{5,13},{6,14},{7,15},{8,0},{9,1},... | collective-permute-start | bytes 2752520 | tf_op jit(solution)/shard_map/ppermute | solution.py:24
  236.5 1.8 copy-start.5
  236.6 2.3 copy-start.9
Sparse Core Ops, SparseCore 0:
  38.4 46.2 all-gather.1
  120.7 44.6 reduce-scatter.1
